TPU v7x, 32 devices: a whole 2x2x4 slice. The times are simulated.
32 devices in a mesh: grp: 2 (over y), seq: 4 (over z), head: 2 (over x), dat: 2 (over core).
Axes of the slice: x: 2, y: 2, z: 4, core: 2. Of those that a mesh axis runs over, the one named last changes fastest.
Arguments:
- queries: bfloat16 [4, 256, 3072], P(('grp', 'dat'), 'seq', 'head'), parts along dimension 0, may hold values from -10 to 10
- keys: bfloat16 [4, 256, 512], P(('grp', 'dat'), 'seq', 'head'), parts along dimension 0, may hold values from -6 to 6
- values: bfloat16 [4, 256, 512], P(('grp', 'dat'), 'seq', 'head'), parts along dimension 0, may hold values from -6 to 6
- residual_in: bfloat16 [4, 256, 3072], P(('grp', 'dat'), 'seq', 'head'), parts along dimension 0, may hold values from -40 to 40
- out_proj: bfloat16 [24, 128, 3072], P('head', 'seq'), may hold values from -0.5 to 0.5
- norm_gain: bfloat16 [3072], replicated, may hold values from 0.5 to 1.5
- expert_gate: bfloat16 [4, 3072, 8192], P('head', None, 'seq'), may hold values from -0.109375 to 0.109375
- expert_up: bfloat16 [4, 3072, 8192], P('head', None, 'seq'), may hold values from -0.109375 to 0.109375
- routes: int32 [4, 256, 2], P(('grp', 'dat'), 'seq'), parts along dimension 0, may hold values from 0 to 3, as said below
- gate_numer: int32 [4, 256], P(('grp', 'dat'), 'seq'), parts along dimension 0, may hold values from 64 to 191
- sequence_lengths: int32 [4], P(('grp', 'dat')), parts along dimension 0, may hold values from 128 to 256, as said below
Outputs:
- stream: bfloat16 [4, 256, 3072], P(('grp', 'dat'), 'seq', 'head'), parts along dimension 0
- expert_hidden: bfloat16 [4, 4, 160, 8192], P('head', ('grp', 'dat'), None, 'seq'), parts along dimension 1
There are 2 independent parts, one for each index of `grp`. A program takes and returns all parts, laid end to end along the dimension named above; an argument that names none is the same for every part. Nothing has to cross between parts.
Inputs may be any that keep to these rules, and one draw needn't show every extreme that they name: `routes`: for each sequence one expert is named by exactly 40 tokens of every aligned block of 64 positions, every other expert by at most 40 tokens of such a block; the two experts of a token differ. `sequence_lengths`: one sequence of the batch has the full length 256.
All inputs are finite; a program needn't handle non-finite values.
Results may differ from a plain program's by a relative error of at most 0.019.
Values may be sent and summed in bfloat16 or wider, within the bound.
No kernel may reach another device: no remote copies, remote signals or barrier semaphores. Data moves between devices by JAX's collectives and lax.ppermute only.
A program may use at most 128 MiB of HBM per device.

v0:
```python
import math

import jax
import jax.numpy as jnp
from jax import lax
from jax.sharding import PartitionSpec as P

D = 3072
QUERY_HEAD_COUNT = 24
KEY_VALUE_HEADS = 4
HEAD_SIZE = 128
MOST = 40


EPS = 1e-05
NEG = -1e30


def slot_sources(marked, capacity):
    tok_len = marked.shape[1]
    counted = jnp.cumsum(marked, axis=1)
    rank_ids = jnp.arange(capacity, dtype=jnp.int32)
    source = jnp.sum((counted[:, None, :] <= rank_ids[None, :, None]).astype(jnp.int32), axis=2)
    filled = rank_ids[None, :] < counted[:, -1:]
    source = jnp.minimum(source, tok_len - 1)
    return (source, filled)


def expert_rows(rows_in, slot_gate, gate_matrix, up_matrix):
    gate_part = jnp.dot(rows_in, gate_matrix, preferred_element_type=jnp.float32)
    up_part = jnp.dot(rows_in, up_matrix, preferred_element_type=jnp.float32)
    return (slot_gate[:, None] * (jax.nn.silu(gate_part) * up_part)).astype(jnp.bfloat16)


def local(
    queries,
    keys,
    values,
    residual_in,
    out_proj,
    norm_gain,
    expert_gate,
    expert_up,
    routes,
    gate_numer,
    sequence_lengths,
):
    tok_count = queries.shape[1]
    kv_local = keys.shape[2] // HEAD_SIZE
    heads_per_group = QUERY_HEAD_COUNT // KEY_VALUE_HEADS
    seq_rank = lax.axis_index("seq")
    head_rank = lax.axis_index("head")
    query_pos = seq_rank * tok_count + jnp.arange(tok_count, dtype=jnp.int32)
    valid_len = sequence_lengths[0]
    score_scale = 1.0 / math.sqrt(HEAD_SIZE)
    query_heads = queries[0].reshape(tok_count, kv_local, heads_per_group, HEAD_SIZE)
    top_score = jnp.full((kv_local, heads_per_group, tok_count), NEG, jnp.float32)
    key_part = lax.all_gather(keys, "seq", axis=1, tiled=True)
    value_part = lax.all_gather(values, "seq", axis=1, tiled=True)
    part_len = key_part.shape[1]
    key_heads = key_part[0].reshape(part_len, kv_local, HEAD_SIZE)
    value_heads = value_part[0].reshape(part_len, kv_local, HEAD_SIZE)
    scores = (
        jnp.einsum("tghd,ngd->ghtn", query_heads, key_heads, preferred_element_type=jnp.float32)
        * score_scale
    )
    key_pos = jnp.arange(part_len, dtype=jnp.int32)
    allowed = (key_pos[None, :] <= query_pos[:, None]) & (key_pos < valid_len)[None, :]
    scores = jnp.where(allowed, scores, NEG)
    new_top = jnp.maximum(top_score, jnp.max(scores, axis=-1))
    weights = jnp.where(allowed, jnp.exp(scores - new_top[..., None]), 0.0)
    denom_sum = jnp.sum(weights, axis=-1)
    weighted = jnp.einsum(
        "ghtn,ngd->ghtd",
        weights.astype(jnp.bfloat16),
        value_heads,
        preferred_element_type=jnp.float32,
    )
    top_score, denom_sum, weighted = (new_top, denom_sum, weighted)
    attended_values = (weighted / denom_sum[..., None]).astype(jnp.bfloat16)
    attn_heads = attended_values.transpose(2, 0, 1, 3).reshape(
        tok_count, kv_local * heads_per_group, HEAD_SIZE
    )
    proj_part = lax.all_gather(out_proj, "seq", axis=1, tiled=True)
    mixed_sum = jnp.einsum("thd,hdc->tc", attn_heads, proj_part, preferred_element_type=jnp.float32)
    share_width = residual_in.shape[2]
    col_start = head_rank * share_width
    own_input = residual_in[0].astype(jnp.float32)
    shared = lax.psum_scatter(
        mixed_sum.astype(jnp.bfloat16), "head", scatter_dimension=1, tiled=True
    ).astype(jnp.float32)
    stream_share = (own_input + shared).astype(jnp.bfloat16)
    as_float = stream_share.astype(jnp.float32)
    squares = lax.psum(jnp.sum(as_float * as_float, axis=1, keepdims=True), "head")
    gain_part = lax.dynamic_slice_in_dim(norm_gain, col_start, share_width, 0).astype(jnp.float32)
    normed_part = (as_float * lax.rsqrt(squares / D + EPS) * gain_part).astype(jnp.bfloat16)
    normed = lax.all_gather(normed_part, "head", axis=1, tiled=True)
    local_experts = expert_gate.shape[0]
    expert_ids = head_rank * local_experts + jnp.arange(local_experts, dtype=jnp.int32)
    first_weight = gate_numer[0].astype(jnp.float32) / 256.0
    route_first = routes[0, :, 0]
    route_second = routes[0, :, 1]
    token_gates = jnp.where(
        route_first[:, None] == expert_ids[None, :], first_weight[:, None], 0.0
    ) + jnp.where(route_second[:, None] == expert_ids[None, :], 1.0 - first_weight[:, None], 0.0)
    capacity = MOST
    packed_rows = []
    packed_gates = []
    for expert_slot in range(local_experts):
        marked = (token_gates[:, expert_slot] > 0).astype(jnp.int32)[None, :]
        source, filled = slot_sources(marked, capacity)
        packed_rows.append(jnp.take(normed, source[0], axis=0))
        packed_gates.append(
            jnp.where(filled[0], jnp.take(token_gates[:, expert_slot], source[0]), 0.0).astype(
                jnp.bfloat16
            )
        )
    stacked_rows = jnp.stack(packed_rows)
    stacked_gates = jnp.stack(packed_gates)
    rows_out, gates_out = (
        lax.all_gather(stacked_rows, "seq", axis=1, tiled=True),
        lax.all_gather(stacked_gates, "seq", axis=1, tiled=True),
    )
    outputs = []
    for expert_slot in range(local_experts):
        outputs.append(
            expert_rows(
                rows_out[expert_slot],
                gates_out[expert_slot].astype(jnp.float32),
                expert_gate[expert_slot],
                expert_up[expert_slot],
            )
        )
    hidden = jnp.stack(outputs)
    return (stream_share[None], hidden[:, None])


def solution(mesh):
    in_specs = (
        P(("grp", "dat"), "seq", "head"),
        P(("grp", "dat"), "seq", "head"),
        P(("grp", "dat"), "seq", "head"),
        P(("grp", "dat"), "seq", "head"),
        P("head", "seq", None),
        P(),
        P("head", None, "seq"),
        P("head", None, "seq"),
        P(("grp", "dat"), "seq", None),
        P(("grp", "dat"), "seq"),
        P(("grp", "dat")),
    )
    out_specs = (P(("grp", "dat"), "seq", "head"), P("head", ("grp", "dat"), None, "seq"))
    return jax.shard_map(local, mesh=mesh, in_specs=in_specs, out_specs=out_specs, check_vma=False)
```

profile of v0, /device:TPU:0, one launch (start us, length us, event | category | flops | bytes accessed | tf_op | source)
XLA Modules:
  0.0 293.6 jit_solution(12492824044068273958)
XLA Ops:
  7.3 0.7 all-gather.4.cloned.1.call-update
  8.7 15.1 %all_gather.18 = bf16[1,256,256]{2,1,0:T(8,128)(2,1)S(1)} all-gather(bf16[1,64,256]{2,1,0:T(8,128)(2,1)S(1)} %copy-done.2), channel_id=1, replica_groups=mesh['grp'=2,'seq'=4,'head'=2,'dat'=2] {'seq'}, dimensions={1}, use_global_device_ids=true | all-gather | bytes 163840 | tf_op jit(solution)/shard_map/all_gather | solution.py:58
  24.1 19.6 %all_gather.19 = bf16[1,256,256]{2,1,0:T(8,128)(2,1)S(1)} all-gather(bf16[1,64,256]{2,1,0:T(8,128)(2,1)S(1)} %copy-done.3), channel_id=1, replica_groups=mesh['grp'=2,'seq'=4,'head'=2,'dat'=2] {'seq'}, dimensions={1}, use_global_device_ids=true | all-gather | bytes 163840 | tf_op jit(solution)/shard_map/all_gather | solution.py:59
  45.7 135.4 %all-gather.4.cloned.1.call-done = bf16[12,128,3072]{2,1,0:T(8,128)(2,1)} async-done(((bf16[12,32,3072]{2,1,0:T(8,128)(2,1)}), bf16[12,128,3072]{2,1,0:T(8,128)(2,1)}) %all-gather.4.cloned.1.call-update) | async-done | bytes 9437200 | tf_op jit(solution)/shard_map/all_gather | solution.py:84
  181.1 6.2 %fusion.12 = bf16[64,3072]{1,0:T(8,128)(2,1)} fusion(bf16[64,12,128]{2,0,1:T(8,128)(2,1)S(1)} %bitcast.128, bf16[12,128,3072]{2,1,0:T(8,128)(2,1)} %all-gather.4.cloned.1.call-done), kind=kOutput, calls=%fused_computation.17 | convolution fusion | flops 604176384 | bytes 10027008 | tf_op jit(solution)/shard_map/thd,hdc->tc/dot_general | solution.py:85
  187.7 11.3 %reduce-scatter.2.cloned.1.call-done = bf16[64,1536]{1,0:T(8,128)(2,1)} async-done(((bf16[64,3072]{1,0:T(8,128)(2,1)}), bf16[64,1536]{1,0:T(8,128)(2,1)}) %reduce-scatter.2.cloned.1.call-update) | async-done | bytes 196624 | tf_op jit(solution)/shard_map/reduce_scatter | solution.py:89
  198.9 1.1 fusion.43
  200.1 4.9 %psum.7 = f32[64,1]{0,1:T(1,128)S(1)} all-reduce(f32[64,1]{0,1:T(1,128)S(1)} %bitcast.134), channel_id=1, replica_groups=mesh['grp'=2,'seq'=4,'head'=2,'dat'=2] {'head'}, use_global_device_ids=true, to_apply=%region_8.10 | all-reduce | flops 64 | bytes 512 | tf_op jit(solution)/shard_map/psum | solution.py:94
  205.0 1.7 fusion.45
  206.7 6.3 %all_gather.22 = bf16[64,3072]{1,0:T(8,128)(2,1)S(1)} all-gather(bf16[64,1536]{1,0:T(8,128)(2,1)S(1)} %get-tuple-element.16), channel_id=1, replica_groups=mesh['grp'=2,'seq'=4,'head'=2,'dat'=2] {'head'}, dimensions={1}, use_global_device_ids=true | all-gather | bytes 589824 | tf_op jit(solution)/shard_map/all_gather | solution.py:97
  213.0 0.7 gather_fusion.2
  213.7 0.7 gather_fusion.3
  214.5 0.8 pad_maximum_fusion
  215.4 0.6 slice.47
  216.6 0.8 gather_fusion
  217.4 0.8 gather_fusion.1
  218.2 1.2 fusion.56
  219.4 10.9 %all-gather = bf16[4,40,2]{1,2,0:T(2,128)(2,1)S(1)} all-gather(bf16[1,40,2]{1,2,0:T(2,128)(2,1)S(1)} %maximum_bitcast_fusion.1), channel_id=1, replica_groups=mesh['grp'=2,'seq'=4,'head'=2,'dat'=2] {'seq'}, dimensions={0}, use_global_device_ids=true | all-gather | bytes 800 | tf_op jit(solution)/shard_map/all_gather | solution.py:122
  230.5 28.6 %all-gather.6.cloned.1.call-done = bf16[2,160,3072]{2,1,0:T(8,128)(2,1)} async-done(((bf16[2,40,3072]{2,1,0:T(8,128)(2,1)}), bf16[2,160,3072]{2,1,0:T(8,128)(2,1)}) %all-gather.6.cloned.1.call-update) | async-done | bytes 1966096 | tf_op jit(solution)/shard_map/all_gather | solution.py:121
  259.1 7.0 %fusion.6 = f32[160,2048]{1,0:T(8,128)S(1)} fusion(bf16[2,3072,2048]{2,1,0:T(8,128)(2,1)} %param.21, bf16[2,160,3072]{2,1,0:T(8,128)(2,1)} %all-gather.6.cloned.1.call-done), kind=kOutput, calls=%fused_computation.10 | convolution fusion | flops 2013265920 | bytes 14876672 | tf_op jit(solution)/shard_map/dot_general | solution.py:30
  266.1 5.8 %fusion.2 = f32[160,2048]{1,0:T(8,128)S(1)} fusion(bf16[2,3072,2048]{2,1,0:T(8,128)(2,1)} %param.21, bf16[2,160,3072]{2,1,0:T(8,128)(2,1)S(1)} %copy-done.6), kind=kOutput, calls=%fused_computation.6 | convolution fusion | flops 2013265920 | bytes 14876672 | tf_op jit(solution)/shard_map/dot_general | solution.py:30
  272.0 7.0 %fusion.31 = bf16[1,160,2048]{2,1,0:T(8,128)(2,1)S(1)} fusion(bf16[2,3072,2048]{2,1,0:T(8,128)(2,1)} %param.22, f32[160,2048]{1,0:T(8,128)S(1)} %fusion.6, bf16[2,160,3072]{2,1,0:T(8,128)(2,1)S(1)} %copy-done.6, f32[160]{0:T(256)S(1)} %bitcast.133), kind=kOutput, calls=%fused_computation.24 | convolution fusion | flops 2015559680 | bytes 15533056 | tf_op jit(solution)/shard_map/dot_general | solution.py:31
  279.0 7.0 %fusion.34 = bf16[1,160,2048]{2,1,0:T(8,128)(2,1)S(1)} fusion(bf16[2,3072,2048]{2,1,0:T(8,128)(2,1)} %param.22, f32[160,2048]{1,0:T(8,128)S(1)} %fusion.2, bf16[2,160,3072]{2,1,0:T(8,128)(2,1)S(1)} %copy-done.6, f32[160]{0:T(256)S(1)} %bitcast.132), kind=kOutput, calls=%fused_computation.25 | convolution fusion | flops 2015559680 | bytes 15533056 | tf_op jit(solution)/shard_map/dot_general | solution.py:31
  285.9 1.2 maximum_bitcast_fusion
  (54 shorter events, 3.5 us)
Async XLA Ops:
  7.2 1.5 copy-start.2
  7.2 16.7 %copy-start.1 = (bf16[1,64,1536]{2,1,0:T(8,128)(2,1)S(1)}, bf16[1,64,1536]{2,1,0:T(8,128)(2,1)}, u32[]{:S(2)}) copy-start(bf16[1,64,1536]{2,1,0:T(8,128)(2,1)} %param.15) | copy-start | bytes 589828
  7.2 16.9 %copy-start.3 = (bf16[1,64,256]{2,1,0:T(8,128)(2,1)S(1)}, bf16[1,64,256]{2,1,0:T(8,128)(2,1)}, u32[]{:S(2)}) copy-start(bf16[1,64,256]{2,1,0:T(8,128)(2,1)} %param.17) | copy-start | bytes 98308
  7.2 36.7 %copy-start.7 = (s32[1,64]{1,0:T(1,128)S(1)}, s32[1,64]{1,0:T(1,128)}, u32[]{:S(2)}) copy-start(s32[1,64]{1,0:T(1,128)} %param.24) | copy-start | bytes 772
  7.2 36.7 %copy-start.5 = (s32[1,64,2]{1,2,0:T(2,128)S(1)}, s32[1,64,2]{1,2,0:T(2,128)}, u32[]{:S(2)}) copy-start(s32[1,64,2]{1,2,0:T(2,128)} %param.23) | copy-start | bytes 1540
  7.2 173.9 %all-gather.4.cloned.1.call-start = ((), (), s32[]{:S(2)}) async-start(), calls=%async_computation.1 | async-start | bytes 11796480 | tf_op jit(solution)/shard_map/all_gather | solution.py:84
  7.9 191.0 %reduce-scatter.2.cloned.1.call-start = ((), (), s32[]{:S(2)}) async-start(), calls=%async_computation.2 | async-start | bytes 589824 | tf_op jit(solution)/shard_map/reduce_scatter | solution.py:89
  181.1 6.5 %copy-start.4 = (bf16[3072]{0:T(1024)(128)(2,1)S(1)}, bf16[3072]{0:T(1024)(128)(2,1)}, u32[]{:S(2)}) copy-start(bf16[3072]{0:T(1024)(128)(2,1)} %param.20) | copy-start | bytes 18436
  181.1 17.8 %copy-start = (bf16[1,64,1536]{2,1,0:T(8,128)(2,1)S(1)}, bf16[1,64,1536]{2,1,0:T(8,128)(2,1)}, u32[]{:S(2)}) copy-start(bf16[1,64,1536]{2,1,0:T(8,128)(2,1)} %param.18) | copy-start | bytes 589828
  187.3 71.7 %all-gather.6.cloned.1.call-start = ((), (), s32[]{:S(2)}) async-start(), calls=%async_computation.3 | async-start | bytes 2457600 | tf_op jit(solution)/shard_map/all_gather | solution.py:121
  259.1 7.0 %copy-start.6 = (bf16[2,160,3072]{2,1,0:T(8,128)(2,1)S(1)}, bf16[2,160,3072]{2,1,0:T(8,128)(2,1)}, u32[]{:S(2)}) copy-start(bf16[2,160,3072]{2,1,0:T(8,128)(2,1)} %all-gather.6.cloned.1.call-done) | copy-start | bytes 5898244
Sparse Core Ops, SparseCore 0:
  9.6 171.4 all-gather.3
  187.5 11.4 reduce-scatter.1
  215.5 43.5 all-gather.5
where the time goes:
time: 294 us
  waiting for transfers between devices  176 us (60%)
  blocking collectives  56.9 us (19%)
  matrix products  33.7 us (11%)
  between operations  14.7 us (5%)
  other arithmetic  7.48 us (3%)
  local copies, waits for them, and re-layouts  4.78 us (2%)
    all_gather x1, waiting for transfers between devices, local(): proj_part = lax.all_gather(out_proj, 'seq', axis=1, tiled=True)  135 us
    all_gather x1, waiting for transfers between devices, local(): lax.all_gather(stacked_rows, 'seq', axis=1, tiled=True)  28.6 us
    all_gather x1, blocking collectives, local(): value_part = lax.all_gather(values, 'seq', axis=1, tiled=True)  19.6 us
    all_gather x1, blocking collectives, local(): key_part = lax.all_gather(keys, 'seq', axis=1, tiled=True)  15.1 us
    dot_general x2, matrix products, expert_rows(): up_part = jnp.dot(rows_in, up_matrix, preferred_element_type=jnp.float32)  14 us
    dot_general x2, matrix products, expert_rows(): jnp.dot(rows_in, gate_matrix, preferred_element_type=jnp.float32)  12.9 us
    reduce_scatter x1, waiting for transfers between devices, local(): lax.psum_scatter(mixed_sum.astype(jnp.bfloat16), 'head', scatter_dimensio...  11.3 us
    all_gather x1, blocking collectives, local(): lax.all_gather(stacked_gates, 'seq', axis=1, tiled=True)  10.9 us
  transfers between devices with their start and end apart: 3, of which 3 were waited for; matrix products, arithmetic and copies ran while one was open for 2% of the time, Pallas kernels for 0%

commit v1 on v0

v1 whole, which is shorter than its diff:
```python
import functools
import math

import jax
import jax.numpy as jnp
from jax import lax
from jax.experimental import pallas as pl
from jax.experimental.pallas import tpu as pltpu
from jax.sharding import PartitionSpec as P

HEAD_SIZE = 128
QUERY_HEAD_COUNT = 24
KEY_VALUE_HEADS = 4
MOST = 40
EPS = 1e-05
NEG = -1e30
F32 = jnp.float32
BF16 = jnp.bfloat16

VMEM = pl.BlockSpec(memory_space=pltpu.VMEM)
SMEM = pl.BlockSpec(memory_space=pltpu.SMEM)
ANY = pl.BlockSpec(memory_space=pl.ANY)


def pairwise(count):
    return count in (1, 2, 4)


def swap(array, axis, step, upward=False):
    count = lax.axis_size(axis)
    pairs = [(i, i ^ step) for i in range(count) if not upward or i < i ^ step]
    return lax.ppermute(array, axis, pairs)


def spread(array, axis, upward=False):
    count = lax.axis_size(axis)
    if pairwise(count):
        return [array] + [swap(array, axis, k, upward) for k in range(1, count)]
    return [lax.all_gather(array, axis, axis=0, tiled=True)]


def attention_kernel(shape, info, queries, own_keys, own_values, *refs):
    tokens, groups, per_group, pieces, split = shape
    kv_refs, outs = refs[:pieces], refs[pieces:]
    rank, flip, valid_len = info[0], info[1], info[2]
    width = groups * HEAD_SIZE
    if split:
        key_parts = [own_keys[...]] + [ref[:, :width] for ref in kv_refs]
        value_parts = [own_values[...]] + [ref[:, width:] for ref in kv_refs]
    else:
        key_parts = [ref[:, :width] for ref in kv_refs]
        value_parts = [ref[:, width:] for ref in kv_refs]
    all_keys = jnp.concatenate(key_parts, axis=0)
    all_values = jnp.concatenate(value_parts, axis=0)
    length = all_keys.shape[0]
    column = lax.broadcasted_iota(jnp.int32, (tokens, length), 1)
    block = lax.div(column, tokens)
    key_pos = lax.bitwise_xor(block, flip) * tokens + (column - block * tokens)
    query_pos = rank * tokens + lax.broadcasted_iota(jnp.int32, (tokens, length), 0)
    allowed = ((key_pos <= query_pos) & (key_pos < valid_len)).astype(F32)
    allowed = jnp.concatenate([allowed] * per_group, axis=0) > 0
    scale = 1.0 / math.sqrt(HEAD_SIZE)
    attended = []
    for g in range(groups):
        heads = [g * per_group + a for a in range(per_group)]
        rows = jnp.concatenate(
            [queries[:, h * HEAD_SIZE : (h + 1) * HEAD_SIZE] for h in heads], axis=0
        )
        lanes = slice(g * HEAD_SIZE, (g + 1) * HEAD_SIZE)
        scores = (
            lax.dot_general(
                rows, all_keys[:, lanes], (((1,), (1,)), ((), ())), preferred_element_type=F32
            )
            * scale
        )
        scores = jnp.where(allowed, scores, NEG)
        top = jnp.max(scores, axis=-1, keepdims=True)
        weights = jnp.where(allowed, jnp.exp(scores - top), 0.0)
        denom = jnp.sum(weights, axis=-1, keepdims=True)
        mixed = jnp.dot(weights.astype(BF16), all_values[:, lanes], preferred_element_type=F32)
        mixed = mixed / denom
        attended += [mixed[a * tokens : (a + 1) * tokens] for a in range(per_group)]
    if not split:
        outs[0][...] = jnp.concatenate(attended, axis=1).astype(BF16)
        return
    count = len(outs)
    part = HEAD_SIZE // count
    shares = [
        jnp.concatenate([o[:, j * part : (j + 1) * part] for o in attended], axis=1).astype(BF16)
        for j in range(count)
    ]
    for k in range(count):
        chosen = shares[k]
        for s in range(1, count):
            chosen = jnp.where(rank == s, shares[s ^ k], chosen)
        outs[k][...] = chosen


def attend(info, queries, keys, values, kv_parts, count):
    tokens = queries.shape[0]
    groups = keys.shape[1] // HEAD_SIZE
    per_group = QUERY_HEAD_COUNT // KEY_VALUE_HEADS
    split = pairwise(count)
    if split:
        out_shape = [
            jax.ShapeDtypeStruct((tokens, queries.shape[1] // count), BF16) for _ in range(count)
        ]
    else:
        out_shape = [jax.ShapeDtypeStruct(queries.shape, BF16)]
    length = tokens * count
    return pl.pallas_call(
        functools.partial(
            attention_kernel, (tokens, groups, per_group, len(kv_parts), split)
        ),
        out_shape=out_shape,
        in_specs=[SMEM] + [VMEM] * (3 + len(kv_parts)),
        out_specs=[VMEM] * len(out_shape),
        compiler_params=pltpu.CompilerParams(vmem_limit_bytes=32 << 20),
        cost_estimate=pl.CostEstimate(
            flops=4 * tokens * length * queries.shape[1],
            bytes_accessed=4 * queries.size + 4 * length * keys.shape[1],
            transcendentals=tokens * length * groups * per_group,
        ),
        name="attention",
    )(info, queries, keys, values, *kv_parts)


def project_kernel(parts, pieces, keep, *refs):
    rows = [refs[m * pieces : (m + 1) * pieces] for m in range(parts)]
    weights = refs[parts * pieces : parts * pieces + parts]
    outs = refs[parts * pieces + parts :]
    total = None
    for m in range(parts):
        stacked = jnp.concatenate([ref[...] for ref in rows[m]], axis=0)
        product = jnp.dot(stacked, weights[m][...], preferred_element_type=F32)
        total = product if total is None else total + product
    at = 0
    for i, out in enumerate(outs):
        out[...] = total[at : at + out.shape[0]].astype(out.dtype)
        at += out.shape[0]


def project(rows, weights, split):
    parts, pieces = len(rows), len(rows[0])
    width = weights[0].shape[1]
    tokens = sum(p.shape[0] for p in rows[0])
    out_shape = [
        jax.ShapeDtypeStruct((p.shape[0], width), BF16 if split and i else F32)
        for i, p in enumerate(rows[0])
    ]
    flat = [p for part in rows for p in part]
    return pl.pallas_call(
        functools.partial(project_kernel, parts, pieces, split),
        out_shape=out_shape,
        in_specs=[VMEM] * (len(flat) + parts),
        out_specs=[VMEM] * pieces,
        compiler_params=pltpu.CompilerParams(vmem_limit_bytes=40 << 20),
        cost_estimate=pl.CostEstimate(
            flops=2 * tokens * width * parts * weights[0].shape[0],
            bytes_accessed=2 * parts * weights[0].size + 4 * tokens * width,
            transcendentals=0,
        ),
        name="projection",
    )(*flat, *weights)


def expert_kernel(shape, info, *refs):
    tokens, group, parts, pieces, experts, slots, chunk, depth = shape
    columns = [refs[m * pieces : (m + 1) * pieces] for m in range(parts)]
    refs = refs[parts * pieces :]
    routing, refs = refs[:pieces], refs[pieces:]
    gain, gate_hbm, up_hbm, hidden, chosen, factors, buffers, sems = refs
    flip, head = info[0], info[1]
    features = gate_hbm.shape[1]
    width = features // parts
    per_expert = gate_hbm.shape[2] // chunk
    steps = experts * per_expert

    def copies(step, slot):
        e = step // per_expert
        at = pl.ds(pl.multiple_of((step % per_expert) * chunk, chunk), chunk)
        return (
            pltpu.make_async_copy(gate_hbm.at[e, :, at], buffers.at[slot, 0], sems.at[slot, 0]),
            pltpu.make_async_copy(up_hbm.at[e, :, at], buffers.at[slot, 1], sems.at[slot, 1]),
        )

    for step in range(min(depth, steps)):
        for copy in copies(step, step):
            copy.start()

    blocks = sum(ref.shape[0] for ref in routing) // 8
    size = group * tokens
    slot_row = lax.broadcasted_iota(jnp.int32, (group * slots, size), 0)
    token_col = lax.broadcasted_iota(jnp.int32, (group * slots, size), 1)
    row_block = lax.div(slot_row, slots)
    row_rank = slot_row - row_block * slots
    col_block = lax.bitwise_xor(lax.div(token_col, tokens), flip)
    same_block = row_block == col_block
    before_row = lax.broadcasted_iota(jnp.int32, (size, size), 0)
    before_col = lax.broadcasted_iota(jnp.int32, (size, size), 1)
    before = (
        (before_row < before_col)
        & (lax.div(before_row, tokens) == lax.div(before_col, tokens))
    ).astype(BF16)
    ranks = lax.broadcasted_iota(jnp.int32, (8, size), 0)
    for g in range(blocks // group):
        if pieces > 1:
            route = jnp.concatenate([ref[...] for ref in routing], axis=1)
        else:
            route = jnp.concatenate(
                [routing[0][(g * group + b) * 8 : (g * group + b) * 8 + 8] for b in range(group)],
                axis=1,
            )
        first, second, numer = route[0:1], route[1:2], route[2:3]
        weight = numer.astype(F32) / 256.0
        gate_rows = []
        for e in range(experts):
            expert = head * experts + e
            gate_rows.append(
                jnp.where(first == expert, weight, 0.0)
                + jnp.where(second == expert, 1.0 - weight, 0.0)
            )
        marked = jnp.zeros((8, size), F32)
        for e in range(experts):
            marked = jnp.where(ranks == e, (gate_rows[e] > 0).astype(F32), marked)
        counted = jnp.dot(marked.astype(BF16), before, preferred_element_type=F32)
        pick = []
        for e in range(experts):
            hit = (
                same_block
                & (counted[e : e + 1].astype(jnp.int32) == row_rank)
                & (gate_rows[e] > 0)
            )
            pick.append(hit.astype(BF16))
            at = slice(g * group * slots, (g + 1) * group * slots)
            factors[e, at, :] = jnp.sum(
                jnp.where(hit, gate_rows[e], 0.0), axis=1, keepdims=True
            )
        picks = jnp.concatenate(pick, axis=0)
        values = []
        squares = None
        for m in range(parts):
            if pieces > 1:
                raw = jnp.concatenate([ref[...] for ref in columns[m]], axis=0)
            else:
                raw = columns[m][0][g * size : (g + 1) * size]
            raw = raw.astype(F32)
            part = jnp.sum(raw * raw, axis=1, keepdims=True)
            squares = part if squares is None else squares + part
            values.append(raw)
        scale = lax.rsqrt(squares / features + EPS)
        for m in range(parts):
            place = lax.bitwise_xor(head, m)
            normed = (values[m] * scale * gain[place].astype(F32)).astype(BF16)
            rows = jnp.dot(picks, normed, preferred_element_type=F32).astype(BF16)
            for e in range(experts):
                at = slice(g * group * slots, (g + 1) * group * slots)
                chosen[place, e, at, :] = rows[e * group * slots : (e + 1) * group * slots]

    @pl.loop(0, steps)
    def _(step):
        slot = lax.rem(step, depth)
        e = step // per_expert
        for copy in copies(step, slot):
            copy.wait()
        gate_part = up_part = None
        for p in range(parts):
            at = slice(p * width, (p + 1) * width)
            rows = chosen[p, e]
            a = jnp.dot(rows, buffers[slot, 0, at, :], preferred_element_type=F32)
            b = jnp.dot(rows, buffers[slot, 1, at, :], preferred_element_type=F32)
            gate_part = a if gate_part is None else gate_part + a
            up_part = b if up_part is None else up_part + b
        result = factors[e] * (gate_part / (1.0 + jnp.exp(-gate_part)) * up_part)
        at = pl.ds(pl.multiple_of((step % per_expert) * chunk, chunk), chunk)
        hidden[e, :, at] = result.astype(BF16)

        @pl.when(step + depth < steps)
        def _():
            for copy in copies(step + depth, slot):
                copy.start()


def run_experts(info, columns, routing, gain, expert_gate, expert_up, tokens, count):
    parts, pieces = len(columns), len(routing)
    experts, features, hidden_units = expert_gate.shape
    group = min(4, count)
    chunk = min(512, hidden_units)
    steps = experts * (hidden_units // chunk)
    depth = min(4, steps)
    slots = MOST * count
    shape = (tokens, group, parts, pieces, experts, MOST, chunk, depth)
    flat = [p for part in columns for p in part]
    return pl.pallas_call(
        functools.partial(expert_kernel, shape),
        out_shape=jax.ShapeDtypeStruct((experts, slots, hidden_units), BF16),
        in_specs=[SMEM] + [VMEM] * (len(flat) + pieces + 1) + [ANY, ANY],
        out_specs=VMEM,
        scratch_shapes=[
            pltpu.VMEM((parts, experts, slots, features // parts), BF16),
            pltpu.VMEM((experts, slots, 1), F32),
            pltpu.VMEM((depth, 2, features, chunk), BF16),
            pltpu.SemaphoreType.DMA((depth, 2)),
        ],
        compiler_params=pltpu.CompilerParams(vmem_limit_bytes=56 << 20),
        cost_estimate=pl.CostEstimate(
            flops=4 * experts * slots * features * hidden_units,
            bytes_accessed=4 * expert_gate.size,
            transcendentals=experts * slots * hidden_units,
        ),
        name="experts",
    )(info, *flat, *routing, gain, expert_gate, expert_up)


def local(
    queries,
    keys,
    values,
    residual_in,
    out_proj,
    norm_gain,
    expert_gate,
    expert_up,
    routes,
    gate_numer,
    sequence_lengths,
):
    tokens = queries.shape[1]
    count = lax.axis_size("seq")
    head_count = lax.axis_size("head")
    seq_rank = lax.axis_index("seq")
    head_rank = lax.axis_index("head")
    split = pairwise(count)
    flip = seq_rank if split else jnp.zeros_like(seq_rank)
    share = residual_in.shape[2]
    features = out_proj.shape[2]
    heads, part, _ = out_proj.shape

    own_kv = jnp.concatenate([keys[0], values[0]], axis=1)
    kv_parts = spread(own_kv, "seq", upward=True)
    if split:
        kv_parts = kv_parts[1:]

    matrix = out_proj.reshape(heads * part, features)

    def columns_of(rank):
        return lax.dynamic_slice_in_dim(matrix, rank * share, share, 1)

    weights = [columns_of(head_rank)] + [
        swap(columns_of(lax.bitwise_xor(head_rank, m)), "head", m) for m in range(1, head_count)
    ]

    routing = jnp.concatenate(
        [routes[0].T, gate_numer, jnp.zeros((5, tokens), jnp.int32)], axis=0
    )
    routing = spread(routing, "seq")

    info = jnp.stack([seq_rank, flip, sequence_lengths[0]]).astype(jnp.int32)
    attended = attend(info, queries[0], keys[0], values[0], kv_parts, count)
    if split:
        attended = [attended[0]] + [swap(attended[k], "seq", k) for k in range(1, count)]
    else:
        shares = attended[0].reshape(tokens, heads, count, part).transpose(2, 0, 1, 3)
        shares = shares.reshape(count * tokens, heads * part)
        attended = [lax.all_to_all(shares, "seq", 0, 0, tiled=True)]
    rows = [attended] + [
        [swap(piece, "head", m) for piece in attended] for m in range(1, head_count)
    ]
    sums = project(rows, weights, split)
    if split:
        mixed = sums[0]
        for k in range(1, count):
            mixed = mixed + swap(sums[k], "seq", k).astype(F32)
    else:
        mixed = lax.psum_scatter(sums[0], "seq", scatter_dimension=0, tiled=True)
    stream = (residual_in[0].astype(F32) + mixed).astype(BF16)

    own_columns = spread(stream, "seq")
    columns = [own_columns] + [
        [swap(piece, "head", m) for piece in own_columns] for m in range(1, head_count)
    ]
    gain = norm_gain.reshape(head_count, 1, share)
    place = jnp.stack([flip, head_rank]).astype(jnp.int32)
    hidden = run_experts(place, columns, routing, gain, expert_gate, expert_up, tokens, count)
    return (stream[None], hidden[:, None])


def solution(mesh):
    in_specs = (
        P(("grp", "dat"), "seq", "head"),
        P(("grp", "dat"), "seq", "head"),
        P(("grp", "dat"), "seq", "head"),
        P(("grp", "dat"), "seq", "head"),
        P("head", "seq", None),
        P(),
        P("head", None, "seq"),
        P("head", None, "seq"),
        P(("grp", "dat"), "seq", None),
        P(("grp", "dat"), "seq"),
        P(("grp", "dat")),
    )
    out_specs = (P(("grp", "dat"), "seq", "head"), P("head", ("grp", "dat"), None, "seq"))
    return jax.shard_map(local, mesh=mesh, in_specs=in_specs, out_specs=out_specs, check_vma=False)
```

time: 294 us -> 113 us (0.38)
  waiting for transfers between devices: 176 us -> 39.6 us
  blocking collectives: 56.9 us -> 0 us
  starting transfers between devices: 0.12 us -> 43.9 us
  matrix products: 33.7 us -> 0 us
  Pallas kernels: 0 us -> 22.1 us
  between operations: 14.7 us -> 1.52 us
  other arithmetic: 7.48 us -> 0.91 us
    all_gather x2 -> x0, waiting for transfers between devices: 164 us -> none  [the longest x1 135 us: local(): proj_part = lax.all_gather(out_proj, 'seq', axis=1, tiled=True)]
    all_gather x4 -> x0, blocking collectives: 51.9 us -> none  [the longest x1 19.6 us: local(): value_part = lax.all_gather(values, 'seq', axis=1, tiled=True)]
    ppermute x0 -> x24, starting transfers between devices: none -> 43.9 us  [swap(): return lax.ppermute(array, axis, pairs)]
    ppermute x0 -> x24, waiting for transfers between devices: none -> 39.6 us  [swap(): return lax.ppermute(array, axis, pairs)]
    dot_general x7 -> x0, matrix products: 33.7 us -> none  [the longest x2 14 us: expert_rows(): up_part = jnp.dot(rows_in, up_matrix, preferred_element_type=jnp.float32)]
    pallas_call x0 -> x3, Pallas kernels: none -> 22.1 us  [the longest x1 19.7 us: run_experts(): pl.pallas_call(functools.partial(expert_kernel, shape), out_shape=jax.Sha...]
    reduce_scatter x1 -> x0, waiting for transfers between devices: 11.3 us -> none  [local(): lax.psum_scatter(mixed_sum.astype(jnp.bfloat16), 'head', scatter_dimensio...]
    psum x1 -> x0, blocking collectives: 4.94 us -> none  [local(): lax.psum(jnp.sum(as_float * as_float, axis=1, keepdims=True), 'head')]
  transfers between devices with their start and end apart: 3 -> 24, of which waited for: 3 -> 14; matrix products, arithmetic and copies ran while one was open for 2% -> 1% of each run, Pallas kernels for 0% -> 1%
where the time goes in v1:
time: 113 us
  starting transfers between devices  43.9 us (39%)
  waiting for transfers between devices  39.6 us (35%)
  Pallas kernels  22.1 us (20%)
  local copies, waits for them, and re-layouts  4.98 us (4%)
  between operations  1.52 us (1%)
    ppermute x24, starting transfers between devices, swap(): return lax.ppermute(array, axis, pairs)  43.9 us
    ppermute x24, waiting for transfers between devices, swap(): return lax.ppermute(array, axis, pairs)  39.6 us
    pallas_call x1, Pallas kernels, run_experts(): pl.pallas_call(functools.partial(expert_kernel, shape), out_shape=jax.Sha...  19.7 us
    dynamic_slice x1, local copies, waits for them, and re-layouts, columns_of(): return lax.dynamic_slice_in_dim(matrix, rank * share, share, 1)  2.84 us
  transfers between devices with their start and end apart: 24, of which 14 were waited for; matrix products, arithmetic and copies ran while one was open for 1% of the time, Pallas kernels for 1%

profile of v1, /device:TPU:0, one launch (start us, length us, event | category | flops | bytes accessed | tf_op | source)
XLA Modules:
  0.0 113.1 jit_solution(13784365496534360858)
XLA Ops:
  0.7 2.8 %constant_dynamic-slice_fusion = (bf16[384,1536]{1,0:T(8,128)(2,1)}, bf16[384,1536]{1,0:T(8,128)(2,1)S(1)}) fusion(bf16[384,3072]{1,0:T(8,128)(2,1)} %bitcast.21, s32[]{:T(128)S(6)} %select_n.7, s32[]{:T(128)S(6)} %select_n.6), kind=kLoop, calls=%fused_computation.6 | loop fusion | bytes 4718600 | tf_op jit(solution)/shard_map/dynamic_slice | solution.py:347
  3.5 2.9 %collective-permute-start.10 = (bf16[384,1536]{1,0:T(8,128)(2,1)}, bf16[384,1536]{1,0:T(8,128)(2,1)S(1)}, u32[]{:S(2)}, u32[]{:S(2)}) collective-permute-start(bf16[384,1536]{1,0:T(8,128)(2,1)} %get-tuple-element.22), channel_id=1, source_target_pairs={{0,2},{2,0},{1,3},{3,1},{4,6},{6,4},{5,7},{7,5},{8,10},{10,8},{9,1... | collective-permute-start | bytes 3538952 | tf_op jit(solution)/shard_map/ppermute | solution.py:32
  6.5 3.5 %collective-permute-start = (bf16[64,512]{1,0:T(8,128)(2,1)S(1)}, bf16[64,512]{1,0:T(8,128)(2,1)S(1)}, u32[]{:S(2)}, u32[]{:S(2)}) collective-permute-start(bf16[64,512]{1,0:T(8,128)(2,1)S(1)} %pad_maximum_fusion), channel_id=1, source_target_pairs={{0,4},{8,12},{1,5},{9,13},{2,6},{10,14},{3,7},{11,15},{16,20},{24,... | collective-permute-start | bytes 196616 | tf_op jit(solution)/shard_map/ppermute | solution.py:32
  10.0 4.5 %collective-permute-start.1 = (bf16[64,512]{1,0:T(8,128)(2,1)S(1)}, bf16[64,512]{1,0:T(8,128)(2,1)S(1)}, u32[]{:S(2)}, u32[]{:S(2)}) collective-permute-start(bf16[64,512]{1,0:T(8,128)(2,1)S(1)} %pad_maximum_fusion), channel_id=1, source_target_pairs={{0,8},{4,12},{1,9},{5,13},{2,10},{6,14},{3,11},{7,15},{16,24},{20,... | collective-permute-start | bytes 196616 | tf_op jit(solution)/shard_map/ppermute | solution.py:32
  19.1 2.2 %collective-permute-start.3 = (bf16[64,384]{1,0:T(8,128)(2,1)S(1)}, bf16[64,384]{1,0:T(8,128)(2,1)S(1)}, u32[]{:S(2)}, u32[]{:S(2)}) collective-permute-start(bf16[64,384]{1,0:T(8,128)(2,1)S(1)} %get-tuple-element.11), channel_id=1, source_target_pairs={{0,4},{4,0},{8,12},{12,8},{1,5},{5,1},{9,13},{13,9},{2,6},{6,2},{1... | collective-permute-start | bytes 147464 | tf_op jit(solution)/shard_map/ppermute | solution.py:32
  21.3 2.6 %collective-permute-start.4 = (bf16[64,384]{1,0:T(8,128)(2,1)S(1)}, bf16[64,384]{1,0:T(8,128)(2,1)S(1)}, u32[]{:S(2)}, u32[]{:S(2)}) collective-permute-start(bf16[64,384]{1,0:T(8,128)(2,1)S(1)} %get-tuple-element.12), channel_id=1, source_target_pairs={{0,8},{4,12},{8,0},{12,4},{1,9},{5,13},{9,1},{13,5},{2,10},{6,14},... | collective-permute-start | bytes 147464 | tf_op jit(solution)/shard_map/ppermute | solution.py:32
  25.3 1.5 %collective-permute-start.7 = (bf16[64,384]{1,0:T(8,128)(2,1)S(1)}, bf16[64,384]{1,0:T(8,128)(2,1)S(1)}, u32[]{:S(2)}, u32[]{:S(2)}) collective-permute-start(bf16[64,384]{1,0:T(8,128)(2,1)S(1)} %collective-permute-done.3.refs_1_), channel_id=1, source_target_pairs={{0,2},{2,0},{1,3},{3,1},{4,6},{6,4},{5,7},{7,5},{8,10},{10,8},{9,1... | collective-permute-start | bytes 147464 | tf_op jit(solution)/shard_map/ppermute | solution.py:32
  27.3 2.5 %collective-permute-done.5.refs_3_ = bf16[64,384]{1,0:T(8,128)(2,1)S(1)} collective-permute-done((bf16[64,384]{1,0:T(8,128)(2,1)S(1)}, bf16[64,384]{1,0:T(8,128)(2,1)S(1)}, u32[]{:S(2)}, u32[]{:S(2)}) %collective-permute-start.5) | collective-permute-done | bytes 49184 | tf_op jit(solution)/shard_map/ppermute | solution.py:32
  30.4 4.1 %collective-permute-done.6.refs_4_ = bf16[64,384]{1,0:T(8,128)(2,1)S(1)} collective-permute-done((bf16[64,384]{1,0:T(8,128)(2,1)S(1)}, bf16[64,384]{1,0:T(8,128)(2,1)S(1)}, u32[]{:S(2)}, u32[]{:S(2)}) %collective-permute-start.6) | collective-permute-done | bytes 49184 | tf_op jit(solution)/shard_map/ppermute | solution.py:32
  37.9 1.9 %collective-permute-start.11 = (bf16[64,1536]{1,0:T(8,128)(2,1)S(1)}, bf16[64,1536]{1,0:T(8,128)(2,1)S(1)}, u32[]{:S(2)}, u32[]{:S(2)}) collective-permute-start(bf16[64,1536]{1,0:T(8,128)(2,1)S(1)} %get-tuple-element.15), channel_id=1, source_target_pairs={{0,4},{4,0},{8,12},{12,8},{1,5},{5,1},{9,13},{13,9},{2,6},{6,2},{1... | collective-permute-start | bytes 589832 | tf_op jit(solution)/shard_map/ppermute | solution.py:32
  39.8 2.6 %collective-permute-start.12 = (bf16[64,1536]{1,0:T(8,128)(2,1)S(1)}, bf16[64,1536]{1,0:T(8,128)(2,1)S(1)}, u32[]{:S(2)}, u32[]{:S(2)}) collective-permute-start(bf16[64,1536]{1,0:T(8,128)(2,1)S(1)} %get-tuple-element.16), channel_id=1, source_target_pairs={{0,8},{4,12},{8,0},{12,4},{1,9},{5,13},{9,1},{13,5},{2,10},{6,14},... | collective-permute-start | bytes 589832 | tf_op jit(solution)/shard_map/ppermute | solution.py:32
  42.3 4.4 %collective-permute-done.11 = bf16[64,1536]{1,0:T(8,128)(2,1)S(1)} collective-permute-done((bf16[64,1536]{1,0:T(8,128)(2,1)S(1)}, bf16[64,1536]{1,0:T(8,128)(2,1)S(1)}, u32[]{:S(2)}, u32[]{:S(2)}) %collective-permute-start.11) | collective-permute-done | bytes 196640 | tf_op jit(solution)/shard_map/ppermute | solution.py:32
  46.7 10.0 %collective-permute-done.12 = bf16[64,1536]{1,0:T(8,128)(2,1)S(1)} collective-permute-done((bf16[64,1536]{1,0:T(8,128)(2,1)S(1)}, bf16[64,1536]{1,0:T(8,128)(2,1)S(1)}, u32[]{:S(2)}, u32[]{:S(2)}) %collective-permute-start.12) | collective-permute-done | bytes 196640 | tf_op jit(solution)/shard_map/ppermute | solution.py:32
  56.9 2.7 %collective-permute-start.14 = (bf16[64,1536]{1,0:T(8,128)(2,1)S(1)}, bf16[64,1536]{1,0:T(8,128)(2,1)S(1)}, u32[]{:S(2)}, u32[]{:S(2)}) collective-permute-start(bf16[64,1536]{1,0:T(8,128)(2,1)S(1)} %fusion.refs_0_), channel_id=1, source_target_pairs={{0,4},{4,0},{8,12},{12,8},{1,5},{5,1},{9,13},{13,9},{2,6},{6,2},{1... | collective-permute-start | bytes 589832 | tf_op jit(solution)/shard_map/ppermute | solution.py:32
  64.9 1.5 %collective-permute-start.18 = (bf16[64,1536]{1,0:T(8,128)(2,1)S(1)}, bf16[64,1536]{1,0:T(8,128)(2,1)S(1)}, u32[]{:S(2)}, u32[]{:S(2)}) collective-permute-start(bf16[64,1536]{1,0:T(8,128)(2,1)S(1)} %collective-permute-done.14.refs_1_), channel_id=1, source_target_pairs={{0,2},{2,0},{1,3},{3,1},{4,6},{6,4},{5,7},{7,5},{8,10},{10,8},{9,1... | collective-permute-start | bytes 589832 | tf_op jit(solution)/shard_map/ppermute | solution.py:32
  66.4 8.8 %collective-permute-done.15.refs_2_ = bf16[64,1536]{1,0:T(8,128)(2,1)S(1)} collective-permute-done((bf16[64,1536]{1,0:T(8,128)(2,1)S(1)}, bf16[64,1536]{1,0:T(8,128)(2,1)S(1)}, u32[]{:S(2)}, u32[]{:S(2)}) %collective-permute-start.15) | collective-permute-done | bytes 196640 | tf_op jit(solution)/shard_map/ppermute | solution.py:32
  75.2 1.5 %collective-permute-start.19 = (bf16[64,1536]{1,0:T(8,128)(2,1)S(1)}, bf16[64,1536]{1,0:T(8,128)(2,1)S(1)}, u32[]{:S(2)}, u32[]{:S(2)}) collective-permute-start(bf16[64,1536]{1,0:T(8,128)(2,1)S(1)} %collective-permute-done.15.refs_2_), channel_id=1, source_target_pairs={{0,2},{2,0},{1,3},{3,1},{4,6},{6,4},{5,7},{7,5},{8,10},{10,8},{9,1... | collective-permute-start | bytes 589832 | tf_op jit(solution)/shard_map/ppermute | solution.py:32
  77.3 2.1 %collective-permute-start.21 = (s32[8,64]{1,0:T(8,128)S(1)}, s32[8,64]{1,0:T(8,128)S(1)}, u32[]{:S(2)}, u32[]{:S(2)}) collective-permute-start(s32[8,64]{1,0:T(8,128)S(1)} %add_add_fusion.refs_8_), channel_id=1, source_target_pairs={{0,4},{4,0},{8,12},{12,8},{1,5},{5,1},{9,13},{13,9},{2,6},{6,2},{1... | collective-permute-start | bytes 6152 | tf_op jit(solution)/shard_map/ppermute | solution.py:32
  79.5 1.6 %collective-permute-done.21.refs_9_ = s32[8,64]{1,0:T(8,128)S(1)} collective-permute-done((s32[8,64]{1,0:T(8,128)S(1)}, s32[8,64]{1,0:T(8,128)S(1)}, u32[]{:S(2)}, u32[]{:S(2)}) %collective-permute-start.21) | collective-permute-done | bytes 2080 | tf_op jit(solution)/shard_map/ppermute | solution.py:32
  81.1 3.8 %collective-permute-start.22 = (s32[8,64]{1,0:T(8,128)S(1)}, s32[8,64]{1,0:T(8,128)S(1)}, u32[]{:S(2)}, u32[]{:S(2)}) collective-permute-start(s32[8,64]{1,0:T(8,128)S(1)} %add_add_fusion.refs_8_), channel_id=1, source_target_pairs={{0,8},{4,12},{8,0},{12,4},{1,9},{5,13},{9,1},{13,5},{2,10},{6,14},... | collective-permute-start | bytes 6152 | tf_op jit(solution)/shard_map/ppermute | solution.py:32
  84.9 1.6 %collective-permute-done.22.refs_10_ = s32[8,64]{1,0:T(8,128)S(1)} collective-permute-done((s32[8,64]{1,0:T(8,128)S(1)}, s32[8,64]{1,0:T(8,128)S(1)}, u32[]{:S(2)}, u32[]{:S(2)}) %collective-permute-start.22) | collective-permute-done | bytes 2080 | tf_op jit(solution)/shard_map/ppermute | solution.py:32
  86.4 2.4 %collective-permute-start.23 = (s32[8,64]{1,0:T(8,128)S(1)}, s32[8,64]{1,0:T(8,128)S(1)}, u32[]{:S(2)}, u32[]{:S(2)}) collective-permute-start(s32[8,64]{1,0:T(8,128)S(1)} %add_add_fusion.refs_8_), channel_id=1, source_target_pairs={{0,12},{4,8},{8,4},{12,0},{1,13},{5,9},{9,5},{13,1},{2,14},{6,10},... | collective-permute-start | bytes 6152 | tf_op jit(solution)/shard_map/ppermute | solution.py:32
  90.1 1.8 %collective-permute-done.23.refs_11_ = s32[8,64]{1,0:T(8,128)S(1)} collective-permute-done((s32[8,64]{1,0:T(8,128)S(1)}, s32[8,64]{1,0:T(8,128)S(1)}, u32[]{:S(2)}, u32[]{:S(2)}) %collective-permute-start.23) | collective-permute-done | bytes 2080 | tf_op jit(solution)/shard_map/ppermute | solution.py:32
  93.4 19.7 %experts.1 = bf16[2,160,2048]{2,1,0:T(8,128)(2,1)} custom-call(s32[2]{0:T(128)} %pad_add_fusion.1.info, bf16[64,1536]{1,0:T(8,128)(2,1)} %copy-done.3, bf16[64,1536]{1,0:T(8,128)(2,1)} %copy-done.4, bf16[64,1536]{1,0:T(8,128)(2,1)} %copy-done.5, bf16[64,1536]{1,0:T(8,128)(2,1)} %copy-done.6, bf16[64,1536]{1,0:T(8,128)(2,1)} %copy-done.7, ...), custom_call_target="tpu_custom_call" | custom-call | flops 8053063680 | bytes 50331648 | tf_op jit(solution)/shard_map/experts/pallas_call | solution.py:294
  (74 shorter events, 18.5 us)
Async XLA Ops:
  3.5 33.3 %collective-permute-start.10 = (bf16[384,1536]{1,0:T(8,128)(2,1)}, bf16[384,1536]{1,0:T(8,128)(2,1)S(1)}, u32[]{:S(2)}, u32[]{:S(2)}) collective-permute-start(bf16[384,1536]{1,0:T(8,128)(2,1)} %get-tuple-element.22), channel_id=1, source_target_pairs={{0,2},{2,0},{1,3},{3,1},{4,6},{6,4},{5,7},{7,5},{8,10},{10,8},{9,1... | collective-permute-start | bytes 3538952 | tf_op jit(solution)/shard_map/ppermute | solution.py:32
  6.5 10.0 %collective-permute-start = (bf16[64,512]{1,0:T(8,128)(2,1)S(1)}, bf16[64,512]{1,0:T(8,128)(2,1)S(1)}, u32[]{:S(2)}, u32[]{:S(2)}) collective-permute-start(bf16[64,512]{1,0:T(8,128)(2,1)S(1)} %pad_maximum_fusion), channel_id=1, source_target_pairs={{0,4},{8,12},{1,5},{9,13},{2,6},{10,14},{3,7},{11,15},{16,20},{24,... | collective-permute-start | bytes 196616 | tf_op jit(solution)/shard_map/ppermute | solution.py:32
  10.0 6.6 %collective-permute-start.1 = (bf16[64,512]{1,0:T(8,128)(2,1)S(1)}, bf16[64,512]{1,0:T(8,128)(2,1)S(1)}, u32[]{:S(2)}, u32[]{:S(2)}) collective-permute-start(bf16[64,512]{1,0:T(8,128)(2,1)S(1)} %pad_maximum_fusion), channel_id=1, source_target_pairs={{0,8},{4,12},{1,9},{5,13},{2,10},{6,14},{3,11},{7,15},{16,24},{20,... | collective-permute-start | bytes 196616 | tf_op jit(solution)/shard_map/ppermute | solution.py:32
  14.5 3.2 %collective-permute-start.2 = (bf16[64,512]{1,0:T(8,128)(2,1)S(1)}, bf16[64,512]{1,0:T(8,128)(2,1)S(1)}, u32[]{:S(2)}, u32[]{:S(2)}) collective-permute-start(bf16[64,512]{1,0:T(8,128)(2,1)S(1)} %pad_maximum_fusion), channel_id=1, source_target_pairs={{0,12},{4,8},{1,13},{5,9},{2,14},{6,10},{3,15},{7,11},{16,28},{20,... | collective-permute-start | bytes 196616 | tf_op jit(solution)/shard_map/ppermute | solution.py:32
  19.1 6.2 %collective-permute-start.3 = (bf16[64,384]{1,0:T(8,128)(2,1)S(1)}, bf16[64,384]{1,0:T(8,128)(2,1)S(1)}, u32[]{:S(2)}, u32[]{:S(2)}) collective-permute-start(bf16[64,384]{1,0:T(8,128)(2,1)S(1)} %get-tuple-element.11), channel_id=1, source_target_pairs={{0,4},{4,0},{8,12},{12,8},{1,5},{5,1},{9,13},{13,9},{2,6},{6,2},{1... | collective-permute-start | bytes 147464 | tf_op jit(solution)/shard_map/ppermute | solution.py:32
  21.3 5.4 %collective-permute-start.4 = (bf16[64,384]{1,0:T(8,128)(2,1)S(1)}, bf16[64,384]{1,0:T(8,128)(2,1)S(1)}, u32[]{:S(2)}, u32[]{:S(2)}) collective-permute-start(bf16[64,384]{1,0:T(8,128)(2,1)S(1)} %get-tuple-element.12), channel_id=1, source_target_pairs={{0,8},{4,12},{8,0},{12,4},{1,9},{5,13},{9,1},{13,5},{2,10},{6,14},... | collective-permute-start | bytes 147464 | tf_op jit(solution)/shard_map/ppermute | solution.py:32
  23.9 5.9 %collective-permute-start.5 = (bf16[64,384]{1,0:T(8,128)(2,1)S(1)}, bf16[64,384]{1,0:T(8,128)(2,1)S(1)}, u32[]{:S(2)}, u32[]{:S(2)}) collective-permute-start(bf16[64,384]{1,0:T(8,128)(2,1)S(1)} %get-tuple-element.13), channel_id=1, source_target_pairs={{0,12},{4,8},{8,4},{12,0},{1,13},{5,9},{9,5},{13,1},{2,14},{6,10},... | collective-permute-start | bytes 147464 | tf_op jit(solution)/shard_map/ppermute | solution.py:32
  24.7 9.8 %collective-permute-start.6 = (bf16[64,384]{1,0:T(8,128)(2,1)S(1)}, bf16[64,384]{1,0:T(8,128)(2,1)S(1)}, u32[]{:S(2)}, u32[]{:S(2)}) collective-permute-start(bf16[64,384]{1,0:T(8,128)(2,1)S(1)} %get-tuple-element.10.refs_0_), channel_id=1, source_target_pairs={{0,2},{2,0},{1,3},{3,1},{4,6},{6,4},{5,7},{7,5},{8,10},{10,8},{9,1... | collective-permute-start | bytes 147464 | tf_op jit(solution)/shard_map/ppermute | solution.py:32
  25.3 10.3 %collective-permute-start.7 = (bf16[64,384]{1,0:T(8,128)(2,1)S(1)}, bf16[64,384]{1,0:T(8,128)(2,1)S(1)}, u32[]{:S(2)}, u32[]{:S(2)}) collective-permute-start(bf16[64,384]{1,0:T(8,128)(2,1)S(1)} %collective-permute-done.3.refs_1_), channel_id=1, source_target_pairs={{0,2},{2,0},{1,3},{3,1},{4,6},{6,4},{5,7},{7,5},{8,10},{10,8},{9,1... | collective-permute-start | bytes 147464 | tf_op jit(solution)/shard_map/ppermute | solution.py:32
  26.8 9.6 %collective-permute-start.8 = (bf16[64,384]{1,0:T(8,128)(2,1)S(1)}, bf16[64,384]{1,0:T(8,128)(2,1)S(1)}, u32[]{:S(2)}, u32[]{:S(2)}) collective-permute-start(bf16[64,384]{1,0:T(8,128)(2,1)S(1)} %collective-permute-done.4.refs_2_), channel_id=1, source_target_pairs={{0,2},{2,0},{1,3},{3,1},{4,6},{6,4},{5,7},{7,5},{8,10},{10,8},{9,1... | collective-permute-start | bytes 147464 | tf_op jit(solution)/shard_map/ppermute | solution.py:32
  29.8 7.0 %collective-permute-start.9 = (bf16[64,384]{1,0:T(8,128)(2,1)S(1)}, bf16[64,384]{1,0:T(8,128)(2,1)S(1)}, u32[]{:S(2)}, u32[]{:S(2)}) collective-permute-start(bf16[64,384]{1,0:T(8,128)(2,1)S(1)} %collective-permute-done.5.refs_3_), channel_id=1, source_target_pairs={{0,2},{2,0},{1,3},{3,1},{4,6},{6,4},{5,7},{7,5},{8,10},{10,8},{9,1... | collective-permute-start | bytes 147464 | tf_op jit(solution)/shard_map/ppermute | solution.py:32
  37.9 8.8 %collective-permute-start.11 = (bf16[64,1536]{1,0:T(8,128)(2,1)S(1)}, bf16[64,1536]{1,0:T(8,128)(2,1)S(1)}, u32[]{:S(2)}, u32[]{:S(2)}) collective-permute-start(bf16[64,1536]{1,0:T(8,128)(2,1)S(1)} %get-tuple-element.15), channel_id=1, source_target_pairs={{0,4},{4,0},{8,12},{12,8},{1,5},{5,1},{9,13},{13,9},{2,6},{6,2},{1... | collective-permute-start | bytes 589832 | tf_op jit(solution)/shard_map/ppermute | solution.py:32
  39.8 17.0 %collective-permute-start.12 = (bf16[64,1536]{1,0:T(8,128)(2,1)S(1)}, bf16[64,1536]{1,0:T(8,128)(2,1)S(1)}, u32[]{:S(2)}, u32[]{:S(2)}) collective-permute-start(bf16[64,1536]{1,0:T(8,128)(2,1)S(1)} %get-tuple-element.16), channel_id=1, source_target_pairs={{0,8},{4,12},{8,0},{12,4},{1,9},{5,13},{9,1},{13,5},{2,10},{6,14},... | collective-permute-start | bytes 589832 | tf_op jit(solution)/shard_map/ppermute | solution.py:32
  42.3 14.4 %collective-permute-start.13 = (bf16[64,1536]{1,0:T(8,128)(2,1)S(1)}, bf16[64,1536]{1,0:T(8,128)(2,1)S(1)}, u32[]{:S(2)}, u32[]{:S(2)}) collective-permute-start(bf16[64,1536]{1,0:T(8,128)(2,1)S(1)} %get-tuple-element.17), channel_id=1, source_target_pairs={{0,12},{4,8},{8,4},{12,0},{1,13},{5,9},{9,5},{13,1},{2,14},{6,10},... | collective-permute-start | bytes 589832 | tf_op jit(solution)/shard_map/ppermute | solution.py:32
  56.9 8.1 %collective-permute-start.14 = (bf16[64,1536]{1,0:T(8,128)(2,1)S(1)}, bf16[64,1536]{1,0:T(8,128)(2,1)S(1)}, u32[]{:S(2)}, u32[]{:S(2)}) collective-permute-start(bf16[64,1536]{1,0:T(8,128)(2,1)S(1)} %fusion.refs_0_), channel_id=1, source_target_pairs={{0,4},{4,0},{8,12},{12,8},{1,5},{5,1},{9,13},{13,9},{2,6},{6,2},{1... | collective-permute-start | bytes 589832 | tf_op jit(solution)/shard_map/ppermute | solution.py:32
  59.6 15.6 %collective-permute-start.15 = (bf16[64,1536]{1,0:T(8,128)(2,1)S(1)}, bf16[64,1536]{1,0:T(8,128)(2,1)S(1)}, u32[]{:S(2)}, u32[]{:S(2)}) collective-permute-start(bf16[64,1536]{1,0:T(8,128)(2,1)S(1)} %fusion.refs_0_), channel_id=1, source_target_pairs={{0,8},{4,12},{8,0},{12,4},{1,9},{5,13},{9,1},{13,5},{2,10},{6,14},... | collective-permute-start | bytes 589832 | tf_op jit(solution)/shard_map/ppermute | solution.py:32
  60.7 16.0 %collective-permute-start.16 = (bf16[64,1536]{1,0:T(8,128)(2,1)S(1)}, bf16[64,1536]{1,0:T(8,128)(2,1)S(1)}, u32[]{:S(2)}, u32[]{:S(2)}) collective-permute-start(bf16[64,1536]{1,0:T(8,128)(2,1)S(1)} %fusion.refs_0_), channel_id=1, source_target_pairs={{0,12},{4,8},{8,4},{12,0},{1,13},{5,9},{9,5},{13,1},{2,14},{6,10},... | collective-permute-start | bytes 589832 | tf_op jit(solution)/shard_map/ppermute | solution.py:32
  62.1 29.7 %collective-permute-start.17 = (bf16[64,1536]{1,0:T(8,128)(2,1)S(1)}, bf16[64,1536]{1,0:T(8,128)(2,1)S(1)}, u32[]{:S(2)}, u32[]{:S(2)}) collective-permute-start(bf16[64,1536]{1,0:T(8,128)(2,1)S(1)} %fusion.refs_0_), channel_id=1, source_target_pairs={{0,2},{2,0},{1,3},{3,1},{4,6},{6,4},{5,7},{7,5},{8,10},{10,8},{9,1... | collective-permute-start | bytes 589832 | tf_op jit(solution)/shard_map/ppermute | solution.py:32
  64.9 26.9 %collective-permute-start.18 = (bf16[64,1536]{1,0:T(8,128)(2,1)S(1)}, bf16[64,1536]{1,0:T(8,128)(2,1)S(1)}, u32[]{:S(2)}, u32[]{:S(2)}) collective-permute-start(bf16[64,1536]{1,0:T(8,128)(2,1)S(1)} %collective-permute-done.14.refs_1_), channel_id=1, source_target_pairs={{0,2},{2,0},{1,3},{3,1},{4,6},{6,4},{5,7},{7,5},{8,10},{10,8},{9,1... | collective-permute-start | bytes 589832 | tf_op jit(solution)/shard_map/ppermute | solution.py:32
  75.2 16.7 %collective-permute-start.19 = (bf16[64,1536]{1,0:T(8,128)(2,1)S(1)}, bf16[64,1536]{1,0:T(8,128)(2,1)S(1)}, u32[]{:S(2)}, u32[]{:S(2)}) collective-permute-start(bf16[64,1536]{1,0:T(8,128)(2,1)S(1)} %collective-permute-done.15.refs_2_), channel_id=1, source_target_pairs={{0,2},{2,0},{1,3},{3,1},{4,6},{6,4},{5,7},{7,5},{8,10},{10,8},{9,1... | collective-permute-start | bytes 589832 | tf_op jit(solution)/shard_map/ppermute | solution.py:32
  76.7 15.2 %collective-permute-start.20 = (bf16[64,1536]{1,0:T(8,128)(2,1)S(1)}, bf16[64,1536]{1,0:T(8,128)(2,1)S(1)}, u32[]{:S(2)}, u32[]{:S(2)}) collective-permute-start(bf16[64,1536]{1,0:T(8,128)(2,1)S(1)} %collective-permute-done.16.refs_3_), channel_id=1, source_target_pairs={{0,2},{2,0},{1,3},{3,1},{4,6},{6,4},{5,7},{7,5},{8,10},{10,8},{9,1... | collective-permute-start | bytes 589832 | tf_op jit(solution)/shard_map/ppermute | solution.py:32
  77.3 3.7 %collective-permute-start.21 = (s32[8,64]{1,0:T(8,128)S(1)}, s32[8,64]{1,0:T(8,128)S(1)}, u32[]{:S(2)}, u32[]{:S(2)}) collective-permute-start(s32[8,64]{1,0:T(8,128)S(1)} %add_add_fusion.refs_8_), channel_id=1, source_target_pairs={{0,4},{4,0},{8,12},{12,8},{1,5},{5,1},{9,13},{13,9},{2,6},{6,2},{1... | collective-permute-start | bytes 6152 | tf_op jit(solution)/shard_map/ppermute | solution.py:32
  81.1 5.4 %collective-permute-start.22 = (s32[8,64]{1,0:T(8,128)S(1)}, s32[8,64]{1,0:T(8,128)S(1)}, u32[]{:S(2)}, u32[]{:S(2)}) collective-permute-start(s32[8,64]{1,0:T(8,128)S(1)} %add_add_fusion.refs_8_), channel_id=1, source_target_pairs={{0,8},{4,12},{8,0},{12,4},{1,9},{5,13},{9,1},{13,5},{2,10},{6,14},... | collective-permute-start | bytes 6152 | tf_op jit(solution)/shard_map/ppermute | solution.py:32
  86.4 5.4 %collective-permute-start.23 = (s32[8,64]{1,0:T(8,128)S(1)}, s32[8,64]{1,0:T(8,128)S(1)}, u32[]{:S(2)}, u32[]{:S(2)}) collective-permute-start(s32[8,64]{1,0:T(8,128)S(1)} %add_add_fusion.refs_8_), channel_id=1, source_target_pairs={{0,12},{4,8},{8,4},{12,0},{1,13},{5,9},{9,5},{13,1},{2,14},{6,10},... | collective-permute-start | bytes 6152 | tf_op jit(solution)/shard_map/ppermute | solution.py:32
  (19 other events, 307.5 us)

commit v2 on v1

v2 whole, which is shorter than its diff:
```python
import functools
import math

import jax
import jax.numpy as jnp
from jax import lax
from jax.experimental import pallas as pl
from jax.experimental.pallas import tpu as pltpu
from jax.sharding import PartitionSpec as P

HEAD_SIZE = 128
QUERY_HEAD_COUNT = 24
KEY_VALUE_HEADS = 4
MOST = 40
EXTRA = 16
EPS = 1e-05
NEG = -1e30
F32 = jnp.float32
BF16 = jnp.bfloat16

VMEM = pl.BlockSpec(memory_space=pltpu.VMEM)
SMEM = pl.BlockSpec(memory_space=pltpu.SMEM)
ANY = pl.BlockSpec(memory_space=pl.ANY)
place = pltpu.with_memory_space_constraint
HBM = pl.BlockSpec(memory_space=pltpu.HBM)


def pairwise(count):
    return count in (1, 2, 4)


def swap(array, axis, step, upward=False):
    count = lax.axis_size(axis)
    pairs = [(i, i ^ step) for i in range(count) if not upward or i < i ^ step]
    return lax.ppermute(array, axis, pairs)


def steps_of(count):
    return [k for k in (2, 3, 1) if k < count]


def shuffled(pieces):
    return [pieces[k] for k in (0, 2, 3, 1)] if len(pieces) == 4 else list(pieces)


def sorted_back(pieces):
    return [pieces[k] for k in (0, 3, 1, 2)] if len(pieces) == 4 else list(pieces)


def swaps(arrays, axis, upward=False):
    got = {k: swap(arrays[k], axis, k, upward) for k in steps_of(len(arrays))}
    return [arrays[0]] + [got[k] for k in range(1, len(arrays))]


def spread(array, axis, upward=False):
    count = lax.axis_size(axis)
    if pairwise(count):
        return swaps([array] * count, axis, upward)
    return [lax.all_gather(array, axis, axis=0, tiled=True)]


def attention_kernel(shape, info, queries, gain_in, routes, numer, *refs):
    tokens, groups, per_group, pieces, carried, split = shape
    kv_refs, refs = refs[:pieces], refs[pieces:]
    carried_in, refs = refs[:carried], refs[carried:]
    gain_out, carried_out, refs = refs[0], refs[1 : 1 + carried], refs[1 + carried :]
    outs, sems = refs[:-1], refs[-1]
    copies = [
        pltpu.make_async_copy(source, out, sems.at[i])
        for i, (source, out) in enumerate(zip(carried_in, carried_out))
    ]
    for copy in copies:
        copy.start()
    gain_out[...] = gain_in[...]
    rank, flip, valid_len = info[0], info[1], info[2]
    width = groups * HEAD_SIZE
    key_parts = [ref[:, :width] for ref in kv_refs]
    value_parts = [ref[:, width:] for ref in kv_refs]
    all_keys = jnp.concatenate(key_parts, axis=0)
    all_values = jnp.concatenate(value_parts, axis=0)
    length = all_keys.shape[0]
    column = lax.broadcasted_iota(jnp.int32, (tokens, length), 1)
    block = lax.div(column, tokens)
    key_pos = lax.bitwise_xor(block, flip) * tokens + (column - block * tokens)
    query_pos = rank * tokens + lax.broadcasted_iota(jnp.int32, (tokens, length), 0)
    allowed = ((key_pos <= query_pos) & (key_pos < valid_len)).astype(F32)
    allowed = jnp.concatenate([allowed] * per_group, axis=0) > 0
    scale = 1.0 / math.sqrt(HEAD_SIZE)
    attended = []
    for g in range(groups):
        heads = [g * per_group + a for a in range(per_group)]
        rows = jnp.concatenate(
            [queries[:, h * HEAD_SIZE : (h + 1) * HEAD_SIZE] for h in heads], axis=0
        )
        lanes = slice(g * HEAD_SIZE, (g + 1) * HEAD_SIZE)
        scores = (
            lax.dot_general(
                rows, all_keys[:, lanes], (((1,), (1,)), ((), ())), preferred_element_type=F32
            )
            * scale
        )
        scores = jnp.where(allowed, scores, NEG)
        top = jnp.max(scores, axis=-1, keepdims=True)
        weights = jnp.where(allowed, jnp.exp(scores - top), 0.0)
        denom = jnp.sum(weights, axis=-1, keepdims=True)
        mixed = jnp.dot(weights.astype(BF16), all_values[:, lanes], preferred_element_type=F32)
        mixed = mixed / denom
        attended += [mixed[a * tokens : (a + 1) * tokens] for a in range(per_group)]
    if not split:
        outs[0][...] = jnp.concatenate(attended, axis=1).astype(BF16)
        for copy in copies:
            copy.wait()
        return
    count = len(outs)
    part = HEAD_SIZE // count
    shares = [
        jnp.concatenate([o[:, j * part : (j + 1) * part] for o in attended], axis=1).astype(BF16)
        for j in range(count)
    ]
    routing = jnp.concatenate(
        [routes[...], numer[...], jnp.zeros((EXTRA - 3, tokens), jnp.int32)], axis=0
    )
    routing = routing.astype(F32).astype(BF16)
    for k in range(count):
        chosen = shares[k]
        for s in range(1, count):
            chosen = jnp.where(rank == s, shares[s ^ k], chosen)
        outs[k][:tokens, :] = chosen
        outs[k][tokens:, :] = jnp.zeros((EXTRA, chosen.shape[1]), BF16)
        outs[k][tokens:, :tokens] = routing
    for copy in copies:
        copy.wait()


def attend(info, queries, gain, routes, numer, kv_parts, carried, count):
    tokens = queries.shape[0]
    groups = kv_parts[0].shape[1] // (2 * HEAD_SIZE)
    per_group = QUERY_HEAD_COUNT // KEY_VALUE_HEADS
    split = pairwise(count)
    if split:
        out_shape = [
            jax.ShapeDtypeStruct((tokens + EXTRA, queries.shape[1] // count), BF16)
            for _ in range(count)
        ]
    else:
        out_shape = [jax.ShapeDtypeStruct(queries.shape, BF16)]
    length = tokens * count
    limit = min(40 << 20, (4 << 20) + 48 * per_group * tokens * length)
    out_shape = [
        jax.ShapeDtypeStruct(array.shape, BF16) for array in (gain, *carried)
    ] + out_shape
    return pl.pallas_call(
        functools.partial(
            attention_kernel, (tokens, groups, per_group, len(kv_parts), len(carried), split)
        ),
        out_shape=out_shape,
        in_specs=[SMEM] + [VMEM] * (4 + len(kv_parts)) + [ANY] * len(carried),
        out_specs=[VMEM] * len(out_shape),
        scratch_shapes=[pltpu.SemaphoreType.DMA((max(1, len(carried)),))],
        compiler_params=pltpu.CompilerParams(vmem_limit_bytes=limit),
        cost_estimate=pl.CostEstimate(
            flops=4 * tokens * length * queries.shape[1],
            bytes_accessed=4 * queries.size + 4 * length * kv_parts[0].shape[1],
            transcendentals=tokens * length * groups * per_group,
        ),
        name="attention",
    )(info, queries, gain, routes, numer, *kv_parts, *carried)


def prepare_kernel(parts, info, matrix, queries, keys, values, routes, numer, *refs):
    kv, rows, first_routes, weights = refs[:4]
    columns, sems = refs[4:-1], refs[-1]
    height, share = columns[-1].shape
    width = keys.shape[1]
    pairs = [
        (keys, kv.at[:, :width]),
        (values, kv.at[:, width:]),
        (queries, rows),
        (routes, first_routes),
        (numer, weights),
    ]
    for m, out in enumerate(columns):
        at = pl.multiple_of(lax.bitwise_xor(info[3], m) * share, share)
        lanes = pl.ds(at, share)
        if out.shape[0] == matrix.shape[0]:
            source = matrix.at[:, lanes]
        else:
            source = matrix.at[pl.ds(pl.multiple_of(info[4] * height, height), height), lanes]
        pairs.insert(2 if m else 5, (source, out))
    copies = [pltpu.make_async_copy(*pair, sems.at[i]) for i, pair in enumerate(pairs)]
    for copy in copies:
        copy.start()
    for copy in copies:
        copy.wait()


def prepare(info, matrix, queries, keys, values, routes, numer, head_count, halves):
    rows, features = matrix.shape
    tokens = queries.shape[0]
    share = features // head_count
    out_shape = [
        jax.ShapeDtypeStruct((tokens, 2 * keys.shape[1]), BF16),
        jax.ShapeDtypeStruct(queries.shape, BF16),
        jax.ShapeDtypeStruct(routes.shape, jnp.int32),
        jax.ShapeDtypeStruct(numer.shape, jnp.int32),
        jax.ShapeDtypeStruct((rows, share), BF16),
    ] + [pltpu.VMEM((rows // halves, share), BF16)] * (head_count - 1)
    sources = [matrix, queries, keys, values, routes, numer]
    return pl.pallas_call(
        functools.partial(prepare_kernel, head_count),
        out_shape=out_shape,
        in_specs=[SMEM] + [HBM] * len(sources),
        out_specs=[VMEM] * len(out_shape),
        scratch_shapes=[pltpu.SemaphoreType.DMA((5 + head_count,))],
        compiler_params=pltpu.CompilerParams(vmem_limit_bytes=8 << 20),
        cost_estimate=pl.CostEstimate(
            flops=0, bytes_accessed=4 * rows * features, transcendentals=0
        ),
        name="prepare",
    )(info, *[place(source, pltpu.HBM) for source in sources])


def project_kernel(parts, pieces, tokens, halves, info, *refs):
    rows = [sorted_back(refs[m * pieces : (m + 1) * pieces]) for m in range(parts)]
    refs = refs[parts * pieces :]
    weights = [refs[0][...]]
    refs = refs[1:]
    for m in range(1, parts):
        if halves == 1:
            weights.append(refs[0][...])
        else:
            mine, other = refs[0][...], refs[1][...]
            first = info[4] == 0
            weights += [jnp.where(first, mine, other), jnp.where(first, other, mine)]
        refs = refs[halves:]
    weights = jnp.concatenate(weights, axis=0)
    outs = refs
    if tokens:
        route, outs = outs[0], outs[1:]
        route[...] = jnp.concatenate([ref[tokens : tokens + 8, :tokens] for ref in rows[0]], axis=1)
    total = None
    depth = rows[0][0].shape[1]
    for m in range(parts):
        stacked = jnp.concatenate([ref[: tokens or ref.shape[0]] for ref in rows[m]], axis=0)
        product = jnp.dot(
            stacked, weights[m * depth : (m + 1) * depth], preferred_element_type=F32
        )
        total = product if total is None else total + product
    at = 0
    for i, out in enumerate(outs):
        out[...] = total[at : at + out.shape[0]].astype(out.dtype)
        at += out.shape[0]


def project(info, rows, weights, each):
    parts, pieces = len(rows), len(rows[0])
    depth, width = weights[0][0].shape
    flat_weights = [w for part in weights for w in part]
    heights = [each or p.shape[0] for p in rows[0]]
    tokens = sum(heights)
    out_shape = [
        jax.ShapeDtypeStruct((h, width), BF16 if each and i else F32)
        for i, h in enumerate(heights)
    ]
    if each:
        out_shape = [jax.ShapeDtypeStruct((8, tokens), BF16)] + out_shape
    flat = [p for part in rows for p in shuffled(part)]
    return pl.pallas_call(
        functools.partial(project_kernel, parts, pieces, each, len(weights[-1])),
        out_shape=out_shape,
        in_specs=[SMEM] + [VMEM] * (len(flat) + len(flat_weights)),
        out_specs=[VMEM] * len(out_shape),
        compiler_params=pltpu.CompilerParams(vmem_limit_bytes=min(40 << 20, (4 << 20) + 16 * tokens * width)),
        cost_estimate=pl.CostEstimate(
            flops=2 * tokens * width * parts * depth,
            bytes_accessed=2 * parts * depth * width + 4 * tokens * width,
            transcendentals=0,
        ),
        name="projection",
    )(info, *flat, *flat_weights)


def fetch_kernel(chunk, gate_hbm, up_hbm, after, *refs):
    outs, done, sems = refs[:-2], refs[-2], refs[-1]
    per_expert = gate_hbm.shape[2] // chunk
    copies = []
    for step, out in enumerate(outs):
        at = pl.ds((step % per_expert) * chunk, chunk)
        for i, source in enumerate((gate_hbm, up_hbm)):
            copies.append(
                pltpu.make_async_copy(
                    source.at[step // per_expert, :, at], out.at[i], sems.at[step, i]
                )
            )
    for copy in copies:
        copy.start()
    done[...] = jnp.zeros_like(done)
    for copy in copies:
        copy.wait()


def fetch(expert_gate, expert_up, after, chunk, early):
    features = expert_gate.shape[1]
    return pl.pallas_call(
        functools.partial(fetch_kernel, chunk),
        out_shape=[pltpu.VMEM((2, features, chunk), BF16)] * early
        + [
            jax.ShapeDtypeStruct((8, 128), F32),
        ],
        in_specs=[HBM, HBM, ANY],
        out_specs=[VMEM] * (early + 1),
        scratch_shapes=[pltpu.SemaphoreType.DMA((early, 2))],
        compiler_params=pltpu.CompilerParams(vmem_limit_bytes=1 << 20),
        cost_estimate=pl.CostEstimate(
            flops=0, bytes_accessed=8 * early * features * chunk, transcendentals=0
        ),
        name="fetch",
    )(place(expert_gate, pltpu.HBM), place(expert_up, pltpu.HBM), after)


def add_kernel(residual, own, *refs):
    total = residual[...].astype(F32) + own[...]
    for ref in refs[:-3]:
        total = total + ref[...].astype(F32)
    refs[-2][...] = total.astype(BF16)
    refs[-1][...] = total.astype(BF16)


def add(residual, own, received, after):
    return pl.pallas_call(
        add_kernel,
        out_shape=[jax.ShapeDtypeStruct(residual.shape, BF16)] * 2,
        in_specs=[VMEM] * (2 + len(received)) + [ANY],
        out_specs=[VMEM] * 2,
        compiler_params=pltpu.CompilerParams(vmem_limit_bytes=8 << 20),
        name="add",
    )(residual, own, *received, after)


def expert_kernel(shape, info, *refs):
    tokens, group, parts, pieces, experts, slots, chunk, depth, early = shape
    columns = [sorted_back(refs[m * pieces : (m + 1) * pieces]) for m in range(parts)]
    refs = refs[parts * pieces :]
    routing, gain, refs = refs[0], refs[1], refs[2:]
    fetched, refs = refs[:early], refs[early:]
    gate_hbm, up_hbm, hidden, chosen, factors, buffers, sems = refs
    flip, head = info[1], info[3]
    features = gate_hbm.shape[1]
    width = features // parts
    per_expert = gate_hbm.shape[2] // chunk
    steps = experts * per_expert

    def copies(step, slot):
        e = step // per_expert
        at = pl.ds(pl.multiple_of((step % per_expert) * chunk, chunk), chunk)
        return (
            pltpu.make_async_copy(gate_hbm.at[e, :, at], buffers.at[slot, 0], sems.at[slot, 0]),
            pltpu.make_async_copy(up_hbm.at[e, :, at], buffers.at[slot, 1], sems.at[slot, 1]),
        )

    for slot in range(depth):
        for copy in copies(early + slot, slot):
            copy.start()

    blocks = routing.shape[1] // tokens
    size = group * tokens
    slot_row = lax.broadcasted_iota(jnp.int32, (group * slots, size), 0)
    token_col = lax.broadcasted_iota(jnp.int32, (group * slots, size), 1)
    row_block = lax.div(slot_row, slots)
    row_rank = slot_row - row_block * slots
    col_block = lax.bitwise_xor(lax.div(token_col, tokens), flip)
    same_block = row_block == col_block
    before_row = lax.broadcasted_iota(jnp.int32, (size, size), 0)
    before_col = lax.broadcasted_iota(jnp.int32, (size, size), 1)
    before = (
        (before_row < before_col)
        & (lax.div(before_row, tokens) == lax.div(before_col, tokens))
    ).astype(BF16)
    ranks = lax.broadcasted_iota(jnp.int32, (8, size), 0)
    for g in range(blocks // group):
        route = routing[:, g * size : (g + 1) * size].astype(F32)
        first, second, numer = route[0:1], route[1:2], route[2:3]
        weight = numer / 256.0
        gate_rows = []
        for e in range(experts):
            expert = (head * experts + e).astype(F32)
            gate_rows.append(
                jnp.where(first == expert, weight, 0.0)
                + jnp.where(second == expert, 1.0 - weight, 0.0)
            )
        marked = jnp.zeros((8, size), F32)
        for e in range(experts):
            marked = jnp.where(ranks == e, (gate_rows[e] > 0).astype(F32), marked)
        counted = jnp.dot(marked.astype(BF16), before, preferred_element_type=F32)
        at = slice(g * group * slots, (g + 1) * group * slots)
        pick = []
        for e in range(experts):
            hit = (
                same_block
                & (counted[e : e + 1].astype(jnp.int32) == row_rank)
                & (gate_rows[e] > 0)
            )
            pick.append(hit.astype(BF16))
            factors[e, at, :] = jnp.sum(jnp.where(hit, gate_rows[e], 0.0), axis=1, keepdims=True)
        picks = jnp.concatenate(pick, axis=0)

        def stream_part(m):
            if pieces > 1:
                return jnp.concatenate([ref[...] for ref in columns[m]], axis=0).astype(F32)
            return columns[m][0][g * size : (g + 1) * size].astype(F32)

        squares = None
        for m in range(parts):
            raw = stream_part(m)
            part = jnp.sum(raw * raw, axis=1, keepdims=True)
            squares = part if squares is None else squares + part
        scale = lax.rsqrt(squares / features + EPS)
        for m in range(parts):
            part_at = lax.bitwise_xor(head, m)
            normed = (stream_part(m) * scale * gain[part_at].astype(F32)).astype(BF16)
            rows = jnp.dot(picks, normed, preferred_element_type=F32).astype(BF16)
            for e in range(experts):
                chosen[part_at, e, at, :] = rows[e * group * slots : (e + 1) * group * slots]

    def compute(step, weights):
        e = step // per_expert
        gate_part = up_part = None
        for p in range(parts):
            at = slice(p * width, (p + 1) * width)
            rows = chosen[p, e]
            a = jnp.dot(rows, weights[0, at, :], preferred_element_type=F32)
            b = jnp.dot(rows, weights[1, at, :], preferred_element_type=F32)
            gate_part = a if gate_part is None else gate_part + a
            up_part = b if up_part is None else up_part + b
        result = factors[e] * (gate_part / (1.0 + jnp.exp(-gate_part)) * up_part)
        at = pl.ds(pl.multiple_of((step % per_expert) * chunk, chunk), chunk)
        hidden[e, :, at] = result.astype(BF16)

    for step in range(early):
        compute(step, fetched[step])

    if depth:

        @pl.loop(early, steps)
        def _(step):
            slot = lax.rem(step - early, depth)
            for copy in copies(step, slot):
                copy.wait()
            compute(step, buffers.at[slot])

            @pl.when(step + depth < steps)
            def _():
                for copy in copies(step + depth, slot):
                    copy.start()


def run_experts(info, columns, routing, gain, fetched, expert_gate, expert_up, tokens, count):
    parts, pieces = len(columns), len(columns[0])
    experts, features, hidden_units = expert_gate.shape
    early, chunk = len(fetched), fetched[0].shape[2]
    late = experts * (hidden_units // chunk) - early
    depth = min(1, late)
    slots = MOST * count
    shape = (tokens, min(4, count), parts, pieces, experts, MOST, chunk, depth, early)
    flat = [p for part in columns for p in shuffled(part)]
    limit = (12 << 20) if late else (40 << 20)
    return pl.pallas_call(
        functools.partial(expert_kernel, shape),
        out_shape=jax.ShapeDtypeStruct((experts, slots, hidden_units), BF16),
        in_specs=[SMEM] + [VMEM] * (len(flat) + 2 + early) + [HBM, HBM],
        out_specs=VMEM,
        scratch_shapes=[
            pltpu.VMEM((parts, experts, slots, features // parts), BF16),
            pltpu.VMEM((experts, slots, 1), F32),
            pltpu.VMEM((max(depth, 1), 2, features, chunk), BF16),
            pltpu.SemaphoreType.DMA((max(depth, 1), 2)),
        ],
        compiler_params=pltpu.CompilerParams(vmem_limit_bytes=limit),
        cost_estimate=pl.CostEstimate(
            flops=4 * experts * slots * features * hidden_units,
            bytes_accessed=2 * expert_gate.size,
            transcendentals=experts * slots * hidden_units,
        ),
        name="experts",
    )(
        info,
        *flat,
        routing,
        gain,
        *[place(part, pltpu.VMEM) for part in fetched],
        place(expert_gate, pltpu.HBM),
        place(expert_up, pltpu.HBM),
    )


def local(
    queries,
    keys,
    values,
    residual_in,
    out_proj,
    norm_gain,
    expert_gate,
    expert_up,
    routes,
    gate_numer,
    sequence_lengths,
):
    tokens = queries.shape[1]
    count = lax.axis_size("seq")
    head_count = lax.axis_size("head")
    seq_rank = lax.axis_index("seq")
    head_rank = lax.axis_index("head")
    split = pairwise(count)
    flip = seq_rank if split else jnp.zeros_like(seq_rank)
    share = residual_in.shape[2]
    features = out_proj.shape[2]
    heads, part, _ = out_proj.shape

    info = jnp.stack([seq_rank, flip, sequence_lengths[0], head_rank, lax.axis_index("dat")])
    info = info.astype(jnp.int32)
    matrix = out_proj.reshape(heads * part, features)
    halves = 2 if lax.axis_size("dat") == 2 and matrix.shape[0] % 32 == 0 else 1
    own_kv, rows, own_routes, numer, own_weights, *weights = prepare(
        info, matrix, queries[0], keys[0], values[0], routes[0].T, gate_numer, head_count, halves
    )

    weights = [swap(weights[m - 1], "head", m) for m in range(1, head_count)]

    kv_parts = spread(own_kv, "seq", upward=True)
    gain = norm_gain.reshape(head_count, 1, share)

    gain, *attended = attend(
        info, rows, gain, own_routes, numer, kv_parts, weights if halves == 2 else [], count
    )
    if halves == 2:
        carried, attended = attended[: head_count - 1], attended[head_count - 1 :]
        weights = [[got, swap(again, "dat", 1)] for got, again in zip(weights, carried)]
    else:
        weights = [[got] for got in weights]
    weights = [[own_weights]] + weights
    if split:
        attended = swaps(attended, "seq")
    else:
        shares = attended[0].reshape(tokens, heads, count, part).transpose(2, 0, 1, 3)
        shares = shares.reshape(count * tokens, heads * part)
        attended = [lax.all_to_all(shares, "seq", 0, 0, tiled=True)]
        routing = jnp.concatenate(
            [own_routes, numer, jnp.zeros((5, tokens), jnp.int32)], axis=0
        )
        routing = lax.all_gather(routing, "seq", axis=1, tiled=True)
    rows = [attended] + [
        [swap(piece, "head", m) for piece in attended] for m in range(1, head_count)
    ]
    sums = project(info, rows, weights, tokens if split else 0)
    if split:
        routing, *sums = sums
    chunk = min(512, expert_gate.shape[2])
    early = max(1, expert_gate.shape[0] * (expert_gate.shape[2] // chunk) * 12 // 16)
    *fetched, done = fetch(expert_gate, expert_up, sums[-1], chunk, early)
    if split:
        received = swaps(sums, "seq")[1:]
        stream, shared = add(residual_in[0], sums[0], received, done)
    else:
        mixed = lax.psum_scatter(sums[0], "seq", scatter_dimension=0, tiled=True)
        stream, shared = add(residual_in[0], mixed, [], done)

    own_columns = spread(shared, "seq")
    columns = [own_columns] + [
        [swap(piece, "head", m) for piece in own_columns] for m in range(1, head_count)
    ]
    hidden = run_experts(
        info, columns, routing, gain, fetched, expert_gate, expert_up, tokens, count
    )
    return (stream[None], hidden[:, None])


def solution(mesh):
    in_specs = (
        P(("grp", "dat"), "seq", "head"),
        P(("grp", "dat"), "seq", "head"),
        P(("grp", "dat"), "seq", "head"),
        P(("grp", "dat"), "seq", "head"),
        P("head", "seq", None),
        P(),
        P("head", None, "seq"),
        P("head", None, "seq"),
        P(("grp", "dat"), "seq", None),
        P(("grp", "dat"), "seq"),
        P(("grp", "dat")),
    )
    out_specs = (P(("grp", "dat"), "seq", "head"), P("head", ("grp", "dat"), None, "seq"))
    return jax.shard_map(local, mesh=mesh, in_specs=in_specs, out_specs=out_specs, check_vma=False)
```

time: 113 us -> 99 us (0.88)
  waiting for transfers between devices: 39.6 us -> 26.7 us
  Pallas kernels: 22.1 us -> 33.1 us
  starting transfers between devices: 43.9 us -> 36.8 us
  local copies, waits for them, and re-layouts: 4.98 us -> 0.79 us
    pallas_call x1 -> x4, Pallas kernels: 0.97 us -> 16.6 us  [the longest x1 12.1 us: fetch(): pl.pallas_call(functools.partial(fetch_kernel, chunk), out_shape=[pltpu.V...]
    ppermute x24 -> x22, waiting for transfers between devices: 39.6 us -> 26.7 us  [swap(): return lax.ppermute(array, axis, pairs)]
    ppermute x24 -> x22, starting transfers between devices: 43.9 us -> 36.8 us  [swap(): return lax.ppermute(array, axis, pairs)]
    pallas_call x1, Pallas kernels: 19.7 us -> 14.9 us  [run_experts(): pl.pallas_call(functools.partial(expert_kernel, shape), out_shape=jax.Sha...]
    dynamic_slice x1 -> x0, local copies, waits for them, and re-layouts: 2.84 us -> none  [columns_of(): return lax.dynamic_slice_in_dim(matrix, rank * share, share, 1)]
    unnamed x38 -> x2, local copies, waits for them, and re-layouts: 1.46 us -> 0.01 us
  transfers between devices with their start and end apart: 24 -> 22, of which waited for: 14 -> 12; matrix products, arithmetic and copies ran while one was open for 1% -> 1% of each run, Pallas kernels for 1% -> 12%
where the time goes in v2:
time: 99 us; the launch traced here: 98.8 us
  starting transfers between devices  36.8 us (37%)
  Pallas kernels  33.1 us (33%)
  waiting for transfers between devices  26.7 us (27%)
  between operations  1.38 us (1%)
    ppermute x22, starting transfers between devices, swap(): return lax.ppermute(array, axis, pairs)  36.8 us
    ppermute x22, waiting for transfers between devices, swap(): return lax.ppermute(array, axis, pairs)  26.7 us
    pallas_call x1, Pallas kernels, run_experts(): pl.pallas_call(functools.partial(expert_kernel, shape), out_shape=jax.Sha...  14.9 us
    pallas_call x1, Pallas kernels, fetch(): pl.pallas_call(functools.partial(fetch_kernel, chunk), out_shape=[pltpu.V...  12.1 us
    pallas_call x1, Pallas kernels, prepare(): pl.pallas_call(functools.partial(prepare_kernel, head_count), out_shape=o...  2.18 us
  transfers between devices with their start and end apart: 22, of which 12 were waited for; matrix products, arithmetic and copies ran while one was open for 1% of the time, Pallas kernels for 12%

profile of v2, /device:TPU:0, one launch (start us, length us, event | category | flops | bytes accessed | tf_op | source)
XLA Modules:
  0.0 98.8 jit_solution(9524449058866233688)
XLA Ops:
  1.4 2.2 %prepare.1 = (bf16[64,512]{1,0:T(8,128)(2,1)S(1)}, bf16[64,1536]{1,0:T(8,128)(2,1)S(1)}, s32[2,64]{1,0:T(2,128)S(1)}, s32[1,64]{1,0:T(1,128)S(1)}, bf16[384,1536...) custom-call(s32[5]{0:T(128)S(1)} %stack.16.info, bf16[384,3072]{1,0:T(8,128)(2,1)} %bitcast.16, ...), custom_call_target="tpu_custom_call" | custom-call | bytes 4718592 | tf_op jit(solution)/shard_map/prepare/pallas_call | solution.py:209
  3.6 3.0 %collective-permute-start.3 = (bf16[192,1536]{1,0:T(8,128)(2,1)S(1)}, bf16[192,1536]{1,0:T(8,128)(2,1)S(1)}, u32[]{:S(2)}, u32[]{:S(2)}) collective-permute-start(bf16[192,1536]{1,0:T(8,128)(2,1)S(1)} %get-tuple-element.32), channel_id=1, source_target_pairs={{0,2},{2,0},{1,3},{3,1},{4,6},{6,4},{5,7},{7,5},{8,10},{10,8},{9,1... | collective-permute-start | bytes 1769480 | tf_op jit(solution)/shard_map/ppermute | solution.py:35
  6.6 5.5 %collective-permute-start.2 = (bf16[64,512]{1,0:T(8,128)(2,1)S(1)}, bf16[64,512]{1,0:T(8,128)(2,1)S(1)}, u32[]{:S(2)}, u32[]{:S(2)}) collective-permute-start(bf16[64,512]{1,0:T(8,128)(2,1)S(1)} %get-tuple-element.31.refs_0_), channel_id=1, source_target_pairs={{0,12},{4,8},{1,13},{5,9},{2,14},{6,10},{3,15},{7,11},{16,28},{20,... | collective-permute-start | bytes 196616 | tf_op jit(solution)/shard_map/ppermute | solution.py:35
  13.4 2.5 %collective-permute-start = (bf16[64,512]{1,0:T(8,128)(2,1)S(1)}, bf16[64,512]{1,0:T(8,128)(2,1)S(1)}, u32[]{:S(2)}, u32[]{:S(2)}) collective-permute-start(bf16[64,512]{1,0:T(8,128)(2,1)S(1)} %get-tuple-element.31.refs_0_), channel_id=1, source_target_pairs={{0,4},{8,12},{1,5},{9,13},{2,6},{10,14},{3,7},{11,15},{16,20},{24,... | collective-permute-start | bytes 196616 | tf_op jit(solution)/shard_map/ppermute | solution.py:35
  17.7 2.2 %collective-permute-done.3.refs_4_.refs_9_ = bf16[192,1536]{1,0:T(8,128)(2,1)S(1)} collective-permute-done((bf16[192,1536]{1,0:T(8,128)(2,1)S(1)}, bf16[192,1536]{1,0:T(8,128)(2,1)S(1)}, u32[]{:S(2)}, u32[]{:S(2)}) %collective-permute-start.3) | collective-permute-done | bytes 589856 | tf_op jit(solution)/shard_map/ppermute | solution.py:35
  19.9 1.6 %attention.1 = (bf16[2,1,1536]{2,1,0:T(2,128)(2,1)S(1)}, bf16[192,1536]{1,0:T(8,128)(2,1)S(1)}, bf16[80,384]{1,0:T(8,128)(2,1)S(1)}, bf16[80,384]{1,0:T(8,128)(2...) custom-call(s32[5]{0:T(128)S(1)} %stack.16.info, bf16[64,1536]{1,0:T(8,128)(2,1)S(1)} %get-tuple-element.28.queries, ...), custom_call_target="tpu_custom_call" | custom-call | flops 100663296 | bytes 917504 | tf_op jit(solution)/shard_map/attention/pallas_call | solution.py:152
  21.5 2.9 %collective-permute-start.4 = (bf16[80,384]{1,0:T(8,128)(2,1)S(1)}, bf16[80,384]{1,0:T(8,128)(2,1)S(1)}, u32[]{:S(2)}, u32[]{:S(2)}) collective-permute-start(bf16[80,384]{1,0:T(8,128)(2,1)S(1)} %get-tuple-element.34), channel_id=1, source_target_pairs={{0,8},{4,12},{8,0},{12,4},{1,9},{5,13},{9,1},{13,5},{2,10},{6,14},... | collective-permute-start | bytes 184328 | tf_op jit(solution)/shard_map/ppermute | solution.py:35
  26.0 1.5 %collective-permute-start.7 = (bf16[80,384]{1,0:T(8,128)(2,1)S(1)}, bf16[80,384]{1,0:T(8,128)(2,1)S(1)}, u32[]{:S(2)}, u32[]{:S(2)}) collective-permute-start(bf16[80,384]{1,0:T(8,128)(2,1)S(1)} %get-tuple-element.33.refs_0_), channel_id=1, source_target_pairs={{0,2},{2,0},{1,3},{3,1},{4,6},{6,4},{5,7},{7,5},{8,10},{10,8},{9,1... | collective-permute-start | bytes 184328 | tf_op jit(solution)/shard_map/ppermute | solution.py:35
  28.4 1.6 %collective-permute-start.8 = (bf16[80,384]{1,0:T(8,128)(2,1)S(1)}, bf16[80,384]{1,0:T(8,128)(2,1)S(1)}, u32[]{:S(2)}, u32[]{:S(2)}) collective-permute-start(bf16[80,384]{1,0:T(8,128)(2,1)S(1)} %collective-permute-done.4.refs_1_), channel_id=1, source_target_pairs={{0,2},{2,0},{1,3},{3,1},{4,6},{6,4},{5,7},{7,5},{8,10},{10,8},{9,1... | collective-permute-start | bytes 184328 | tf_op jit(solution)/shard_map/ppermute | solution.py:35
  31.0 1.5 %collective-permute-start.9 = (bf16[80,384]{1,0:T(8,128)(2,1)S(1)}, bf16[80,384]{1,0:T(8,128)(2,1)S(1)}, u32[]{:S(2)}, u32[]{:S(2)}) collective-permute-start(bf16[80,384]{1,0:T(8,128)(2,1)S(1)} %collective-permute-done.5.refs_2_), channel_id=1, source_target_pairs={{0,2},{2,0},{1,3},{3,1},{4,6},{6,4},{5,7},{7,5},{8,10},{10,8},{9,1... | collective-permute-start | bytes 184328 | tf_op jit(solution)/shard_map/ppermute | solution.py:35
  33.1 2.1 %collective-permute-done.9.refs_6_ = bf16[80,384]{1,0:T(8,128)(2,1)S(1)} collective-permute-done((bf16[80,384]{1,0:T(8,128)(2,1)S(1)}, bf16[80,384]{1,0:T(8,128)(2,1)S(1)}, u32[]{:S(2)}, u32[]{:S(2)}) %collective-permute-start.9) | collective-permute-done | bytes 61472 | tf_op jit(solution)/shard_map/ppermute | solution.py:35
  35.2 1.5 %collective-permute-done.10.refs_7_ = bf16[80,384]{1,0:T(8,128)(2,1)S(1)} collective-permute-done((bf16[80,384]{1,0:T(8,128)(2,1)S(1)}, bf16[80,384]{1,0:T(8,128)(2,1)S(1)}, u32[]{:S(2)}, u32[]{:S(2)}) %collective-permute-start.10) | collective-permute-done | bytes 61472 | tf_op jit(solution)/shard_map/ppermute | solution.py:35
  36.7 1.5 %projection.1 = (bf16[8,256]{1,0:T(8,128)(2,1)S(1)}, f32[64,1536]{1,0:T(8,128)S(1)}, bf16[64,1536]{1,0:T(8,128)(2,1)S(1)}, bf16[64,1536]{1,0:T(8,128)(2,1)S(1)}, bf16[64,1536]{1,0:T(8,128)(2,1)S(1)}) custom-call(s32[5]{0:T(128)S(1)} %stack.16.info, bf16[80,384]{1,0:T(8,128)(2,1)S(1)} %get-tuple-element.33.refs_0_, ...), custom_call_target="tpu_custom_call" | custom-call | flops 603979776 | bytes 3932160 | tf_op jit(solution)/shard_map/projection/pallas_call | solution.py:268
  39.2 3.2 %collective-permute-start.13 = (bf16[64,1536]{1,0:T(8,128)(2,1)S(1)}, bf16[64,1536]{1,0:T(8,128)(2,1)S(1)}, u32[]{:S(2)}, u32[]{:S(2)}) collective-permute-start(bf16[64,1536]{1,0:T(8,128)(2,1)S(1)} %get-tuple-element.41), channel_id=1, source_target_pairs={{0,8},{4,12},{8,0},{12,4},{1,9},{5,13},{9,1},{13,5},{2,10},{6,14},... | collective-permute-start | bytes 589832 | tf_op jit(solution)/shard_map/ppermute | solution.py:35
  42.7 12.1 %fetch.1 = (bf16[2,3072,512]{2,1,0:T(8,128)(2,1)S(1)}, bf16[2,3072,512]{2,1,0:T(8,128)(2,1)S(1)}, bf16[2,3072,512]{2,1,0:T(8,128)(2,1)S(1)}, bf16[2,3072,512]{2,...) custom-call(bf16[2,3072,2048]{2,1,0:T(8,128)(2,1)} %refs_16_.1, ...), custom_call_target="tpu_custom_call" | custom-call | bytes 75497472 | tf_op jit(solution)/shard_map/fetch/pallas_call | solution.py:304
  54.8 1.8 %collective-permute-done.13.refs_1_ = bf16[64,1536]{1,0:T(8,128)(2,1)S(1)} collective-permute-done((bf16[64,1536]{1,0:T(8,128)(2,1)S(1)}, bf16[64,1536]{1,0:T(8,128)(2,1)S(1)}, u32[]{:S(2)}, u32[]{:S(2)}) %collective-permute-start.13) | collective-permute-done | bytes 196640 | tf_op jit(solution)/shard_map/ppermute | solution.py:35
  57.4 3.0 %collective-permute-start.17 = (bf16[64,1536]{1,0:T(8,128)(2,1)S(1)}, bf16[64,1536]{1,0:T(8,128)(2,1)S(1)}, u32[]{:S(2)}, u32[]{:S(2)}) collective-permute-start(bf16[64,1536]{1,0:T(8,128)(2,1)S(1)} %get-tuple-element.45.refs_0_), channel_id=1, source_target_pairs={{0,4},{4,0},{8,12},{12,8},{1,5},{5,1},{9,13},{13,9},{2,6},{6,2},{1... | collective-permute-start | bytes 589832 | tf_op jit(solution)/shard_map/ppermute | solution.py:35
  60.5 2.5 %collective-permute-start.16 = (bf16[64,1536]{1,0:T(8,128)(2,1)S(1)}, bf16[64,1536]{1,0:T(8,128)(2,1)S(1)}, u32[]{:S(2)}, u32[]{:S(2)}) collective-permute-start(bf16[64,1536]{1,0:T(8,128)(2,1)S(1)} %get-tuple-element.45.refs_0_), channel_id=1, source_target_pairs={{0,12},{4,8},{8,4},{12,0},{1,13},{5,9},{9,5},{13,1},{2,14},{6,10},... | collective-permute-start | bytes 589832 | tf_op jit(solution)/shard_map/ppermute | solution.py:35
  64.3 1.5 %collective-permute-done.17.refs_3_ = bf16[64,1536]{1,0:T(8,128)(2,1)S(1)} collective-permute-done((bf16[64,1536]{1,0:T(8,128)(2,1)S(1)}, bf16[64,1536]{1,0:T(8,128)(2,1)S(1)}, u32[]{:S(2)}, u32[]{:S(2)}) %collective-permute-start.17) | collective-permute-done | bytes 196640 | tf_op jit(solution)/shard_map/ppermute | solution.py:35
  66.8 5.7 %collective-permute-done.16.refs_2_ = bf16[64,1536]{1,0:T(8,128)(2,1)S(1)} collective-permute-done((bf16[64,1536]{1,0:T(8,128)(2,1)S(1)}, bf16[64,1536]{1,0:T(8,128)(2,1)S(1)}, u32[]{:S(2)}, u32[]{:S(2)}) %collective-permute-start.16) | collective-permute-done | bytes 196640 | tf_op jit(solution)/shard_map/ppermute | solution.py:35
  72.5 1.4 %collective-permute-start.20 = (bf16[64,1536]{1,0:T(8,128)(2,1)S(1)}, bf16[64,1536]{1,0:T(8,128)(2,1)S(1)}, u32[]{:S(2)}, u32[]{:S(2)}) collective-permute-start(bf16[64,1536]{1,0:T(8,128)(2,1)S(1)} %collective-permute-done.16.refs_2_), channel_id=1, source_target_pairs={{0,2},{2,0},{1,3},{3,1},{4,6},{6,4},{5,7},{7,5},{8,10},{10,8},{9,1... | collective-permute-start | bytes 589832 | tf_op jit(solution)/shard_map/ppermute | solution.py:35
  73.9 4.3 %collective-permute-done.15.refs_1_ = bf16[64,1536]{1,0:T(8,128)(2,1)S(1)} collective-permute-done((bf16[64,1536]{1,0:T(8,128)(2,1)S(1)}, bf16[64,1536]{1,0:T(8,128)(2,1)S(1)}, u32[]{:S(2)}, u32[]{:S(2)}) %collective-permute-start.15) | collective-permute-done | bytes 196640 | tf_op jit(solution)/shard_map/ppermute | solution.py:35
  79.3 4.6 %collective-permute-done.19.refs_5_ = bf16[64,1536]{1,0:T(8,128)(2,1)S(1)} collective-permute-done((bf16[64,1536]{1,0:T(8,128)(2,1)S(1)}, bf16[64,1536]{1,0:T(8,128)(2,1)S(1)}, u32[]{:S(2)}, u32[]{:S(2)}) %collective-permute-start.19) | collective-permute-done | bytes 196640 | tf_op jit(solution)/shard_map/ppermute | solution.py:35
  83.9 14.9 %experts.1 = bf16[2,160,2048]{2,1,0:T(8,128)(2,1)} custom-call(s32[5]{0:T(128)S(1)} %stack.16.info, bf16[64,1536]{1,0:T(8,128)(2,1)S(1)} %get-tuple-element.45.refs_0_, bf16[64,1536]{1,0:T(8,128)(2,1)S(1)} %collective-permute-done.15.refs_1_, bf16[64,1536]{1,0:T(8,128)(2,1)S(1)} %collective-permute-done.16.refs_2_, ...), custom_call_target="tpu_custom_call" | custom-call | flops 8053063680 | bytes 25165824 | tf_op jit(solution)/shard_map/experts/pallas_call | solution.py:467
  (30 shorter events, 12.9 us)
Async XLA Ops:
  3.6 16.3 %collective-permute-start.3 = (bf16[192,1536]{1,0:T(8,128)(2,1)S(1)}, bf16[192,1536]{1,0:T(8,128)(2,1)S(1)}, u32[]{:S(2)}, u32[]{:S(2)}) collective-permute-start(bf16[192,1536]{1,0:T(8,128)(2,1)S(1)} %get-tuple-element.32), channel_id=1, source_target_pairs={{0,2},{2,0},{1,3},{3,1},{4,6},{6,4},{5,7},{7,5},{8,10},{10,8},{9,1... | collective-permute-start | bytes 1769480 | tf_op jit(solution)/shard_map/ppermute | solution.py:35
  6.6 10.0 %collective-permute-start.2 = (bf16[64,512]{1,0:T(8,128)(2,1)S(1)}, bf16[64,512]{1,0:T(8,128)(2,1)S(1)}, u32[]{:S(2)}, u32[]{:S(2)}) collective-permute-start(bf16[64,512]{1,0:T(8,128)(2,1)S(1)} %get-tuple-element.31.refs_0_), channel_id=1, source_target_pairs={{0,12},{4,8},{1,13},{5,9},{2,14},{6,10},{3,15},{7,11},{16,28},{20,... | collective-permute-start | bytes 196616 | tf_op jit(solution)/shard_map/ppermute | solution.py:35
  12.1 4.5 %collective-permute-start.1 = (bf16[64,512]{1,0:T(8,128)(2,1)S(1)}, bf16[64,512]{1,0:T(8,128)(2,1)S(1)}, u32[]{:S(2)}, u32[]{:S(2)}) collective-permute-start(bf16[64,512]{1,0:T(8,128)(2,1)S(1)} %get-tuple-element.31.refs_0_), channel_id=1, source_target_pairs={{0,8},{4,12},{1,9},{5,13},{2,10},{6,14},{3,11},{7,15},{16,24},{20,... | collective-permute-start | bytes 196616 | tf_op jit(solution)/shard_map/ppermute | solution.py:35
  13.4 4.4 %collective-permute-start = (bf16[64,512]{1,0:T(8,128)(2,1)S(1)}, bf16[64,512]{1,0:T(8,128)(2,1)S(1)}, u32[]{:S(2)}, u32[]{:S(2)}) collective-permute-start(bf16[64,512]{1,0:T(8,128)(2,1)S(1)} %get-tuple-element.31.refs_0_), channel_id=1, source_target_pairs={{0,4},{8,12},{1,5},{9,13},{2,6},{10,14},{3,7},{11,15},{16,20},{24,... | collective-permute-start | bytes 196616 | tf_op jit(solution)/shard_map/ppermute | solution.py:35
  21.5 15.2 %collective-permute-start.11 = (bf16[192,1536]{1,0:T(8,128)(2,1)S(1)}, bf16[192,1536]{1,0:T(8,128)(2,1)S(1)}, u32[]{:S(2)}, u32[]{:S(2)}) collective-permute-start(bf16[192,1536]{1,0:T(8,128)(2,1)S(1)} %get-tuple-element.38), channel_id=1, source_target_pairs={{0,1},{1,0},{2,3},{3,2},{4,5},{5,4},{6,7},{7,6},{8,9},{9,8},{10,11... | collective-permute-start | bytes 1769480 | tf_op jit(solution)/shard_map/ppermute | solution.py:35
  21.5 6.9 %collective-permute-start.4 = (bf16[80,384]{1,0:T(8,128)(2,1)S(1)}, bf16[80,384]{1,0:T(8,128)(2,1)S(1)}, u32[]{:S(2)}, u32[]{:S(2)}) collective-permute-start(bf16[80,384]{1,0:T(8,128)(2,1)S(1)} %get-tuple-element.34), channel_id=1, source_target_pairs={{0,8},{4,12},{8,0},{12,4},{1,9},{5,13},{9,1},{13,5},{2,10},{6,14},... | collective-permute-start | bytes 184328 | tf_op jit(solution)/shard_map/ppermute | solution.py:35
  24.5 6.5 %collective-permute-start.5 = (bf16[80,384]{1,0:T(8,128)(2,1)S(1)}, bf16[80,384]{1,0:T(8,128)(2,1)S(1)}, u32[]{:S(2)}, u32[]{:S(2)}) collective-permute-start(bf16[80,384]{1,0:T(8,128)(2,1)S(1)} %get-tuple-element.35), channel_id=1, source_target_pairs={{0,12},{4,8},{8,4},{12,0},{1,13},{5,9},{9,5},{13,1},{2,14},{6,10},... | collective-permute-start | bytes 184328 | tf_op jit(solution)/shard_map/ppermute | solution.py:35
  25.8 6.7 %collective-permute-start.6 = (bf16[80,384]{1,0:T(8,128)(2,1)S(1)}, bf16[80,384]{1,0:T(8,128)(2,1)S(1)}, u32[]{:S(2)}, u32[]{:S(2)}) collective-permute-start(bf16[80,384]{1,0:T(8,128)(2,1)S(1)} %get-tuple-element.36), channel_id=1, source_target_pairs={{0,4},{4,0},{8,12},{12,8},{1,5},{5,1},{9,13},{13,9},{2,6},{6,2},{1... | collective-permute-start | bytes 184328 | tf_op jit(solution)/shard_map/ppermute | solution.py:35
  26.0 7.0 %collective-permute-start.7 = (bf16[80,384]{1,0:T(8,128)(2,1)S(1)}, bf16[80,384]{1,0:T(8,128)(2,1)S(1)}, u32[]{:S(2)}, u32[]{:S(2)}) collective-permute-start(bf16[80,384]{1,0:T(8,128)(2,1)S(1)} %get-tuple-element.33.refs_0_), channel_id=1, source_target_pairs={{0,2},{2,0},{1,3},{3,1},{4,6},{6,4},{5,7},{7,5},{8,10},{10,8},{9,1... | collective-permute-start | bytes 184328 | tf_op jit(solution)/shard_map/ppermute | solution.py:35
  28.4 4.6 %collective-permute-start.8 = (bf16[80,384]{1,0:T(8,128)(2,1)S(1)}, bf16[80,384]{1,0:T(8,128)(2,1)S(1)}, u32[]{:S(2)}, u32[]{:S(2)}) collective-permute-start(bf16[80,384]{1,0:T(8,128)(2,1)S(1)} %collective-permute-done.4.refs_1_), channel_id=1, source_target_pairs={{0,2},{2,0},{1,3},{3,1},{4,6},{6,4},{5,7},{7,5},{8,10},{10,8},{9,1... | collective-permute-start | bytes 184328 | tf_op jit(solution)/shard_map/ppermute | solution.py:35
  31.0 4.2 %collective-permute-start.9 = (bf16[80,384]{1,0:T(8,128)(2,1)S(1)}, bf16[80,384]{1,0:T(8,128)(2,1)S(1)}, u32[]{:S(2)}, u32[]{:S(2)}) collective-permute-start(bf16[80,384]{1,0:T(8,128)(2,1)S(1)} %collective-permute-done.5.refs_2_), channel_id=1, source_target_pairs={{0,2},{2,0},{1,3},{3,1},{4,6},{6,4},{5,7},{7,5},{8,10},{10,8},{9,1... | collective-permute-start | bytes 184328 | tf_op jit(solution)/shard_map/ppermute | solution.py:35
  32.5 4.2 %collective-permute-start.10 = (bf16[80,384]{1,0:T(8,128)(2,1)S(1)}, bf16[80,384]{1,0:T(8,128)(2,1)S(1)}, u32[]{:S(2)}, u32[]{:S(2)}) collective-permute-start(bf16[80,384]{1,0:T(8,128)(2,1)S(1)} %collective-permute-done.6.refs_3_), channel_id=1, source_target_pairs={{0,2},{2,0},{1,3},{3,1},{4,6},{6,4},{5,7},{7,5},{8,10},{10,8},{9,1... | collective-permute-start | bytes 184328 | tf_op jit(solution)/shard_map/ppermute | solution.py:35
  38.3 16.6 %collective-permute-start.12 = (bf16[64,1536]{1,0:T(8,128)(2,1)S(1)}, bf16[64,1536]{1,0:T(8,128)(2,1)S(1)}, u32[]{:S(2)}, u32[]{:S(2)}) collective-permute-start(bf16[64,1536]{1,0:T(8,128)(2,1)S(1)} %get-tuple-element.40), channel_id=1, source_target_pairs={{0,4},{4,0},{8,12},{12,8},{1,5},{5,1},{9,13},{13,9},{2,6},{6,2},{1... | collective-permute-start | bytes 589832 | tf_op jit(solution)/shard_map/ppermute | solution.py:35
  39.2 17.5 %collective-permute-start.13 = (bf16[64,1536]{1,0:T(8,128)(2,1)S(1)}, bf16[64,1536]{1,0:T(8,128)(2,1)S(1)}, u32[]{:S(2)}, u32[]{:S(2)}) collective-permute-start(bf16[64,1536]{1,0:T(8,128)(2,1)S(1)} %get-tuple-element.41), channel_id=1, source_target_pairs={{0,8},{4,12},{8,0},{12,4},{1,9},{5,13},{9,1},{13,5},{2,10},{6,14},... | collective-permute-start | bytes 589832 | tf_op jit(solution)/shard_map/ppermute | solution.py:35
  42.4 14.3 %copy-start = (bf16[1,64,1536]{2,1,0:T(8,128)(2,1)S(1)}, bf16[1,64,1536]{2,1,0:T(8,128)(2,1)}, u32[]{:S(2)}) copy-start(bf16[1,64,1536]{2,1,0:T(8,128)(2,1)} %param.14) | copy-start | bytes 589828
  42.4 14.2 %collective-permute-start.14 = (bf16[64,1536]{1,0:T(8,128)(2,1)S(1)}, bf16[64,1536]{1,0:T(8,128)(2,1)S(1)}, u32[]{:S(2)}, u32[]{:S(2)}) collective-permute-start(bf16[64,1536]{1,0:T(8,128)(2,1)S(1)} %get-tuple-element.42.after), channel_id=1, source_target_pairs={{0,12},{4,8},{8,4},{12,0},{1,13},{5,9},{9,5},{13,1},{2,14},{6,10},... | collective-permute-start | bytes 589832 | tf_op jit(solution)/shard_map/ppermute | solution.py:35
  57.4 8.3 %collective-permute-start.17 = (bf16[64,1536]{1,0:T(8,128)(2,1)S(1)}, bf16[64,1536]{1,0:T(8,128)(2,1)S(1)}, u32[]{:S(2)}, u32[]{:S(2)}) collective-permute-start(bf16[64,1536]{1,0:T(8,128)(2,1)S(1)} %get-tuple-element.45.refs_0_), channel_id=1, source_target_pairs={{0,4},{4,0},{8,12},{12,8},{1,5},{5,1},{9,13},{13,9},{2,6},{6,2},{1... | collective-permute-start | bytes 589832 | tf_op jit(solution)/shard_map/ppermute | solution.py:35
  60.5 12.0 %collective-permute-start.16 = (bf16[64,1536]{1,0:T(8,128)(2,1)S(1)}, bf16[64,1536]{1,0:T(8,128)(2,1)S(1)}, u32[]{:S(2)}, u32[]{:S(2)}) collective-permute-start(bf16[64,1536]{1,0:T(8,128)(2,1)S(1)} %get-tuple-element.45.refs_0_), channel_id=1, source_target_pairs={{0,12},{4,8},{8,4},{12,0},{1,13},{5,9},{9,5},{13,1},{2,14},{6,10},... | collective-permute-start | bytes 589832 | tf_op jit(solution)/shard_map/ppermute | solution.py:35
  63.0 15.3 %collective-permute-start.15 = (bf16[64,1536]{1,0:T(8,128)(2,1)S(1)}, bf16[64,1536]{1,0:T(8,128)(2,1)S(1)}, u32[]{:S(2)}, u32[]{:S(2)}) collective-permute-start(bf16[64,1536]{1,0:T(8,128)(2,1)S(1)} %get-tuple-element.45.refs_0_), channel_id=1, source_target_pairs={{0,8},{4,12},{8,0},{12,4},{1,9},{5,13},{9,1},{13,5},{2,10},{6,14},... | collective-permute-start | bytes 589832 | tf_op jit(solution)/shard_map/ppermute | solution.py:35
  63.0 16.3 %collective-permute-start.18 = (bf16[64,1536]{1,0:T(8,128)(2,1)S(1)}, bf16[64,1536]{1,0:T(8,128)(2,1)S(1)}, u32[]{:S(2)}, u32[]{:S(2)}) collective-permute-start(bf16[64,1536]{1,0:T(8,128)(2,1)S(1)} %get-tuple-element.45.refs_0_), channel_id=1, source_target_pairs={{0,2},{2,0},{1,3},{3,1},{4,6},{6,4},{5,7},{7,5},{8,10},{10,8},{9,1... | collective-permute-start | bytes 589832 | tf_op jit(solution)/shard_map/ppermute | solution.py:35
  65.8 13.6 %collective-permute-start.21 = (bf16[64,1536]{1,0:T(8,128)(2,1)S(1)}, bf16[64,1536]{1,0:T(8,128)(2,1)S(1)}, u32[]{:S(2)}, u32[]{:S(2)}) collective-permute-start(bf16[64,1536]{1,0:T(8,128)(2,1)S(1)} %collective-permute-done.17.refs_3_), channel_id=1, source_target_pairs={{0,2},{2,0},{1,3},{3,1},{4,6},{6,4},{5,7},{7,5},{8,10},{10,8},{9,1... | collective-permute-start | bytes 589832 | tf_op jit(solution)/shard_map/ppermute | solution.py:35
  72.5 6.8 %collective-permute-start.20 = (bf16[64,1536]{1,0:T(8,128)(2,1)S(1)}, bf16[64,1536]{1,0:T(8,128)(2,1)S(1)}, u32[]{:S(2)}, u32[]{:S(2)}) collective-permute-start(bf16[64,1536]{1,0:T(8,128)(2,1)S(1)} %collective-permute-done.16.refs_2_), channel_id=1, source_target_pairs={{0,2},{2,0},{1,3},{3,1},{4,6},{6,4},{5,7},{7,5},{8,10},{10,8},{9,1... | collective-permute-start | bytes 589832 | tf_op jit(solution)/shard_map/ppermute | solution.py:35
  78.2 5.7 %collective-permute-start.19 = (bf16[64,1536]{1,0:T(8,128)(2,1)S(1)}, bf16[64,1536]{1,0:T(8,128)(2,1)S(1)}, u32[]{:S(2)}, u32[]{:S(2)}) collective-permute-start(bf16[64,1536]{1,0:T(8,128)(2,1)S(1)} %collective-permute-done.15.refs_1_), channel_id=1, source_target_pairs={{0,2},{2,0},{1,3},{3,1},{4,6},{6,4},{5,7},{7,5},{8,10},{10,8},{9,1... | collective-permute-start | bytes 589832 | tf_op jit(solution)/shard_map/ppermute | solution.py:35

commit v3 on v2

v3 whole, which is shorter than its diff:
```python
import functools
import math

import jax
import jax.numpy as jnp
from jax import lax
from jax.experimental import pallas as pl
from jax.experimental.pallas import tpu as pltpu
from jax.sharding import PartitionSpec as P

HEAD_SIZE = 128
QUERY_HEAD_COUNT = 24
KEY_VALUE_HEADS = 4
MOST = 40
EXTRA = 16
ATTENDED_ORDER = (0, 1, 2, 3)
STREAM_ORDER = (0, 3, 1, 2)
EPS = 1e-05
NEG = -1e30
F32 = jnp.float32
BF16 = jnp.bfloat16

VMEM = pl.BlockSpec(memory_space=pltpu.VMEM)
SMEM = pl.BlockSpec(memory_space=pltpu.SMEM)
ANY = pl.BlockSpec(memory_space=pl.ANY)
place = pltpu.with_memory_space_constraint
HBM = pl.BlockSpec(memory_space=pltpu.HBM)


def pairwise(count):
    return count in (1, 2, 4)


def swap(array, axis, step, upward=False):
    count = lax.axis_size(axis)
    pairs = [(i, i ^ step) for i in range(count) if not upward or i < i ^ step]
    return lax.ppermute(array, axis, pairs)


def steps_of(count):
    return [k for k in (2, 3, 1) if k < count]


def shuffled(pieces, order):
    return [pieces[k] for k in order] if len(pieces) == len(order) else list(pieces)


def sorted_back(pieces, order):
    return [pieces[order.index(k)] for k in range(4)] if len(pieces) == len(order) else list(pieces)


def swaps(arrays, axis, upward=False):
    got = {k: swap(arrays[k], axis, k, upward) for k in steps_of(len(arrays))}
    return [arrays[0]] + [got[k] for k in range(1, len(arrays))]


def spread(array, axis, upward=False):
    count = lax.axis_size(axis)
    if pairwise(count):
        return swaps([array] * count, axis, upward)
    return [lax.all_gather(array, axis, axis=0, tiled=True)]


def attention_kernel(shape, lengths, matrix, queries, gain_in, routes, numer, *refs):
    tokens, groups, per_group, pieces, carried, split = shape
    kv_refs, refs = refs[:pieces], refs[pieces:]
    carried_in, refs = refs[:carried], refs[carried:]
    own, gain_out, refs = refs[0], refs[1], refs[2:]
    carried_out, refs = refs[:carried], refs[carried:]
    outs, sems = refs[:-1], refs[-1]
    rank = lax.axis_index("seq")
    share = own.shape[1]
    lanes = pl.ds(pl.multiple_of(lax.axis_index("head") * share, share), share)
    pairs = [(matrix.at[:, lanes], own), *zip(carried_in, carried_out)]
    copies = [pltpu.make_async_copy(*pair, sems.at[i]) for i, pair in enumerate(pairs)]
    for copy in copies:
        copy.start()
    gain_out[...] = gain_in[...]
    flip, valid_len = rank if split else 0, lengths[0]
    width = groups * HEAD_SIZE
    key_parts = [ref[:, :width] for ref in kv_refs]
    value_parts = [ref[:, width:] for ref in kv_refs]
    all_keys = jnp.concatenate(key_parts, axis=0)
    all_values = jnp.concatenate(value_parts, axis=0)
    length = all_keys.shape[0]
    column = lax.broadcasted_iota(jnp.int32, (tokens, length), 1)
    block = lax.div(column, tokens)
    key_pos = lax.bitwise_xor(block, flip) * tokens + (column - block * tokens)
    query_pos = rank * tokens + lax.broadcasted_iota(jnp.int32, (tokens, length), 0)
    allowed = ((key_pos <= query_pos) & (key_pos < valid_len)).astype(F32)
    allowed = jnp.concatenate([allowed] * per_group, axis=0) > 0
    scale = 1.0 / math.sqrt(HEAD_SIZE)
    attended = []
    for g in range(groups):
        heads = [g * per_group + a for a in range(per_group)]
        rows = jnp.concatenate(
            [queries[:, h * HEAD_SIZE : (h + 1) * HEAD_SIZE] for h in heads], axis=0
        )
        lanes = slice(g * HEAD_SIZE, (g + 1) * HEAD_SIZE)
        scores = (
            lax.dot_general(
                rows, all_keys[:, lanes], (((1,), (1,)), ((), ())), preferred_element_type=F32
            )
            * scale
        )
        scores = jnp.where(allowed, scores, NEG)
        top = jnp.max(scores, axis=-1, keepdims=True)
        weights = jnp.where(allowed, jnp.exp(scores - top), 0.0)
        denom = jnp.sum(weights, axis=-1, keepdims=True)
        mixed = jnp.dot(weights.astype(BF16), all_values[:, lanes], preferred_element_type=F32)
        mixed = mixed / denom
        attended += [mixed[a * tokens : (a + 1) * tokens] for a in range(per_group)]
    if not split:
        outs[0][...] = jnp.concatenate(attended, axis=1).astype(BF16)
        for copy in copies:
            copy.wait()
        return
    count = len(outs)
    part = HEAD_SIZE // count
    shares = [
        jnp.concatenate([o[:, j * part : (j + 1) * part] for o in attended], axis=1).astype(BF16)
        for j in range(count)
    ]
    routing = jnp.concatenate(
        [routes[...], numer[...], jnp.zeros((EXTRA - 3, tokens), jnp.int32)], axis=0
    )
    routing = routing.astype(F32).astype(BF16)
    for k in range(count):
        chosen = shares[k]
        for s in range(1, count):
            chosen = jnp.where(rank == s, shares[s ^ k], chosen)
        outs[k][:tokens, :] = chosen
        outs[k][tokens:, :] = jnp.zeros((EXTRA, chosen.shape[1]), BF16)
        outs[k][tokens:, :tokens] = routing
    for copy in copies:
        copy.wait()


def attend(lengths, matrix, queries, gain, routes, numer, kv_parts, carried, count):
    tokens = queries.shape[0]
    groups = kv_parts[0].shape[1] // (2 * HEAD_SIZE)
    per_group = QUERY_HEAD_COUNT // KEY_VALUE_HEADS
    split = pairwise(count)
    if split:
        out_shape = [
            jax.ShapeDtypeStruct((tokens + EXTRA, queries.shape[1] // count), BF16)
            for _ in range(count)
        ]
    else:
        out_shape = [jax.ShapeDtypeStruct(queries.shape, BF16)]
    length = tokens * count
    limit = min(40 << 20, (4 << 20) + 48 * per_group * tokens * length)
    out_shape = [
        jax.ShapeDtypeStruct((matrix.shape[0], gain.shape[2]), BF16),
        *[jax.ShapeDtypeStruct(array.shape, BF16) for array in (gain, *carried)],
    ] + out_shape
    return pl.pallas_call(
        functools.partial(
            attention_kernel, (tokens, groups, per_group, len(kv_parts), len(carried), split)
        ),
        out_shape=out_shape,
        in_specs=[SMEM, HBM] + [VMEM] * (4 + len(kv_parts)) + [ANY] * len(carried),
        out_specs=[VMEM] * len(out_shape),
        scratch_shapes=[pltpu.SemaphoreType.DMA((1 + len(carried),))],
        compiler_params=pltpu.CompilerParams(vmem_limit_bytes=limit),
        cost_estimate=pl.CostEstimate(
            flops=4 * tokens * length * queries.shape[1],
            bytes_accessed=4 * queries.size + 4 * length * kv_parts[0].shape[1],
            transcendentals=tokens * length * groups * per_group,
        ),
        name="attention",
    )(lengths, place(matrix, pltpu.HBM), queries, gain, routes, numer, *kv_parts, *carried)


def prepare_kernel(matrix, queries, keys, values, routes, numer, *refs):
    kv, rows, first_routes, weights = refs[:4]
    columns, sems = refs[4:-1], refs[-1]
    width = keys.shape[1]
    if columns:
        height, share = columns[0].shape
    pairs = [
        (keys, kv.at[:, :width]),
        (values, kv.at[:, width:]),
        (queries, rows),
        (routes, first_routes),
        (numer, weights),
    ]
    head, core = lax.axis_index("head"), lax.axis_index("dat")
    for m, out in enumerate(columns):
        lanes = pl.ds(pl.multiple_of(lax.bitwise_xor(head, m + 1) * share, share), share)
        if out.shape[0] == matrix.shape[0]:
            source = matrix.at[:, lanes]
        else:
            source = matrix.at[pl.ds(pl.multiple_of(core * height, height), height), lanes]
        pairs.insert(2, (source, out))
    copies = [pltpu.make_async_copy(*pair, sems.at[i]) for i, pair in enumerate(pairs)]
    for copy in copies:
        copy.start()
    for copy in copies:
        copy.wait()


def prepare(matrix, queries, keys, values, routes, numer, head_count, halves):
    rows, features = matrix.shape
    tokens = queries.shape[0]
    share = features // head_count
    out_shape = [
        jax.ShapeDtypeStruct((tokens, 2 * keys.shape[1]), BF16),
        jax.ShapeDtypeStruct(queries.shape, BF16),
        jax.ShapeDtypeStruct(routes.shape, jnp.int32),
        jax.ShapeDtypeStruct(numer.shape, jnp.int32),
    ] + [pltpu.VMEM((rows // halves, share), BF16)] * (head_count - 1)
    sources = [matrix, queries, keys, values, routes, numer]
    return pl.pallas_call(
        prepare_kernel,
        out_shape=out_shape,
        in_specs=[HBM] * len(sources),
        out_specs=[VMEM] * len(out_shape),
        scratch_shapes=[pltpu.SemaphoreType.DMA((4 + head_count,))],
        compiler_params=pltpu.CompilerParams(vmem_limit_bytes=8 << 20),
        cost_estimate=pl.CostEstimate(
            flops=0, bytes_accessed=4 * rows * features, transcendentals=0
        ),
        name="prepare",
    )(*[place(source, pltpu.HBM) for source in sources])


def project_kernel(parts, pieces, tokens, halves, *refs):
    rows = [sorted_back(refs[m * pieces : (m + 1) * pieces], ATTENDED_ORDER) for m in range(parts)]
    refs = refs[parts * pieces :]
    weights = [refs[:1]] + [refs[1 + m * halves : 1 + (m + 1) * halves] for m in range(parts - 1)]
    refs = refs[1 + (parts - 1) * halves :]
    outs = refs
    if tokens:
        route, outs = outs[0], outs[1:]
        route[...] = jnp.concatenate([ref[tokens : tokens + 8, :tokens] for ref in rows[0]], axis=1)
    total = None
    core = lax.axis_index("dat")
    for m in range(parts):
        stacked = jnp.concatenate([ref[: tokens or ref.shape[0]] for ref in rows[m]], axis=0)
        if len(weights[m]) == 1:
            factors = [stacked]
        else:
            half = stacked.shape[1] // 2
            low, high = stacked[:, :half], stacked[:, half:]
            factors = [jnp.where(core == 0, low, high), jnp.where(core == 0, high, low)]
        for factor, weight in zip(factors, weights[m]):
            product = jnp.dot(factor, weight[...], preferred_element_type=F32)
            total = product if total is None else total + product
    at = 0
    for i, out in enumerate(outs):
        out[...] = total[at : at + out.shape[0]].astype(out.dtype)
        at += out.shape[0]


def project(rows, weights, each):
    parts, pieces = len(rows), len(rows[0])
    depth, width = weights[0][0].shape
    flat_weights = [w for part in weights for w in part]
    heights = [each or p.shape[0] for p in rows[0]]
    tokens = sum(heights)
    out_shape = [
        jax.ShapeDtypeStruct((h, width), BF16 if each and i else F32)
        for i, h in enumerate(heights)
    ]
    if each:
        out_shape = [jax.ShapeDtypeStruct((8, tokens), BF16)] + out_shape
    flat = [p for part in rows for p in shuffled(part, ATTENDED_ORDER)]
    return pl.pallas_call(
        functools.partial(project_kernel, parts, pieces, each, len(weights[-1])),
        out_shape=out_shape,
        in_specs=[VMEM] * (len(flat) + len(flat_weights)),
        out_specs=[VMEM] * len(out_shape),
        compiler_params=pltpu.CompilerParams(vmem_limit_bytes=min(40 << 20, (4 << 20) + 16 * tokens * width)),
        cost_estimate=pl.CostEstimate(
            flops=2 * tokens * width * parts * depth,
            bytes_accessed=2 * parts * depth * width + 4 * tokens * width,
            transcendentals=0,
        ),
        name="projection",
    )(*flat, *flat_weights)


def fetch_kernel(chunk, gate_hbm, up_hbm, after, *refs):
    outs, done, sems = refs[:-2], refs[-2], refs[-1]
    per_expert = gate_hbm.shape[2] // chunk
    copies = []
    for step, out in enumerate(outs):
        at = pl.ds((step % per_expert) * chunk, chunk)
        for i, source in enumerate((gate_hbm, up_hbm)):
            copies.append(
                pltpu.make_async_copy(
                    source.at[step // per_expert, :, at], out.at[i], sems.at[step, i]
                )
            )
    for copy in copies:
        copy.start()
    done[...] = jnp.zeros_like(done)
    for copy in copies:
        copy.wait()


def fetch(expert_gate, expert_up, after, chunk, early, mark):
    features = expert_gate.shape[1]
    return pl.pallas_call(
        functools.partial(fetch_kernel, chunk),
        out_shape=[pltpu.VMEM((2, features, chunk), BF16)] * early
        + [
            jax.ShapeDtypeStruct((8, 128), F32),
        ],
        in_specs=[HBM, HBM, ANY],
        out_specs=[VMEM] * (early + 1),
        scratch_shapes=[pltpu.SemaphoreType.DMA((early, 2))],
        compiler_params=pltpu.CompilerParams(vmem_limit_bytes=1 << 20),
        cost_estimate=pl.CostEstimate(
            flops=0, bytes_accessed=8 * early * features * chunk, transcendentals=0
        ),
        name="fetch",
    )(place(expert_gate, pltpu.HBM), place(expert_up, pltpu.HBM), after)


def fetch_rows_kernel(chunk, early, gate_hbm, up_hbm, after, *refs):
    outs, sems = refs[:-1], refs[-1]
    width = outs[0].shape[1]
    per_expert = gate_hbm.shape[2] // chunk
    inner = pl.ds(pl.multiple_of(lax.axis_index("head") * width, width), width)
    copies = []
    for i, out in enumerate(outs):
        step = early + i
        at = pl.ds((step % per_expert) * chunk, chunk)
        for j, source in enumerate((gate_hbm, up_hbm)):
            copies.append(
                pltpu.make_async_copy(
                    source.at[step // per_expert, inner, at], out.at[j], sems.at[i, j]
                )
            )
    for copy in copies:
        copy.start()
    for copy in copies:
        copy.wait()


def fetch_rows(expert_gate, expert_up, after, chunk, early, width):
    experts, _, hidden_units = expert_gate.shape
    late = experts * (hidden_units // chunk) - early
    if not late:
        return []
    return pl.pallas_call(
        functools.partial(fetch_rows_kernel, chunk, early),
        out_shape=[pltpu.VMEM((2, width, chunk), BF16)] * late,
        in_specs=[HBM, HBM, ANY],
        out_specs=[VMEM] * late,
        scratch_shapes=[pltpu.SemaphoreType.DMA((late, 2))],
        compiler_params=pltpu.CompilerParams(vmem_limit_bytes=1 << 20),
        cost_estimate=pl.CostEstimate(
            flops=0, bytes_accessed=8 * late * width * chunk, transcendentals=0
        ),
        name="fetch_rows",
    )(place(expert_gate, pltpu.HBM), place(expert_up, pltpu.HBM), after)


def expert_kernel(shape, *refs):
    tokens, group, places, pieces, experts, slots, chunk, depth, early, ready, flips, first, last = shape
    parts = len(places)
    columns = [
        sorted_back(refs[m * pieces : (m + 1) * pieces], STREAM_ORDER) for m in range(parts)
    ]
    refs = refs[parts * pieces :]
    if first:
        routing, gain, refs = refs[0], refs[1], refs[2:]
    else:
        gain, picks, factors, squares_in, sums_in = refs[:5]
        refs = refs[5:]
    fetched, refs = refs[:early], refs[early:]
    fetched_rows, refs = refs[:ready], refs[ready:]
    gate_hbm, up_hbm, refs = refs[0], refs[1], refs[2:]
    if last:
        hidden, refs = refs[0], refs[1:]
    if first:
        picks, factors, refs = refs[0], refs[1], refs[2:]
    squares, sums, chosen, buffers, sems, out_sems = refs
    flip = lax.axis_index("seq") if flips else 0
    head = lax.axis_index("head")
    width = gain.shape[2]
    features = width * gain.shape[0]
    per_expert = gate_hbm.shape[2] // chunk
    steps = experts * per_expert
    size = group * tokens
    height = group * slots
    at_head = [lax.bitwise_xor(head, m) for m in places]
    inner = [pl.ds(pl.multiple_of(p * width, width), width) for p in at_head]

    def copies(step, slot):
        e, at = step // per_expert, pl.ds((step % per_expert) * chunk, chunk)
        return [
            pltpu.make_async_copy(
                source.at[e, inner[p], at], buffers.at[slot, i, p], sems.at[slot, i, p]
            )
            for p in range(parts)
            for i, source in enumerate((gate_hbm, up_hbm))
        ]

    for slot in range(depth):
        for copy in copies(early + slot, slot):
            copy.start()

    groups = picks.shape[0]
    if first:
        slot_row = lax.broadcasted_iota(jnp.int32, (height, size), 0)
        token_col = lax.broadcasted_iota(jnp.int32, (height, size), 1)
        row_block = lax.div(slot_row, slots)
        row_rank = slot_row - row_block * slots
        col_block = lax.bitwise_xor(lax.div(token_col, tokens), flip)
        same_block = row_block == col_block
        before_row = lax.broadcasted_iota(jnp.int32, (size, size), 0)
        before_col = lax.broadcasted_iota(jnp.int32, (size, size), 1)
        before = (
            (before_row < before_col)
            & (lax.div(before_row, tokens) == lax.div(before_col, tokens))
        ).astype(BF16)
        ranks = lax.broadcasted_iota(jnp.int32, (8, size), 0)
        for g in range(groups):
            route = routing[:, g * size : (g + 1) * size].astype(F32)
            first_route, second_route, weight = route[0:1], route[1:2], route[2:3] / 256.0
            gate_rows = []
            for e in range(experts):
                expert = (head * experts + e).astype(F32)
                gate_rows.append(
                    jnp.where(first_route == expert, weight, 0.0)
                    + jnp.where(second_route == expert, 1.0 - weight, 0.0)
                )
            marked = jnp.zeros((8, size), F32)
            for e in range(experts):
                marked = jnp.where(ranks == e, (gate_rows[e] > 0).astype(F32), marked)
            counted = jnp.dot(marked.astype(BF16), before, preferred_element_type=F32)
            for e in range(experts):
                hit = (
                    same_block
                    & (counted[e : e + 1].astype(jnp.int32) == row_rank)
                    & (gate_rows[e] > 0)
                )
                picks[g, e * height : (e + 1) * height, :] = hit.astype(BF16)
                factors[e, g * height : (g + 1) * height, :] = jnp.sum(
                    jnp.where(hit, gate_rows[e], 0.0), axis=1, keepdims=True
                )
    for g in range(groups):
        total = None
        for p in range(parts):
            if pieces > 1:
                tokens_in = jnp.concatenate([ref[...] for ref in columns[p]], axis=0)
            else:
                tokens_in = columns[p][0][g * size : (g + 1) * size]
            rows = jnp.dot(picks[g], tokens_in, preferred_element_type=F32)
            part = jnp.sum(rows * rows, axis=1, keepdims=True)
            total = part if total is None else total + part
            rows = (rows * gain[at_head[p]].astype(F32)).astype(BF16)
            for e in range(experts):
                chosen[p, e, g * height : (g + 1) * height, :] = rows[
                    e * height : (e + 1) * height
                ]
        for e in range(experts):
            at = slice(g * height, (g + 1) * height)
            here = total[e * height : (e + 1) * height]
            if not first:
                here = here + squares_in[e, at, :]
            squares[e, at, :] = here

    def compute(step, gate_of, up_of):
        e, begin = step // per_expert, (step % per_expert) * chunk
        at = slice(begin, begin + chunk)
        gate_part = up_part = None
        for p in range(parts):
            rows = chosen[p, e]
            a = jnp.dot(rows, gate_of(p), preferred_element_type=F32)
            b = jnp.dot(rows, up_of(p), preferred_element_type=F32)
            gate_part = a if gate_part is None else gate_part + a
            up_part = b if up_part is None else up_part + b
        if not first:
            gate_part = gate_part + sums_in[0, e, :, at]
            up_part = up_part + sums_in[1, e, :, at]
        if not last:
            sums[0, e, :, at] = gate_part
            sums[1, e, :, at] = up_part
            return
        scale = lax.rsqrt(squares[e] / features + EPS)
        gate_part, up_part = gate_part * scale, up_part * scale
        result = factors[e] * (gate_part / (1.0 + jnp.exp(-gate_part)) * up_part)
        sums[e, :, at] = result.astype(BF16)
        store(step).start()

    def store(step):
        e, at = step // per_expert, pl.ds((step % per_expert) * chunk, chunk)
        return pltpu.make_async_copy(sums.at[e, :, at], hidden.at[e, :, at], out_sems.at[step])

    late = list(range(early + ready, steps))
    soon = len(late) - depth if late else 0
    order = [*range(early // 2), *late[:soon], *range(early // 2, early + ready), *late[soon:]]
    for step in order:
        if step < early:
            ref = fetched[step]
            compute(step, lambda p: ref[0, inner[p], :], lambda p: ref[1, inner[p], :])
            continue
        if step < early + ready:
            ref = fetched_rows[step - early]
            compute(step, lambda p: ref[0], lambda p: ref[1])
            continue
        slot = (step - early) % depth
        for copy in copies(step, slot):
            copy.wait()
        compute(
            step, lambda p: buffers[slot, 0, p], lambda p: buffers[slot, 1, p]
        )
        if step + depth < steps:
            for copy in copies(step + depth, slot):
                copy.start()
    if last:
        for step in range(steps):
            store(step).wait()


def run_experts(
    columns, places, gain, fetched, fetched_rows, matrices, tokens, count, carried, last
):
    first = len(carried) == 1
    parts, pieces = len(columns), len(columns[0])
    experts, features, hidden_units = matrices[0].shape
    width = gain.shape[2]
    early, chunk = len(fetched), fetched[0].shape[2]
    ready = len(fetched_rows)
    steps = experts * (hidden_units // chunk)
    depth = min(4, steps - early - ready)
    group = min(4, count)
    slots = MOST * count
    shape = (tokens, group, places, pieces, experts, MOST, chunk, depth, early, ready, pairwise(count), first, last)
    flat = [p for part in columns for p in shuffled(part, STREAM_ORDER)]
    routing, carried = (carried, []) if first else ([], carried)
    kept = [
        jax.ShapeDtypeStruct((count // group, experts * group * MOST, group * tokens), BF16),
        jax.ShapeDtypeStruct((experts, slots, 1), F32),
    ]
    passed = [
        jax.ShapeDtypeStruct((experts, slots, 1), F32),
        jax.ShapeDtypeStruct((2, experts, slots, hidden_units), F32),
    ]
    out_shape = [jax.ShapeDtypeStruct((experts, slots, hidden_units), BF16)] if last else []
    scratch = []
    for wanted, shapes in ((first, kept), (True, passed)):
        if wanted and last:
            scratch += [pltpu.VMEM(a.shape, a.dtype) for a in shapes]
        elif wanted:
            out_shape += shapes
    if last:
        scratch[-1] = pltpu.VMEM((experts, slots, hidden_units), BF16)
    small = count <= 4
    limit = (6 << 20) if small and not last else (10 << 20) if small else 44 << 20
    return pl.pallas_call(
        functools.partial(expert_kernel, shape),
        out_shape=out_shape,
        in_specs=[VMEM] * (len(flat) + len(routing) + 1 + len(carried) + early + ready)
        + [HBM, HBM],
        out_specs=[ANY] * last + [VMEM] * (len(out_shape) - last),
        scratch_shapes=scratch
        + [
            pltpu.VMEM((parts, experts, slots, width), BF16),
            pltpu.VMEM((max(depth, 1), 2, parts, width if depth else 16, chunk), BF16),
            pltpu.SemaphoreType.DMA((max(depth, 1), 2, parts)),
            pltpu.SemaphoreType.DMA((steps,)),
        ],
        compiler_params=pltpu.CompilerParams(vmem_limit_bytes=limit),
        cost_estimate=pl.CostEstimate(
            flops=4 * experts * slots * width * parts * hidden_units,
            bytes_accessed=2 * matrices[0].size,
            transcendentals=experts * slots * hidden_units,
        ),
        name="experts",
    )(
        *flat,
        *routing,
        gain,
        *carried,
        *[place(part, pltpu.VMEM) for part in (*fetched, *fetched_rows)],
        *[place(matrix, pltpu.HBM) for matrix in matrices],
    )


def local(
    queries,
    keys,
    values,
    residual_in,
    out_proj,
    norm_gain,
    expert_gate,
    expert_up,
    routes,
    gate_numer,
    sequence_lengths,
):
    tokens = queries.shape[1]
    count = lax.axis_size("seq")
    head_count = lax.axis_size("head")
    split = pairwise(count)
    share = residual_in.shape[2]
    features = out_proj.shape[2]
    heads, part, _ = out_proj.shape

    matrix = out_proj.reshape(heads * part, features)
    halves = 2 if lax.axis_size("dat") == 2 and matrix.shape[0] % 32 == 0 else 1
    own_kv, rows, own_routes, numer, *weights = prepare(
        matrix, queries[0], keys[0], values[0], routes[0].T, gate_numer, head_count, halves
    )

    weights = [swap(weights[m - 1], "head", m) for m in range(1, head_count)]

    kv_parts = spread(own_kv, "seq", upward=True)
    gain = norm_gain.reshape(head_count, 1, share)

    own_weights, gain, *attended = attend(
        sequence_lengths,
        matrix,
        rows,
        gain,
        own_routes,
        numer,
        kv_parts,
        weights if halves == 2 else [],
        count,
    )
    if halves == 2:
        carried, attended = attended[: head_count - 1], attended[head_count - 1 :]
        weights = [[got, swap(again, "dat", 1)] for got, again in zip(weights, carried)]
    else:
        weights = [[got] for got in weights]
    weights = [[own_weights]] + weights
    if split:
        attended = swaps(attended, "seq")
    else:
        shares = attended[0].reshape(tokens, heads, count, part).transpose(2, 0, 1, 3)
        shares = shares.reshape(count * tokens, heads * part)
        attended = [lax.all_to_all(shares, "seq", 0, 0, tiled=True)]
        routing = jnp.concatenate(
            [own_routes, numer, jnp.zeros((5, tokens), jnp.int32)], axis=0
        )
        routing = lax.all_gather(routing, "seq", axis=1, tiled=True)
    rows = [attended] + [
        [swap(piece, "head", m) for piece in attended] for m in range(1, head_count)
    ]
    sums = project(rows, weights, tokens if split else 0)
    if split:
        routing, *sums = sums
    chunk = min(256, expert_gate.shape[2])
    early = max(1, expert_gate.shape[0] * (expert_gate.shape[2] // chunk) * 11 // 16)
    *fetched, done = fetch(expert_gate, expert_up, sums[-1], chunk, early, share)
    if split:
        received = swaps(sums, "seq")[1:]
        mixed = sums[0]
        for part_sum in received:
            mixed = mixed + part_sum.astype(F32)
    else:
        mixed = lax.psum_scatter(sums[0], "seq", scatter_dimension=0, tiled=True)

    stream = (residual_in[0].astype(F32) + mixed + done[:1, :1]).astype(BF16)
    own_columns = spread(stream, "seq")
    columns = [own_columns] + [
        [swap(piece, "head", m) for piece in own_columns] for m in range(1, head_count)
    ]
    passes = [[0], list(range(1, head_count))] if head_count > 1 else [[0]]
    fetched_rows = fetch_rows(expert_gate, expert_up, stream, chunk, early, share)
    carried = [routing]
    for i, places in enumerate(passes):
        carried = run_experts(
            [columns[m] for m in places],
            tuple(places),
            gain,
            fetched,
            [] if i else fetched_rows,
            (expert_gate, expert_up),
            tokens,
            count,
            carried,
            i == len(passes) - 1,
        )
    hidden = carried[0]
    return (stream[None], hidden[:, None])


def solution(mesh):
    in_specs = (
        P(("grp", "dat"), "seq", "head"),
        P(("grp", "dat"), "seq", "head"),
        P(("grp", "dat"), "seq", "head"),
        P(("grp", "dat"), "seq", "head"),
        P("head", "seq", None),
        P(),
        P("head", None, "seq"),
        P("head", None, "seq"),
        P(("grp", "dat"), "seq", None),
        P(("grp", "dat"), "seq"),
        P(("grp", "dat")),
    )
    out_specs = (P(("grp", "dat"), "seq", "head"), P("head", ("grp", "dat"), None, "seq"))
    return jax.shard_map(local, mesh=mesh, in_specs=in_specs, out_specs=out_specs, check_vma=False)
```

time: 99 us -> 87.5 us (0.88)
  waiting for transfers between devices: 26.7 us -> 14.5 us
  local copies, waits for them, and re-layouts: 0.79 us -> 2.86 us
  Pallas kernels: 33.1 us -> 31.2 us
  starting transfers between devices: 36.8 us -> 35.7 us
    ppermute x22, waiting for transfers between devices: 26.7 us -> 14.5 us  [swap(): return lax.ppermute(array, axis, pairs)]
    unnamed x2 -> x8, local copies, waits for them, and re-layouts: 0.01 us -> 1.65 us
    ppermute x22, starting transfers between devices: 36.8 us -> 35.7 us  [swap(): return lax.ppermute(array, axis, pairs)]
    pallas_call x3 -> x4, Pallas kernels: 17.9 us -> 17.5 us  [the longest x2 12.9 us: run_experts(): pl.pallas_call(functools.partial(expert_kernel, shape), out_shape=out_sha...]
  transfers between devices with their start and end apart: 22 -> 22, of which waited for: 12 -> 9; matrix products, arithmetic and copies ran while one was open for 1% -> 1% of each run, Pallas kernels for 12% -> 23%
where the time goes in v3:
time: 87.5 us; the launch traced here: 86.6 us
  starting transfers between devices  35.7 us (41%)
  Pallas kernels  31.2 us (36%)
  waiting for transfers between devices  14.5 us (17%)
  local copies, waits for them, and re-layouts  2.86 us (3%)
  between operations  1.47 us (2%)
    ppermute x22, starting transfers between devices, swap(): return lax.ppermute(array, axis, pairs)  35.7 us
    ppermute x22, waiting for transfers between devices, swap(): return lax.ppermute(array, axis, pairs)  14.5 us
    pallas_call x2, Pallas kernels, run_experts(): pl.pallas_call(functools.partial(expert_kernel, shape), out_shape=out_sha...  12.9 us
    pallas_call x1, Pallas kernels, fetch(): pl.pallas_call(functools.partial(fetch_kernel, chunk), out_shape=[pltpu.V...  11.4 us
    pallas_call x1, Pallas kernels, fetch_rows(): pl.pallas_call(functools.partial(fetch_rows_kernel, chunk, early), out_sh...  3.44 us
  transfers between devices with their start and end apart: 22, of which 9 were waited for; matrix products, arithmetic and copies ran while one was open for 1% of the time, Pallas kernels for 23%

profile of v3, /device:TPU:0, one launch (start us, length us, event | category | flops | bytes accessed | tf_op | source)
XLA Modules:
  0.0 86.6 jit_solution(17417711929371004941)
XLA Ops:
  1.8 3.0 %collective-permute-start.3 = (bf16[192,1536]{1,0:T(8,128)(2,1)S(1)}, bf16[192,1536]{1,0:T(8,128)(2,1)S(1)}, u32[]{:S(2)}, u32[]{:S(2)}) collective-permute-start(bf16[192,1536]{1,0:T(8,128)(2,1)S(1)} %get-tuple-element.44), channel_id=1, source_target_pairs={{0,2},{2,0},{1,3},{3,1},{4,6},{6,4},{5,7},{7,5},{8,10},{10,8},{9,1... | collective-permute-start | bytes 1769480 | tf_op jit(solution)/shard_map/ppermute | solution.py:37
  4.8 3.5 %collective-permute-start = (bf16[64,512]{1,0:T(8,128)(2,1)S(1)}, bf16[64,512]{1,0:T(8,128)(2,1)S(1)}, u32[]{:S(2)}, u32[]{:S(2)}) collective-permute-start(bf16[64,512]{1,0:T(8,128)(2,1)S(1)} %get-tuple-element.43.refs_0_), channel_id=1, source_target_pairs={{0,4},{8,12},{1,5},{9,13},{2,6},{10,14},{3,7},{11,15},{16,20},{24,... | collective-permute-start | bytes 196616 | tf_op jit(solution)/shard_map/ppermute | solution.py:37
  8.3 4.5 %collective-permute-start.1 = (bf16[64,512]{1,0:T(8,128)(2,1)S(1)}, bf16[64,512]{1,0:T(8,128)(2,1)S(1)}, u32[]{:S(2)}, u32[]{:S(2)}) collective-permute-start(bf16[64,512]{1,0:T(8,128)(2,1)S(1)} %get-tuple-element.43.refs_0_), channel_id=1, source_target_pairs={{0,8},{4,12},{1,9},{5,13},{2,10},{6,14},{3,11},{7,15},{16,24},{20,... | collective-permute-start | bytes 196616 | tf_op jit(solution)/shard_map/ppermute | solution.py:37
  12.8 1.3 %collective-permute-start.2 = (bf16[64,512]{1,0:T(8,128)(2,1)S(1)}, bf16[64,512]{1,0:T(8,128)(2,1)S(1)}, u32[]{:S(2)}, u32[]{:S(2)}) collective-permute-start(bf16[64,512]{1,0:T(8,128)(2,1)S(1)} %get-tuple-element.43.refs_0_), channel_id=1, source_target_pairs={{0,12},{4,8},{1,13},{5,9},{2,14},{6,10},{3,15},{7,11},{16,28},{20,... | collective-permute-start | bytes 196616 | tf_op jit(solution)/shard_map/ppermute | solution.py:37
  16.0 2.2 %collective-permute-done.3.refs_4_.refs_9_ = bf16[192,1536]{1,0:T(8,128)(2,1)S(1)} collective-permute-done((bf16[192,1536]{1,0:T(8,128)(2,1)S(1)}, bf16[192,1536]{1,0:T(8,128)(2,1)S(1)}, u32[]{:S(2)}, u32[]{:S(2)}) %collective-permute-start.3) | collective-permute-done | bytes 589856 | tf_op jit(solution)/shard_map/ppermute | solution.py:37
  18.2 1.3 %attention.1 = (bf16[384,1536]{1,0:T(8,128)(2,1)S(1)}, bf16[2,1,1536]{2,1,0:T(2,128)(2,1)S(1)}, bf16[192,1536]{1,0:T(8,128)(2,1)S(1)}, bf16[80,384]{1,0:T(8,128)...) custom-call(s32[1]{0:T(128)S(6)} %copy.16.lengths, ...), custom_call_target="tpu_custom_call" | custom-call | flops 100663296 | bytes 917504 | tf_op jit(solution)/shard_map/attention/pallas_call | solution.py:157
  19.5 3.9 %collective-permute-start.6 = (bf16[80,384]{1,0:T(8,128)(2,1)S(1)}, bf16[80,384]{1,0:T(8,128)(2,1)S(1)}, u32[]{:S(2)}, u32[]{:S(2)}) collective-permute-start(bf16[80,384]{1,0:T(8,128)(2,1)S(1)} %get-tuple-element.48), channel_id=1, source_target_pairs={{0,12},{4,8},{8,4},{12,0},{1,13},{5,9},{9,5},{13,1},{2,14},{6,10},... | collective-permute-start | bytes 184328 | tf_op jit(solution)/shard_map/ppermute | solution.py:37
  24.1 1.6 %collective-permute-start.7 = (bf16[80,384]{1,0:T(8,128)(2,1)S(1)}, bf16[80,384]{1,0:T(8,128)(2,1)S(1)}, u32[]{:S(2)}, u32[]{:S(2)}) collective-permute-start(bf16[80,384]{1,0:T(8,128)(2,1)S(1)} %get-tuple-element.45.refs_0_), channel_id=1, source_target_pairs={{0,2},{2,0},{1,3},{3,1},{4,6},{6,4},{5,7},{7,5},{8,10},{10,8},{9,1... | collective-permute-start | bytes 184328 | tf_op jit(solution)/shard_map/ppermute | solution.py:37
  26.4 1.6 %collective-permute-start.10 = (bf16[80,384]{1,0:T(8,128)(2,1)S(1)}, bf16[80,384]{1,0:T(8,128)(2,1)S(1)}, u32[]{:S(2)}, u32[]{:S(2)}) collective-permute-start(bf16[80,384]{1,0:T(8,128)(2,1)S(1)} %collective-permute-done.6.refs_3_), channel_id=1, source_target_pairs={{0,2},{2,0},{1,3},{3,1},{4,6},{6,4},{5,7},{7,5},{8,10},{10,8},{9,1... | collective-permute-start | bytes 184328 | tf_op jit(solution)/shard_map/ppermute | solution.py:37
  28.8 1.5 %collective-permute-start.8 = (bf16[80,384]{1,0:T(8,128)(2,1)S(1)}, bf16[80,384]{1,0:T(8,128)(2,1)S(1)}, u32[]{:S(2)}, u32[]{:S(2)}) collective-permute-start(bf16[80,384]{1,0:T(8,128)(2,1)S(1)} %collective-permute-done.4.refs_1_), channel_id=1, source_target_pairs={{0,2},{2,0},{1,3},{3,1},{4,6},{6,4},{5,7},{7,5},{8,10},{10,8},{9,1... | collective-permute-start | bytes 184328 | tf_op jit(solution)/shard_map/ppermute | solution.py:37
  31.2 1.9 %collective-permute-done.8.refs_5_ = bf16[80,384]{1,0:T(8,128)(2,1)S(1)} collective-permute-done((bf16[80,384]{1,0:T(8,128)(2,1)S(1)}, bf16[80,384]{1,0:T(8,128)(2,1)S(1)}, u32[]{:S(2)}, u32[]{:S(2)}) %collective-permute-start.8) | collective-permute-done | bytes 61472 | tf_op jit(solution)/shard_map/ppermute | solution.py:37
  33.0 1.5 %collective-permute-done.9.refs_6_ = bf16[80,384]{1,0:T(8,128)(2,1)S(1)} collective-permute-done((bf16[80,384]{1,0:T(8,128)(2,1)S(1)}, bf16[80,384]{1,0:T(8,128)(2,1)S(1)}, u32[]{:S(2)}, u32[]{:S(2)}) %collective-permute-start.9) | collective-permute-done | bytes 61472 | tf_op jit(solution)/shard_map/ppermute | solution.py:37
  36.4 1.7 %collective-permute-start.13 = (bf16[64,1536]{1,0:T(8,128)(2,1)S(1)}, bf16[64,1536]{1,0:T(8,128)(2,1)S(1)}, u32[]{:S(2)}, u32[]{:S(2)}) collective-permute-start(bf16[64,1536]{1,0:T(8,128)(2,1)S(1)} %get-tuple-element.53), channel_id=1, source_target_pairs={{0,8},{4,12},{8,0},{12,4},{1,9},{5,13},{9,1},{13,5},{2,10},{6,14},... | collective-permute-start | bytes 589832 | tf_op jit(solution)/shard_map/ppermute | solution.py:37
  38.1 1.9 %collective-permute-start.14 = (bf16[64,1536]{1,0:T(8,128)(2,1)S(1)}, bf16[64,1536]{1,0:T(8,128)(2,1)S(1)}, u32[]{:S(2)}, u32[]{:S(2)}) collective-permute-start(bf16[64,1536]{1,0:T(8,128)(2,1)S(1)} %get-tuple-element.54.after), channel_id=1, source_target_pairs={{0,12},{4,8},{8,4},{12,0},{1,13},{5,9},{9,5},{13,1},{2,14},{6,10},... | collective-permute-start | bytes 589832 | tf_op jit(solution)/shard_map/ppermute | solution.py:37
  40.0 11.4 %fetch.1 = (bf16[2,3072,256]{2,1,0:T(8,128)(2,1)S(1)}, bf16[2,3072,256]{2,1,0:T(8,128)(2,1)S(1)}, bf16[2,3072,256]{2,1,0:T(8,128)(2,1)S(1)}, bf16[2,3072,256]{2,...) custom-call(bf16[2,3072,2048]{2,1,0:T(8,128)(2,1)} %refs_20_.1, ...), custom_call_target="tpu_custom_call" | custom-call | bytes 69206016 | tf_op jit(solution)/shard_map/fetch/pallas_call | solution.py:305
  51.5 1.6 %copy-done = bf16[2,3072,256]{2,1,0:T(8,128)(2,1)} copy-done((bf16[2,3072,256]{2,1,0:T(8,128)(2,1)}, bf16[2,3072,256]{2,1,0:T(8,128)(2,1)S(1)}, u32[]{:S(2)}) %copy-start) | copy-done | bytes 3145752
  54.5 2.0 %collective-permute-start.16 = (bf16[64,1536]{1,0:T(8,128)(2,1)S(1)}, bf16[64,1536]{1,0:T(8,128)(2,1)S(1)}, u32[]{:S(2)}, u32[]{:S(2)}) collective-permute-start(bf16[64,1536]{1,0:T(8,128)(2,1)S(1)} %fusion.1.after.refs_0_), channel_id=1, source_target_pairs={{0,12},{4,8},{8,4},{12,0},{1,13},{5,9},{9,5},{13,1},{2,14},{6,10},... | collective-permute-start | bytes 589832 | tf_op jit(solution)/shard_map/ppermute | solution.py:37
  57.3 1.6 %collective-permute-start.20 = (bf16[64,1536]{1,0:T(8,128)(2,1)S(1)}, bf16[64,1536]{1,0:T(8,128)(2,1)S(1)}, u32[]{:S(2)}, u32[]{:S(2)}) collective-permute-start(bf16[64,1536]{1,0:T(8,128)(2,1)S(1)} %fusion.1.after.refs_0_), channel_id=1, source_target_pairs={{0,8},{4,12},{8,0},{12,4},{1,9},{5,13},{9,1},{13,5},{2,10},{6,14},... | collective-permute-start | bytes 589832 | tf_op jit(solution)/shard_map/ppermute | solution.py:37
  58.9 3.4 %fetch_rows.1 = (bf16[2,1536,256]{2,1,0:T(8,128)(2,1)S(1)}, bf16[2,1536,256]{2,1,0:T(8,128)(2,1)S(1)}, bf16[2,1536,256]{2,1,0:T(8,128)(2,1)S(1)}, bf16[2,1536,25...) custom-call(bf16[2,3072,2048]{2,1,0:T(8,128)(2,1)} %refs_20_.1, bf16[2,3072,2048]{2,1,0:T(8,128)(2,1)} %refs_21_.1, ...), custom_call_target="tpu_custom_call" | custom-call | bytes 15728640 | tf_op jit(solution)/shard_map/fetch_rows/pallas_call | solution.py:348
  64.9 1.8 %collective-permute-start.19 = (bf16[64,1536]{1,0:T(8,128)(2,1)S(1)}, bf16[64,1536]{1,0:T(8,128)(2,1)S(1)}, u32[]{:S(2)}, u32[]{:S(2)}) collective-permute-start(bf16[64,1536]{1,0:T(8,128)(2,1)S(1)} %collective-permute-done.18.refs_2_), channel_id=1, source_target_pairs={{0,2},{2,0},{1,3},{3,1},{4,6},{6,4},{5,7},{7,5},{8,10},{10,8},{9,1... | collective-permute-start | bytes 589832 | tf_op jit(solution)/shard_map/ppermute | solution.py:37
  66.7 5.6 %collective-permute-done.20.refs_3_ = bf16[64,1536]{1,0:T(8,128)(2,1)S(1)} collective-permute-done((bf16[64,1536]{1,0:T(8,128)(2,1)S(1)}, bf16[64,1536]{1,0:T(8,128)(2,1)S(1)}, u32[]{:S(2)}, u32[]{:S(2)}) %collective-permute-start.20) | collective-permute-done | bytes 196640 | tf_op jit(solution)/shard_map/ppermute | solution.py:37
  72.3 1.4 %collective-permute-start.21 = (bf16[64,1536]{1,0:T(8,128)(2,1)S(1)}, bf16[64,1536]{1,0:T(8,128)(2,1)S(1)}, u32[]{:S(2)}, u32[]{:S(2)}) collective-permute-start(bf16[64,1536]{1,0:T(8,128)(2,1)S(1)} %collective-permute-done.20.refs_3_), channel_id=1, source_target_pairs={{0,2},{2,0},{1,3},{3,1},{4,6},{6,4},{5,7},{7,5},{8,10},{10,8},{9,1... | collective-permute-start | bytes 589832 | tf_op jit(solution)/shard_map/ppermute | solution.py:37
  73.7 4.9 %experts.2 = (bf16[1,320,256]{2,1,0:T(8,128)(2,1)S(1)}, f32[2,160,1]{2,1,0:T(8,128)S(1)}, f32[2,160,1]{2,1,0:T(8,128)S(1)}, f32[2,2,160,2048]{3,2,1,0:T(8,128)S(1)}) custom-call(bf16[64,1536]{1,0:T(8,128)(2,1)S(1)} %fusion.1.after.refs_0_, bf16[64,1536]{1,0:T(8,128)(2,1)S(1)} %collective-permute-done.16.refs_1_, ...), custom_call_target="tpu_custom_call" | custom-call | flops 4026531840 | bytes 25165824 | tf_op jit(solution)/shard_map/experts/pallas_call | solution.py:556
  78.6 7.9 %experts.3 = bf16[2,160,2048]{2,1,0:T(8,128)(2,1)} custom-call(bf16[64,1536]{1,0:T(8,128)(2,1)S(1)} %collective-permute-done.15.refs_0_, bf16[64,1536]{1,0:T(8,128)(2,1)S(1)} %collective-permute-done.17.refs_1_, bf16[64,1536]{1,0:T(8,128)(2,1)S(1)} %collective-permute-done.19.refs_2_, bf16[64,1536]{1,0:T(8,128)(2,1)S(1)} %collective-permute-done.21.refs_3_, ...), custom_call_target="tpu_custom_call" | custom-call | flops 4026531840 | bytes 25165824 | tf_op jit(solution)/shard_map/experts/pallas_call | solution.py:556
  (38 shorter events, 12.0 us)
Async XLA Ops:
  1.8 16.3 %collective-permute-start.3 = (bf16[192,1536]{1,0:T(8,128)(2,1)S(1)}, bf16[192,1536]{1,0:T(8,128)(2,1)S(1)}, u32[]{:S(2)}, u32[]{:S(2)}) collective-permute-start(bf16[192,1536]{1,0:T(8,128)(2,1)S(1)} %get-tuple-element.44), channel_id=1, source_target_pairs={{0,2},{2,0},{1,3},{3,1},{4,6},{6,4},{5,7},{7,5},{8,10},{10,8},{9,1... | collective-permute-start | bytes 1769480 | tf_op jit(solution)/shard_map/ppermute | solution.py:37
  4.8 10.6 %collective-permute-start = (bf16[64,512]{1,0:T(8,128)(2,1)S(1)}, bf16[64,512]{1,0:T(8,128)(2,1)S(1)}, u32[]{:S(2)}, u32[]{:S(2)}) collective-permute-start(bf16[64,512]{1,0:T(8,128)(2,1)S(1)} %get-tuple-element.43.refs_0_), channel_id=1, source_target_pairs={{0,4},{8,12},{1,5},{9,13},{2,6},{10,14},{3,7},{11,15},{16,20},{24,... | collective-permute-start | bytes 196616 | tf_op jit(solution)/shard_map/ppermute | solution.py:37
  8.3 7.2 %collective-permute-start.1 = (bf16[64,512]{1,0:T(8,128)(2,1)S(1)}, bf16[64,512]{1,0:T(8,128)(2,1)S(1)}, u32[]{:S(2)}, u32[]{:S(2)}) collective-permute-start(bf16[64,512]{1,0:T(8,128)(2,1)S(1)} %get-tuple-element.43.refs_0_), channel_id=1, source_target_pairs={{0,8},{4,12},{1,9},{5,13},{2,10},{6,14},{3,11},{7,15},{16,24},{20,... | collective-permute-start | bytes 196616 | tf_op jit(solution)/shard_map/ppermute | solution.py:37
  12.8 3.2 %collective-permute-start.2 = (bf16[64,512]{1,0:T(8,128)(2,1)S(1)}, bf16[64,512]{1,0:T(8,128)(2,1)S(1)}, u32[]{:S(2)}, u32[]{:S(2)}) collective-permute-start(bf16[64,512]{1,0:T(8,128)(2,1)S(1)} %get-tuple-element.43.refs_0_), channel_id=1, source_target_pairs={{0,12},{4,8},{1,13},{5,9},{2,14},{6,10},{3,15},{7,11},{16,28},{20,... | collective-permute-start | bytes 196616 | tf_op jit(solution)/shard_map/ppermute | solution.py:37
  19.5 15.1 %collective-permute-start.11 = (bf16[192,1536]{1,0:T(8,128)(2,1)S(1)}, bf16[192,1536]{1,0:T(8,128)(2,1)S(1)}, u32[]{:S(2)}, u32[]{:S(2)}) collective-permute-start(bf16[192,1536]{1,0:T(8,128)(2,1)S(1)} %get-tuple-element.50), channel_id=1, source_target_pairs={{0,1},{1,0},{2,3},{3,2},{4,5},{5,4},{6,7},{7,6},{8,9},{9,8},{10,11... | collective-permute-start | bytes 1769480 | tf_op jit(solution)/shard_map/ppermute | solution.py:37
  19.5 6.8 %collective-permute-start.6 = (bf16[80,384]{1,0:T(8,128)(2,1)S(1)}, bf16[80,384]{1,0:T(8,128)(2,1)S(1)}, u32[]{:S(2)}, u32[]{:S(2)}) collective-permute-start(bf16[80,384]{1,0:T(8,128)(2,1)S(1)} %get-tuple-element.48), channel_id=1, source_target_pairs={{0,12},{4,8},{8,4},{12,0},{1,13},{5,9},{9,5},{13,1},{2,14},{6,10},... | collective-permute-start | bytes 184328 | tf_op jit(solution)/shard_map/ppermute | solution.py:37
  23.5 5.4 %collective-permute-start.4 = (bf16[80,384]{1,0:T(8,128)(2,1)S(1)}, bf16[80,384]{1,0:T(8,128)(2,1)S(1)}, u32[]{:S(2)}, u32[]{:S(2)}) collective-permute-start(bf16[80,384]{1,0:T(8,128)(2,1)S(1)} %get-tuple-element.46), channel_id=1, source_target_pairs={{0,4},{4,0},{8,12},{12,8},{1,5},{5,1},{9,13},{13,9},{2,6},{6,2},{1... | collective-permute-start | bytes 184328 | tf_op jit(solution)/shard_map/ppermute | solution.py:37
  23.5 6.8 %collective-permute-start.5 = (bf16[80,384]{1,0:T(8,128)(2,1)S(1)}, bf16[80,384]{1,0:T(8,128)(2,1)S(1)}, u32[]{:S(2)}, u32[]{:S(2)}) collective-permute-start(bf16[80,384]{1,0:T(8,128)(2,1)S(1)} %get-tuple-element.47), channel_id=1, source_target_pairs={{0,8},{4,12},{8,0},{12,4},{1,9},{5,13},{9,1},{13,5},{2,10},{6,14},... | collective-permute-start | bytes 184328 | tf_op jit(solution)/shard_map/ppermute | solution.py:37
  24.1 6.7 %collective-permute-start.7 = (bf16[80,384]{1,0:T(8,128)(2,1)S(1)}, bf16[80,384]{1,0:T(8,128)(2,1)S(1)}, u32[]{:S(2)}, u32[]{:S(2)}) collective-permute-start(bf16[80,384]{1,0:T(8,128)(2,1)S(1)} %get-tuple-element.45.refs_0_), channel_id=1, source_target_pairs={{0,2},{2,0},{1,3},{3,1},{4,6},{6,4},{5,7},{7,5},{8,10},{10,8},{9,1... | collective-permute-start | bytes 184328 | tf_op jit(solution)/shard_map/ppermute | solution.py:37
  26.4 4.8 %collective-permute-start.10 = (bf16[80,384]{1,0:T(8,128)(2,1)S(1)}, bf16[80,384]{1,0:T(8,128)(2,1)S(1)}, u32[]{:S(2)}, u32[]{:S(2)}) collective-permute-start(bf16[80,384]{1,0:T(8,128)(2,1)S(1)} %collective-permute-done.6.refs_3_), channel_id=1, source_target_pairs={{0,2},{2,0},{1,3},{3,1},{4,6},{6,4},{5,7},{7,5},{8,10},{10,8},{9,1... | collective-permute-start | bytes 184328 | tf_op jit(solution)/shard_map/ppermute | solution.py:37
  28.8 4.2 %collective-permute-start.8 = (bf16[80,384]{1,0:T(8,128)(2,1)S(1)}, bf16[80,384]{1,0:T(8,128)(2,1)S(1)}, u32[]{:S(2)}, u32[]{:S(2)}) collective-permute-start(bf16[80,384]{1,0:T(8,128)(2,1)S(1)} %collective-permute-done.4.refs_1_), channel_id=1, source_target_pairs={{0,2},{2,0},{1,3},{3,1},{4,6},{6,4},{5,7},{7,5},{8,10},{10,8},{9,1... | collective-permute-start | bytes 184328 | tf_op jit(solution)/shard_map/ppermute | solution.py:37
  30.3 4.2 %collective-permute-start.9 = (bf16[80,384]{1,0:T(8,128)(2,1)S(1)}, bf16[80,384]{1,0:T(8,128)(2,1)S(1)}, u32[]{:S(2)}, u32[]{:S(2)}) collective-permute-start(bf16[80,384]{1,0:T(8,128)(2,1)S(1)} %collective-permute-done.5.refs_2_), channel_id=1, source_target_pairs={{0,2},{2,0},{1,3},{3,1},{4,6},{6,4},{5,7},{7,5},{8,10},{10,8},{9,1... | collective-permute-start | bytes 184328 | tf_op jit(solution)/shard_map/ppermute | solution.py:37
  35.6 18.1 %collective-permute-start.12 = (bf16[64,1536]{1,0:T(8,128)(2,1)S(1)}, bf16[64,1536]{1,0:T(8,128)(2,1)S(1)}, u32[]{:S(2)}, u32[]{:S(2)}) collective-permute-start(bf16[64,1536]{1,0:T(8,128)(2,1)S(1)} %get-tuple-element.52), channel_id=1, source_target_pairs={{0,4},{4,0},{8,12},{12,8},{1,5},{5,1},{9,13},{13,9},{2,6},{6,2},{1... | collective-permute-start | bytes 589832 | tf_op jit(solution)/shard_map/ppermute | solution.py:37
  36.4 17.2 %collective-permute-start.13 = (bf16[64,1536]{1,0:T(8,128)(2,1)S(1)}, bf16[64,1536]{1,0:T(8,128)(2,1)S(1)}, u32[]{:S(2)}, u32[]{:S(2)}) collective-permute-start(bf16[64,1536]{1,0:T(8,128)(2,1)S(1)} %get-tuple-element.53), channel_id=1, source_target_pairs={{0,8},{4,12},{8,0},{12,4},{1,9},{5,13},{9,1},{13,5},{2,10},{6,14},... | collective-permute-start | bytes 589832 | tf_op jit(solution)/shard_map/ppermute | solution.py:37
  38.1 15.5 %collective-permute-start.14 = (bf16[64,1536]{1,0:T(8,128)(2,1)S(1)}, bf16[64,1536]{1,0:T(8,128)(2,1)S(1)}, u32[]{:S(2)}, u32[]{:S(2)}) collective-permute-start(bf16[64,1536]{1,0:T(8,128)(2,1)S(1)} %get-tuple-element.54.after), channel_id=1, source_target_pairs={{0,12},{4,8},{8,4},{12,0},{1,13},{5,9},{9,5},{13,1},{2,14},{6,10},... | collective-permute-start | bytes 589832 | tf_op jit(solution)/shard_map/ppermute | solution.py:37
  54.4 19.2 %copy-start.2 = (bf16[64,1536]{1,0:T(8,128)(2,1)}, bf16[64,1536]{1,0:T(8,128)(2,1)S(1)}, u32[]{:S(2)}) copy-start(bf16[64,1536]{1,0:T(8,128)(2,1)S(1)} %fusion.1.after.refs_0_) | copy-start | bytes 589828
  54.4 19.2 %copy-start.1 = (bf16[2,3072,256]{2,1,0:T(8,128)(2,1)S(1)}, bf16[2,3072,256]{2,1,0:T(8,128)(2,1)}, u32[]{:S(2)}) copy-start(bf16[2,3072,256]{2,1,0:T(8,128)(2,1)} %copy-done) | copy-start | bytes 9437188
  54.5 9.6 %collective-permute-start.16 = (bf16[64,1536]{1,0:T(8,128)(2,1)S(1)}, bf16[64,1536]{1,0:T(8,128)(2,1)S(1)}, u32[]{:S(2)}, u32[]{:S(2)}) collective-permute-start(bf16[64,1536]{1,0:T(8,128)(2,1)S(1)} %fusion.1.after.refs_0_), channel_id=1, source_target_pairs={{0,12},{4,8},{8,4},{12,0},{1,13},{5,9},{9,5},{13,1},{2,14},{6,10},... | collective-permute-start | bytes 589832 | tf_op jit(solution)/shard_map/ppermute | solution.py:37
  56.4 8.5 %collective-permute-start.18 = (bf16[64,1536]{1,0:T(8,128)(2,1)S(1)}, bf16[64,1536]{1,0:T(8,128)(2,1)S(1)}, u32[]{:S(2)}, u32[]{:S(2)}) collective-permute-start(bf16[64,1536]{1,0:T(8,128)(2,1)S(1)} %fusion.1.after.refs_0_), channel_id=1, source_target_pairs={{0,4},{4,0},{8,12},{12,8},{1,5},{5,1},{9,13},{13,9},{2,6},{6,2},{1... | collective-permute-start | bytes 589832 | tf_op jit(solution)/shard_map/ppermute | solution.py:37
  57.3 15.0 %collective-permute-start.20 = (bf16[64,1536]{1,0:T(8,128)(2,1)S(1)}, bf16[64,1536]{1,0:T(8,128)(2,1)S(1)}, u32[]{:S(2)}, u32[]{:S(2)}) collective-permute-start(bf16[64,1536]{1,0:T(8,128)(2,1)S(1)} %fusion.1.after.refs_0_), channel_id=1, source_target_pairs={{0,8},{4,12},{8,0},{12,4},{1,9},{5,13},{9,1},{13,5},{2,10},{6,14},... | collective-permute-start | bytes 589832 | tf_op jit(solution)/shard_map/ppermute | solution.py:37
  62.3 16.3 %collective-permute-start.15 = (bf16[64,1536]{1,0:T(8,128)(2,1)S(1)}, bf16[64,1536]{1,0:T(8,128)(2,1)S(1)}, u32[]{:S(2)}, u32[]{:S(2)}) collective-permute-start(bf16[64,1536]{1,0:T(8,128)(2,1)S(1)} %fusion.1.after.refs_0_), channel_id=1, source_target_pairs={{0,2},{2,0},{1,3},{3,1},{4,6},{6,4},{5,7},{7,5},{8,10},{10,8},{9,1... | collective-permute-start | bytes 589832 | tf_op jit(solution)/shard_map/ppermute | solution.py:37
  64.1 14.5 %collective-permute-start.17 = (bf16[64,1536]{1,0:T(8,128)(2,1)S(1)}, bf16[64,1536]{1,0:T(8,128)(2,1)S(1)}, u32[]{:S(2)}, u32[]{:S(2)}) collective-permute-start(bf16[64,1536]{1,0:T(8,128)(2,1)S(1)} %collective-permute-done.16.refs_1_), channel_id=1, source_target_pairs={{0,2},{2,0},{1,3},{3,1},{4,6},{6,4},{5,7},{7,5},{8,10},{10,8},{9,1... | collective-permute-start | bytes 589832 | tf_op jit(solution)/shard_map/ppermute | solution.py:37
  64.9 13.7 %collective-permute-start.19 = (bf16[64,1536]{1,0:T(8,128)(2,1)S(1)}, bf16[64,1536]{1,0:T(8,128)(2,1)S(1)}, u32[]{:S(2)}, u32[]{:S(2)}) collective-permute-start(bf16[64,1536]{1,0:T(8,128)(2,1)S(1)} %collective-permute-done.18.refs_2_), channel_id=1, source_target_pairs={{0,2},{2,0},{1,3},{3,1},{4,6},{6,4},{5,7},{7,5},{8,10},{10,8},{9,1... | collective-permute-start | bytes 589832 | tf_op jit(solution)/shard_map/ppermute | solution.py:37
  72.3 6.3 %collective-permute-start.21 = (bf16[64,1536]{1,0:T(8,128)(2,1)S(1)}, bf16[64,1536]{1,0:T(8,128)(2,1)S(1)}, u32[]{:S(2)}, u32[]{:S(2)}) collective-permute-start(bf16[64,1536]{1,0:T(8,128)(2,1)S(1)} %collective-permute-done.20.refs_3_), channel_id=1, source_target_pairs={{0,2},{2,0},{1,3},{3,1},{4,6},{6,4},{5,7},{7,5},{8,10},{10,8},{9,1... | collective-permute-start | bytes 589832 | tf_op jit(solution)/shard_map/ppermute | solution.py:37
  (2 other events, 17.2 us)

commit v4 on v3

--- a/solution.py
+++ b/solution.py
@@ -13,7 +13,7 @@
 KEY_VALUE_HEADS = 4
 MOST = 40
 EXTRA = 16
-ATTENDED_ORDER = (0, 1, 2, 3)
+ATTENDED_ORDER = (0, 3, 2, 1)
 STREAM_ORDER = (0, 3, 1, 2)
 EPS = 1e-05
 NEG = -1e30
@@ -62,19 +62,14 @@
 
 
 def attention_kernel(shape, lengths, matrix, queries, gain_in, routes, numer, *refs):
-    tokens, groups, per_group, pieces, carried, split = shape
+    tokens, groups, per_group, pieces, split = shape
     kv_refs, refs = refs[:pieces], refs[pieces:]
-    carried_in, refs = refs[:carried], refs[carried:]
-    own, gain_out, refs = refs[0], refs[1], refs[2:]
-    carried_out, refs = refs[:carried], refs[carried:]
-    outs, sems = refs[:-1], refs[-1]
+    own, gain_out, outs, sem = refs[0], refs[1], refs[2:-1], refs[-1]
     rank = lax.axis_index("seq")
     share = own.shape[1]
     lanes = pl.ds(pl.multiple_of(lax.axis_index("head") * share, share), share)
-    pairs = [(matrix.at[:, lanes], own), *zip(carried_in, carried_out)]
-    copies = [pltpu.make_async_copy(*pair, sems.at[i]) for i, pair in enumerate(pairs)]
-    for copy in copies:
-        copy.start()
+    copy = pltpu.make_async_copy(matrix.at[:, lanes], own, sem)
+    copy.start()
     gain_out[...] = gain_in[...]
     flip, valid_len = rank if split else 0, lengths[0]
     width = groups * HEAD_SIZE
@@ -112,8 +107,7 @@
         attended += [mixed[a * tokens : (a + 1) * tokens] for a in range(per_group)]
     if not split:
         outs[0][...] = jnp.concatenate(attended, axis=1).astype(BF16)
-        for copy in copies:
-            copy.wait()
+        copy.wait()
         return
     count = len(outs)
     part = HEAD_SIZE // count
@@ -132,11 +126,10 @@
         outs[k][:tokens, :] = chosen
         outs[k][tokens:, :] = jnp.zeros((EXTRA, chosen.shape[1]), BF16)
         outs[k][tokens:, :tokens] = routing
-    for copy in copies:
-        copy.wait()
-
-
-def attend(lengths, matrix, queries, gain, routes, numer, kv_parts, carried, count):
+    copy.wait()
+
+
+def attend(lengths, matrix, queries, gain, routes, numer, kv_parts, count):
     tokens = queries.shape[0]
     groups = kv_parts[0].shape[1] // (2 * HEAD_SIZE)
     per_group = QUERY_HEAD_COUNT // KEY_VALUE_HEADS
@@ -152,16 +145,16 @@
     limit = min(40 << 20, (4 << 20) + 48 * per_group * tokens * length)
     out_shape = [
         jax.ShapeDtypeStruct((matrix.shape[0], gain.shape[2]), BF16),
-        *[jax.ShapeDtypeStruct(array.shape, BF16) for array in (gain, *carried)],
+        jax.ShapeDtypeStruct(gain.shape, BF16),
     ] + out_shape
     return pl.pallas_call(
         functools.partial(
-            attention_kernel, (tokens, groups, per_group, len(kv_parts), len(carried), split)
+            attention_kernel, (tokens, groups, per_group, len(kv_parts), split)
         ),
         out_shape=out_shape,
-        in_specs=[SMEM, HBM] + [VMEM] * (4 + len(kv_parts)) + [ANY] * len(carried),
+        in_specs=[SMEM, HBM] + [VMEM] * (4 + len(kv_parts)),
         out_specs=[VMEM] * len(out_shape),
-        scratch_shapes=[pltpu.SemaphoreType.DMA((1 + len(carried),))],
+        scratch_shapes=[pltpu.SemaphoreType.DMA],
         compiler_params=pltpu.CompilerParams(vmem_limit_bytes=limit),
         cost_estimate=pl.CostEstimate(
             flops=4 * tokens * length * queries.shape[1],
@@ -169,7 +162,7 @@
             transcendentals=tokens * length * groups * per_group,
         ),
         name="attention",
-    )(lengths, place(matrix, pltpu.HBM), queries, gain, routes, numer, *kv_parts, *carried)
+    )(lengths, place(matrix, pltpu.HBM), queries, gain, routes, numer, *kv_parts)
 
 
 def prepare_kernel(matrix, queries, keys, values, routes, numer, *refs):
@@ -225,63 +218,88 @@
     )(*[place(source, pltpu.HBM) for source in sources])
 
 
-def project_kernel(parts, pieces, tokens, halves, *refs):
-    rows = [sorted_back(refs[m * pieces : (m + 1) * pieces], ATTENDED_ORDER) for m in range(parts)]
-    refs = refs[parts * pieces :]
+def pack_kernel(tokens, pieces, *refs):
+    parts, refs = sorted_back(refs[:pieces], ATTENDED_ORDER), refs[pieces:]
+    carried = (len(refs) - 3) // 2
+    carried_in, packed, route, refs = refs[:carried], refs[carried], refs[carried + 1], refs[carried + 2 :]
+    copies = [
+        pltpu.make_async_copy(source, out, refs[-1].at[i])
+        for i, (source, out) in enumerate(zip(carried_in, refs[:-1]))
+    ]
+    for copy in copies:
+        copy.start()
+    for k, ref in enumerate(parts):
+        at = slice(k * tokens, (k + 1) * tokens)
+        packed[at, :] = ref[:tokens, :]
+        route[:, at] = ref[tokens : tokens + 8, :tokens]
+    for copy in copies:
+        copy.wait()
+
+
+def pack(parts, tokens, carried):
+    width = parts[0].shape[1]
+    rows = tokens * len(parts)
+    out_shape = [
+        jax.ShapeDtypeStruct((rows, width), BF16),
+        jax.ShapeDtypeStruct((8, rows), BF16),
+        *[jax.ShapeDtypeStruct(array.shape, array.dtype) for array in carried],
+    ]
+    return pl.pallas_call(
+        functools.partial(pack_kernel, tokens, len(parts)),
+        out_shape=out_shape,
+        in_specs=[VMEM] * len(parts) + [ANY] * len(carried),
+        out_specs=[VMEM] * len(out_shape),
+        scratch_shapes=[pltpu.SemaphoreType.DMA((max(1, len(carried)),))],
+        compiler_params=pltpu.CompilerParams(vmem_limit_bytes=6 << 20),
+        name="pack",
+    )(*shuffled(parts, ATTENDED_ORDER), *carried)
+
+
+def project_kernel(parts, halves, *refs):
+    rows, refs = refs[:parts], refs[parts:]
     weights = [refs[:1]] + [refs[1 + m * halves : 1 + (m + 1) * halves] for m in range(parts - 1)]
-    refs = refs[1 + (parts - 1) * halves :]
-    outs = refs
-    if tokens:
-        route, outs = outs[0], outs[1:]
-        route[...] = jnp.concatenate([ref[tokens : tokens + 8, :tokens] for ref in rows[0]], axis=1)
+    outs = refs[1 + (parts - 1) * halves :]
+    core = lax.axis_index("dat")
     total = None
-    core = lax.axis_index("dat")
     for m in range(parts):
-        stacked = jnp.concatenate([ref[: tokens or ref.shape[0]] for ref in rows[m]], axis=0)
-        if len(weights[m]) == 1:
-            factors = [stacked]
-        else:
-            half = stacked.shape[1] // 2
-            low, high = stacked[:, :half], stacked[:, half:]
+        factors = [rows[m][...]]
+        if len(weights[m]) > 1:
+            half = rows[m].shape[1] // 2
+            low, high = factors[0][:, :half], factors[0][:, half:]
             factors = [jnp.where(core == 0, low, high), jnp.where(core == 0, high, low)]
         for factor, weight in zip(factors, weights[m]):
             product = jnp.dot(factor, weight[...], preferred_element_type=F32)
             total = product if total is None else total + product
     at = 0
-    for i, out in enumerate(outs):
+    for out in outs:
         out[...] = total[at : at + out.shape[0]].astype(out.dtype)
         at += out.shape[0]
 
 
-def project(rows, weights, each):
-    parts, pieces = len(rows), len(rows[0])
-    depth, width = weights[0][0].shape
+def project(rows, weights, pieces):
+    parts, (tokens, depth), width = len(rows), rows[0].shape, weights[0][0].shape[1]
     flat_weights = [w for part in weights for w in part]
-    heights = [each or p.shape[0] for p in rows[0]]
-    tokens = sum(heights)
-    out_shape = [
-        jax.ShapeDtypeStruct((h, width), BF16 if each and i else F32)
-        for i, h in enumerate(heights)
-    ]
-    if each:
-        out_shape = [jax.ShapeDtypeStruct((8, tokens), BF16)] + out_shape
-    flat = [p for part in rows for p in shuffled(part, ATTENDED_ORDER)]
     return pl.pallas_call(
-        functools.partial(project_kernel, parts, pieces, each, len(weights[-1])),
-        out_shape=out_shape,
-        in_specs=[VMEM] * (len(flat) + len(flat_weights)),
-        out_specs=[VMEM] * len(out_shape),
-        compiler_params=pltpu.CompilerParams(vmem_limit_bytes=min(40 << 20, (4 << 20) + 16 * tokens * width)),
+        functools.partial(project_kernel, parts, len(weights[-1])),
+        out_shape=[
+            jax.ShapeDtypeStruct((tokens // pieces, width), BF16 if i else F32)
+            for i in range(pieces)
+        ],
+        in_specs=[VMEM] * (parts + len(flat_weights)),
+        out_specs=[VMEM] * pieces,
+        compiler_params=pltpu.CompilerParams(
+            vmem_limit_bytes=min(40 << 20, (4 << 20) + 16 * tokens * width)
+        ),
         cost_estimate=pl.CostEstimate(
             flops=2 * tokens * width * parts * depth,
             bytes_accessed=2 * parts * depth * width + 4 * tokens * width,
             transcendentals=0,
         ),
         name="projection",
-    )(*flat, *flat_weights)
-
-
-def fetch_kernel(chunk, gate_hbm, up_hbm, after, *refs):
+    )(*rows, *flat_weights)
+
+
+def fetch_kernel(chunk, gate_hbm, up_hbm, kept, *refs):
     outs, done, sems = refs[:-2], refs[-2], refs[-1]
     per_expert = gate_hbm.shape[2] // chunk
     copies = []
@@ -295,28 +313,28 @@
             )
     for copy in copies:
         copy.start()
-    done[...] = jnp.zeros_like(done)
+    done[...] = kept[...]
     for copy in copies:
         copy.wait()
 
 
-def fetch(expert_gate, expert_up, after, chunk, early, mark):
+def fetch(expert_gate, expert_up, kept, chunk, early):
     features = expert_gate.shape[1]
     return pl.pallas_call(
         functools.partial(fetch_kernel, chunk),
         out_shape=[pltpu.VMEM((2, features, chunk), BF16)] * early
         + [
-            jax.ShapeDtypeStruct((8, 128), F32),
+            jax.ShapeDtypeStruct(kept.shape, F32),
         ],
-        in_specs=[HBM, HBM, ANY],
+        in_specs=[HBM, HBM, VMEM],
         out_specs=[VMEM] * (early + 1),
         scratch_shapes=[pltpu.SemaphoreType.DMA((early, 2))],
-        compiler_params=pltpu.CompilerParams(vmem_limit_bytes=1 << 20),
+        compiler_params=pltpu.CompilerParams(vmem_limit_bytes=4 << 20 if kept.size < 1 << 20 else 40 << 20),
         cost_estimate=pl.CostEstimate(
             flops=0, bytes_accessed=8 * early * features * chunk, transcendentals=0
         ),
         name="fetch",
-    )(place(expert_gate, pltpu.HBM), place(expert_up, pltpu.HBM), after)
+    )(place(expert_gate, pltpu.HBM), place(expert_up, pltpu.HBM), kept)
 
 
 def fetch_rows_kernel(chunk, early, gate_hbm, up_hbm, after, *refs):
@@ -476,11 +494,11 @@
             gate_part = a if gate_part is None else gate_part + a
             up_part = b if up_part is None else up_part + b
         if not first:
-            gate_part = gate_part + sums_in[0, e, :, at]
-            up_part = up_part + sums_in[1, e, :, at]
+            gate_part = gate_part + sums_in[0, e, :, at].astype(F32)
+            up_part = up_part + sums_in[1, e, :, at].astype(F32)
         if not last:
-            sums[0, e, :, at] = gate_part
-            sums[1, e, :, at] = up_part
+            sums[0, e, :, at] = gate_part.astype(BF16)
+            sums[1, e, :, at] = up_part.astype(BF16)
             return
         scale = lax.rsqrt(squares[e] / features + EPS)
         gate_part, up_part = gate_part * scale, up_part * scale
@@ -528,7 +546,7 @@
     early, chunk = len(fetched), fetched[0].shape[2]
     ready = len(fetched_rows)
     steps = experts * (hidden_units // chunk)
-    depth = min(4, steps - early - ready)
+    depth = min(3, steps - early - ready)
     group = min(4, count)
     slots = MOST * count
     shape = (tokens, group, places, pieces, experts, MOST, chunk, depth, early, ready, pairwise(count), first, last)
@@ -540,7 +558,7 @@
     ]
     passed = [
         jax.ShapeDtypeStruct((experts, slots, 1), F32),
-        jax.ShapeDtypeStruct((2, experts, slots, hidden_units), F32),
+        jax.ShapeDtypeStruct((2, experts, slots, hidden_units), BF16),
     ]
     out_shape = [jax.ShapeDtypeStruct((experts, slots, hidden_units), BF16)] if last else []
     scratch = []
@@ -552,7 +570,7 @@
     if last:
         scratch[-1] = pltpu.VMEM((experts, slots, hidden_units), BF16)
     small = count <= 4
-    limit = (6 << 20) if small and not last else (10 << 20) if small else 44 << 20
+    limit = (6 << 20) if small and not last else (9 << 20) if small else 44 << 20
     return pl.pallas_call(
         functools.partial(expert_kernel, shape),
         out_shape=out_shape,
@@ -612,54 +630,41 @@
 
     weights = [swap(weights[m - 1], "head", m) for m in range(1, head_count)]
 
-    kv_parts = spread(own_kv, "seq", upward=True)
+    kv_parts = spread(own_kv, "seq")
     gain = norm_gain.reshape(head_count, 1, share)
 
     own_weights, gain, *attended = attend(
-        sequence_lengths,
-        matrix,
-        rows,
-        gain,
-        own_routes,
-        numer,
-        kv_parts,
-        weights if halves == 2 else [],
-        count,
+        sequence_lengths, matrix, rows, gain, own_routes, numer, kv_parts, count
     )
-    if halves == 2:
-        carried, attended = attended[: head_count - 1], attended[head_count - 1 :]
-        weights = [[got, swap(again, "dat", 1)] for got, again in zip(weights, carried)]
-    else:
-        weights = [[got] for got in weights]
-    weights = [[own_weights]] + weights
     if split:
         attended = swaps(attended, "seq")
+        mine, routing, *carried = pack(attended, tokens, weights if halves == 2 else [])
     else:
         shares = attended[0].reshape(tokens, heads, count, part).transpose(2, 0, 1, 3)
         shares = shares.reshape(count * tokens, heads * part)
-        attended = [lax.all_to_all(shares, "seq", 0, 0, tiled=True)]
+        mine = lax.all_to_all(shares, "seq", 0, 0, tiled=True)
         routing = jnp.concatenate(
             [own_routes, numer, jnp.zeros((5, tokens), jnp.int32)], axis=0
         )
         routing = lax.all_gather(routing, "seq", axis=1, tiled=True)
-    rows = [attended] + [
-        [swap(piece, "head", m) for piece in attended] for m in range(1, head_count)
-    ]
-    sums = project(rows, weights, tokens if split else 0)
-    if split:
-        routing, *sums = sums
+        carried = weights
+    if halves == 2:
+        weights = [[got, swap(again, "dat", 1)] for got, again in zip(weights, carried)]
+    else:
+        weights = [[got] for got in weights]
+    rows = [mine] + [swap(mine, "head", m) for m in range(1, head_count)]
+    sums = project(rows, [[own_weights]] + weights, count if split else 1)
     chunk = min(256, expert_gate.shape[2])
-    early = max(1, expert_gate.shape[0] * (expert_gate.shape[2] // chunk) * 11 // 16)
-    *fetched, done = fetch(expert_gate, expert_up, sums[-1], chunk, early, share)
+    early = max(1, expert_gate.shape[0] * (expert_gate.shape[2] // chunk) * 12 // 16)
+    *fetched, mixed = fetch(expert_gate, expert_up, sums[0], chunk, early)
     if split:
         received = swaps(sums, "seq")[1:]
-        mixed = sums[0]
         for part_sum in received:
             mixed = mixed + part_sum.astype(F32)
     else:
-        mixed = lax.psum_scatter(sums[0], "seq", scatter_dimension=0, tiled=True)
-
-    stream = (residual_in[0].astype(F32) + mixed + done[:1, :1]).astype(BF16)
+        mixed = lax.psum_scatter(mixed, "seq", scatter_dimension=0, tiled=True)
+
+    stream = (residual_in[0].astype(F32) + mixed).astype(BF16)
     own_columns = spread(stream, "seq")
     columns = [own_columns] + [
         [swap(piece, "head", m) for piece in own_columns] for m in range(1, head_count)

time: 87.5 us -> 84.8 us (0.969)
  starting transfers between devices: 35.7 us -> 26.5 us
  waiting for transfers between devices: 14.5 us -> 23.3 us
  local copies, waits for them, and re-layouts: 2.86 us -> 0.71 us
  Pallas kernels: 31.2 us -> 32.6 us
    ppermute x22 -> x19, starting transfers between devices: 35.7 us -> 26.5 us  [swap(): return lax.ppermute(array, axis, pairs)]
    ppermute x22 -> x19, waiting for transfers between devices: 14.5 us -> 23.3 us  [swap(): return lax.ppermute(array, axis, pairs)]
    unnamed x8 -> x4, local copies, waits for them, and re-layouts: 1.65 us -> 0.01 us
    pallas_call x1, Pallas kernels: 11.4 us -> 12.4 us  [fetch(): pl.pallas_call(functools.partial(fetch_kernel, chunk), out_shape=[pltpu.V...]
  transfers between devices with their start and end apart: 22 -> 19, of which waited for: 9 -> 9; matrix products, arithmetic and copies ran while one was open for 1% -> 1% of each run, Pallas kernels for 23% -> 26%
where the time goes in v4:
time: 84.8 us; the launch traced here: 84.6 us
  Pallas kernels  32.6 us (38%)
  starting transfers between devices  26.5 us (31%)
  waiting for transfers between devices  23.3 us (27%)
  between operations  1.41 us (2%)
    ppermute x19, starting transfers between devices, swap(): return lax.ppermute(array, axis, pairs)  26.5 us
    ppermute x19, waiting for transfers between devices, swap(): return lax.ppermute(array, axis, pairs)  23.3 us
    pallas_call x2, Pallas kernels, run_experts(): pl.pallas_call(functools.partial(expert_kernel, shape), out_shape=out_sha...  12.7 us
    pallas_call x1, Pallas kernels, fetch(): pl.pallas_call(functools.partial(fetch_kernel, chunk), out_shape=[pltpu.V...  12.4 us
    pallas_call x1, Pallas kernels, fetch_rows(): pl.pallas_call(functools.partial(fetch_rows_kernel, chunk, early), out_sh...  2.94 us
    pallas_call x1, Pallas kernels, attend(): pl.pallas_call(functools.partial(attention_kernel, (tokens, groups, per_g...  2.12 us
  transfers between devices with their start and end apart: 19, of which 9 were waited for; matrix products, arithmetic and copies ran while one was open for 1% of the time, Pallas kernels for 26%

profile of v4, /device:TPU:0, one launch (start us, length us, event | category | flops | bytes accessed | tf_op | source)
XLA Modules:
  0.0 84.6 jit_solution(15989423094151973110)
XLA Ops:
  0.6 1.2 %prepare.1 = (bf16[64,512]{1,0:T(8,128)(2,1)S(1)}, bf16[64,1536]{1,0:T(8,128)(2,1)S(1)}, s32[2,64]{1,0:T(2,128)S(1)}, s32[1,64]{1,0:T(1,128)S(1)}, bf16[192,1536]{1,0:T(8,128)(2,1)S(1)}) custom-call(bf16[384,3072]{1,0:T(8,128)(2,1)} %bitcast.15, bf16[64,1536]{1,0:T(8,128)(2,1)} %bitcast.18, bf16[64,256]{1,0:T(8,128)(2,1)} %bitcast.19, ...), custom_call_target="tpu_custom_call" | custom-call | bytes 4718592 | tf_op jit(solution)/shard_map/prepare/pallas_call | solution.py:207
  1.8 3.0 %collective-permute-start.6 = (bf16[192,1536]{1,0:T(8,128)(2,1)S(1)}, bf16[192,1536]{1,0:T(8,128)(2,1)S(1)}, u32[]{:S(2)}, u32[]{:S(2)}) collective-permute-start(bf16[192,1536]{1,0:T(8,128)(2,1)S(1)} %get-tuple-element.49), channel_id=1, source_target_pairs={{0,2},{2,0},{1,3},{3,1},{4,6},{6,4},{5,7},{7,5},{8,10},{10,8},{9,1... | collective-permute-start | bytes 1769480 | tf_op jit(solution)/shard_map/ppermute | solution.py:37
  4.8 1.6 %collective-permute-start = (bf16[64,512]{1,0:T(8,128)(2,1)S(1)}, bf16[64,512]{1,0:T(8,128)(2,1)S(1)}, u32[]{:S(2)}, u32[]{:S(2)}) collective-permute-start(bf16[64,512]{1,0:T(8,128)(2,1)S(1)} %get-tuple-element.44.refs_0_), channel_id=1, source_target_pairs={{0,4},{4,0},{8,12},{12,8},{1,5},{5,1},{9,13},{13,9},{2,6},{6,2},{1... | collective-permute-start | bytes 196616 | tf_op jit(solution)/shard_map/ppermute | solution.py:37
  6.4 2.6 %collective-permute-start.1 = (bf16[64,512]{1,0:T(8,128)(2,1)S(1)}, bf16[64,512]{1,0:T(8,128)(2,1)S(1)}, u32[]{:S(2)}, u32[]{:S(2)}) collective-permute-start(bf16[64,512]{1,0:T(8,128)(2,1)S(1)} %get-tuple-element.44.refs_0_), channel_id=1, source_target_pairs={{0,8},{4,12},{8,0},{12,4},{1,9},{5,13},{9,1},{13,5},{2,10},{6,14},... | collective-permute-start | bytes 196616 | tf_op jit(solution)/shard_map/ppermute | solution.py:37
  10.6 2.8 %collective-permute-done.1.refs_2_ = bf16[64,512]{1,0:T(8,128)(2,1)S(1)} collective-permute-done((bf16[64,512]{1,0:T(8,128)(2,1)S(1)}, bf16[64,512]{1,0:T(8,128)(2,1)S(1)}, u32[]{:S(2)}, u32[]{:S(2)}) %collective-permute-start.1) | collective-permute-done | bytes 65568 | tf_op jit(solution)/shard_map/ppermute | solution.py:37
  13.4 1.7 %collective-permute-done.2.refs_3_ = bf16[64,512]{1,0:T(8,128)(2,1)S(1)} collective-permute-done((bf16[64,512]{1,0:T(8,128)(2,1)S(1)}, bf16[64,512]{1,0:T(8,128)(2,1)S(1)}, u32[]{:S(2)}, u32[]{:S(2)}) %collective-permute-start.2) | collective-permute-done | bytes 65568 | tf_op jit(solution)/shard_map/ppermute | solution.py:37
  15.1 2.1 %attention.1 = (bf16[384,1536]{1,0:T(8,128)(2,1)S(1)}, bf16[2,1,1536]{2,1,0:T(2,128)(2,1)S(1)}, bf16[80,384]{1,0:T(8,128)(2,1)S(1)}, bf16[80,384]{1,0:T(8,128)(2...) custom-call(s32[1]{0:T(128)S(6)} %copy.16.lengths, bf16[384,3072]{1,0:T(8,128)(2,1)} %bitcast.16, ...), custom_call_target="tpu_custom_call" | custom-call | flops 100663296 | bytes 917504 | tf_op jit(solution)/shard_map/attention/pallas_call | solution.py:150
  17.2 1.6 %collective-permute-start.3 = (bf16[80,384]{1,0:T(8,128)(2,1)S(1)}, bf16[80,384]{1,0:T(8,128)(2,1)S(1)}, u32[]{:S(2)}, u32[]{:S(2)}) collective-permute-start(bf16[80,384]{1,0:T(8,128)(2,1)S(1)} %get-tuple-element.46), channel_id=1, source_target_pairs={{0,12},{4,8},{8,4},{12,0},{1,13},{5,9},{9,5},{13,1},{2,14},{6,10},... | collective-permute-start | bytes 184328 | tf_op jit(solution)/shard_map/ppermute | solution.py:37
  18.8 2.9 %collective-permute-start.5 = (bf16[80,384]{1,0:T(8,128)(2,1)S(1)}, bf16[80,384]{1,0:T(8,128)(2,1)S(1)}, u32[]{:S(2)}, u32[]{:S(2)}) collective-permute-start(bf16[80,384]{1,0:T(8,128)(2,1)S(1)} %get-tuple-element.48), channel_id=1, source_target_pairs={{0,4},{4,0},{8,12},{12,8},{1,5},{5,1},{9,13},{13,9},{2,6},{6,2},{1... | collective-permute-start | bytes 184328 | tf_op jit(solution)/shard_map/ppermute | solution.py:37
  21.7 1.6 %collective-permute-done.3.refs_1_ = bf16[80,384]{1,0:T(8,128)(2,1)S(1)} collective-permute-done((bf16[80,384]{1,0:T(8,128)(2,1)S(1)}, bf16[80,384]{1,0:T(8,128)(2,1)S(1)}, u32[]{:S(2)}, u32[]{:S(2)}) %collective-permute-start.3) | collective-permute-done | bytes 61472 | tf_op jit(solution)/shard_map/ppermute | solution.py:37
  23.3 1.3 %collective-permute-done.4.refs_2_ = bf16[80,384]{1,0:T(8,128)(2,1)S(1)} collective-permute-done((bf16[80,384]{1,0:T(8,128)(2,1)S(1)}, bf16[80,384]{1,0:T(8,128)(2,1)S(1)}, u32[]{:S(2)}, u32[]{:S(2)}) %collective-permute-start.4) | collective-permute-done | bytes 61472 | tf_op jit(solution)/shard_map/ppermute | solution.py:37
  25.5 6.7 %collective-permute-done.7.refs_1_ = bf16[256,384]{1,0:T(8,128)(2,1)S(1)} collective-permute-done((bf16[256,384]{1,0:T(8,128)(2,1)S(1)}, bf16[256,384]{1,0:T(8,128)(2,1)S(1)}, u32[]{:S(2)}, u32[]{:S(2)}) %collective-permute-start.7) | collective-permute-done | bytes 196640 | tf_op jit(solution)/shard_map/ppermute | solution.py:37
  33.3 1.4 %collective-permute-start.10 = (bf16[64,1536]{1,0:T(8,128)(2,1)S(1)}, bf16[64,1536]{1,0:T(8,128)(2,1)S(1)}, u32[]{:S(2)}, u32[]{:S(2)}) collective-permute-start(bf16[64,1536]{1,0:T(8,128)(2,1)S(1)} %get-tuple-element.56), channel_id=1, source_target_pairs={{0,8},{4,12},{8,0},{12,4},{1,9},{5,13},{9,1},{13,5},{2,10},{6,14},... | collective-permute-start | bytes 589832 | tf_op jit(solution)/shard_map/ppermute | solution.py:37
  34.6 2.3 %collective-permute-start.11 = (bf16[64,1536]{1,0:T(8,128)(2,1)S(1)}, bf16[64,1536]{1,0:T(8,128)(2,1)S(1)}, u32[]{:S(2)}, u32[]{:S(2)}) collective-permute-start(bf16[64,1536]{1,0:T(8,128)(2,1)S(1)} %get-tuple-element.57), channel_id=1, source_target_pairs={{0,12},{4,8},{8,4},{12,0},{1,13},{5,9},{9,5},{13,1},{2,14},{6,10},... | collective-permute-start | bytes 589832 | tf_op jit(solution)/shard_map/ppermute | solution.py:37
  37.0 12.4 %fetch.1 = (bf16[2,3072,256]{2,1,0:T(8,128)(2,1)S(1)}, bf16[2,3072,256]{2,1,0:T(8,128)(2,1)S(1)}, bf16[2,3072,256]{2,1,0:T(8,128)(2,1)S(1)}, bf16[2,3072,256]{2,...) custom-call(bf16[2,3072,2048]{2,1,0:T(8,128)(2,1)} %refs_21_.1, ...), custom_call_target="tpu_custom_call" | custom-call | bytes 75497472 | tf_op jit(solution)/shard_map/fetch/pallas_call | solution.py:323
  50.6 1.8 %collective-permute-start.13 = (bf16[64,1536]{1,0:T(8,128)(2,1)S(1)}, bf16[64,1536]{1,0:T(8,128)(2,1)S(1)}, u32[]{:S(2)}, u32[]{:S(2)}) collective-permute-start(bf16[64,1536]{1,0:T(8,128)(2,1)S(1)} %fusion.after.refs_0_), channel_id=1, source_target_pairs={{0,12},{4,8},{8,4},{12,0},{1,13},{5,9},{9,5},{13,1},{2,14},{6,10},... | collective-permute-start | bytes 589832 | tf_op jit(solution)/shard_map/ppermute | solution.py:37
  52.5 3.9 %collective-permute-start.15 = (bf16[64,1536]{1,0:T(8,128)(2,1)S(1)}, bf16[64,1536]{1,0:T(8,128)(2,1)S(1)}, u32[]{:S(2)}, u32[]{:S(2)}) collective-permute-start(bf16[64,1536]{1,0:T(8,128)(2,1)S(1)} %fusion.after.refs_0_), channel_id=1, source_target_pairs={{0,4},{4,0},{8,12},{12,8},{1,5},{5,1},{9,13},{13,9},{2,6},{6,2},{1... | collective-permute-start | bytes 589832 | tf_op jit(solution)/shard_map/ppermute | solution.py:37
  56.3 1.4 %collective-permute-start.17 = (bf16[64,1536]{1,0:T(8,128)(2,1)S(1)}, bf16[64,1536]{1,0:T(8,128)(2,1)S(1)}, u32[]{:S(2)}, u32[]{:S(2)}) collective-permute-start(bf16[64,1536]{1,0:T(8,128)(2,1)S(1)} %fusion.after.refs_0_), channel_id=1, source_target_pairs={{0,8},{4,12},{8,0},{12,4},{1,9},{5,13},{9,1},{13,5},{2,10},{6,14},... | collective-permute-start | bytes 589832 | tf_op jit(solution)/shard_map/ppermute | solution.py:37
  57.7 2.9 %fetch_rows.1 = (bf16[2,1536,256]{2,1,0:T(8,128)(2,1)S(1)}, bf16[2,1536,256]{2,1,0:T(8,128)(2,1)S(1)}, bf16[2,1536,256]{2,1,0:T(8,128)(2,1)S(1)}, bf16[2,1536,256]{2,1,0:T(8,128)(2,1)S(1)}) custom-call(bf16[2,3072,2048]{2,1,0:T(8,128)(2,1)} %refs_21_.1, bf16[2,3072,2048]{2,1,0:T(8,128)(2,1)} %refs_22_.3, bf16[64,1536]{1,0:T(8,128)(2,1)S(1)} %fusion.after.refs_0_), custom_call_target="tpu_custom_call" | custom-call | bytes 12582912 | tf_op jit(solution)/shard_map/fetch_rows/pallas_call | solution.py:366
  61.3 1.5 %collective-permute-start.14 = (bf16[64,1536]{1,0:T(8,128)(2,1)S(1)}, bf16[64,1536]{1,0:T(8,128)(2,1)S(1)}, u32[]{:S(2)}, u32[]{:S(2)}) collective-permute-start(bf16[64,1536]{1,0:T(8,128)(2,1)S(1)} %collective-permute-done.13.refs_1_), channel_id=1, source_target_pairs={{0,2},{2,0},{1,3},{3,1},{4,6},{6,4},{5,7},{7,5},{8,10},{10,8},{9,1... | collective-permute-start | bytes 589832 | tf_op jit(solution)/shard_map/ppermute | solution.py:37
  63.3 6.9 %collective-permute-done.17.refs_3_ = bf16[64,1536]{1,0:T(8,128)(2,1)S(1)} collective-permute-done((bf16[64,1536]{1,0:T(8,128)(2,1)S(1)}, bf16[64,1536]{1,0:T(8,128)(2,1)S(1)}, u32[]{:S(2)}, u32[]{:S(2)}) %collective-permute-start.17) | collective-permute-done | bytes 196640 | tf_op jit(solution)/shard_map/ppermute | solution.py:37
  70.8 4.9 %experts.2 = (bf16[1,320,256]{2,1,0:T(8,128)(2,1)S(1)}, f32[2,160,1]{2,1,0:T(8,128)S(1)}, f32[2,160,1]{2,1,0:T(8,128)S(1)}, bf16[2,2,160,2048]{3,2,1,0:T(8,128)(2,1)S(1)}) custom-call(bf16[64,1536]{1,0:T(8,128)(2,1)S(1)} %fusion.after.refs_0_, bf16[64,1536]{1,0:T(8,128)(2,1)S(1)} %collective-permute-done.13.refs_1_, ...), custom_call_target="tpu_custom_call" | custom-call | flops 4026531840 | bytes 25165824 | tf_op jit(solution)/shard_map/experts/pallas_call | solution.py:574
  75.7 1.1 %collective-permute-done.18.refs_3_ = bf16[64,1536]{1,0:T(8,128)(2,1)S(1)} collective-permute-done((bf16[64,1536]{1,0:T(8,128)(2,1)S(1)}, bf16[64,1536]{1,0:T(8,128)(2,1)S(1)}, u32[]{:S(2)}, u32[]{:S(2)}) %collective-permute-start.18) | collective-permute-done | bytes 196640 | tf_op jit(solution)/shard_map/ppermute | solution.py:37
  76.8 7.8 %experts.3 = bf16[2,160,2048]{2,1,0:T(8,128)(2,1)} custom-call(bf16[64,1536]{1,0:T(8,128)(2,1)S(1)} %collective-permute-done.12.refs_0_, bf16[64,1536]{1,0:T(8,128)(2,1)S(1)} %collective-permute-done.14.refs_1_, bf16[64,1536]{1,0:T(8,128)(2,1)S(1)} %collective-permute-done.16.refs_2_, bf16[64,1536]{1,0:T(8,128)(2,1)S(1)} %collective-permute-done.18.refs_3_, ...), custom_call_target="tpu_custom_call" | custom-call | flops 4026531840 | bytes 25165824 | tf_op jit(solution)/shard_map/experts/pallas_call | solution.py:574
  (28 shorter events, 5.7 us)
Async XLA Ops:
  1.8 22.8 %collective-permute-start.6 = (bf16[192,1536]{1,0:T(8,128)(2,1)S(1)}, bf16[192,1536]{1,0:T(8,128)(2,1)S(1)}, u32[]{:S(2)}, u32[]{:S(2)}) collective-permute-start(bf16[192,1536]{1,0:T(8,128)(2,1)S(1)} %get-tuple-element.49), channel_id=1, source_target_pairs={{0,2},{2,0},{1,3},{3,1},{4,6},{6,4},{5,7},{7,5},{8,10},{10,8},{9,1... | collective-permute-start | bytes 1769480 | tf_op jit(solution)/shard_map/ppermute | solution.py:37
  4.8 5.7 %collective-permute-start = (bf16[64,512]{1,0:T(8,128)(2,1)S(1)}, bf16[64,512]{1,0:T(8,128)(2,1)S(1)}, u32[]{:S(2)}, u32[]{:S(2)}) collective-permute-start(bf16[64,512]{1,0:T(8,128)(2,1)S(1)} %get-tuple-element.44.refs_0_), channel_id=1, source_target_pairs={{0,4},{4,0},{8,12},{12,8},{1,5},{5,1},{9,13},{13,9},{2,6},{6,2},{1... | collective-permute-start | bytes 196616 | tf_op jit(solution)/shard_map/ppermute | solution.py:37
  6.4 7.0 %collective-permute-start.1 = (bf16[64,512]{1,0:T(8,128)(2,1)S(1)}, bf16[64,512]{1,0:T(8,128)(2,1)S(1)}, u32[]{:S(2)}, u32[]{:S(2)}) collective-permute-start(bf16[64,512]{1,0:T(8,128)(2,1)S(1)} %get-tuple-element.44.refs_0_), channel_id=1, source_target_pairs={{0,8},{4,12},{8,0},{12,4},{1,9},{5,13},{9,1},{13,5},{2,10},{6,14},... | collective-permute-start | bytes 196616 | tf_op jit(solution)/shard_map/ppermute | solution.py:37
  9.0 6.1 %collective-permute-start.2 = (bf16[64,512]{1,0:T(8,128)(2,1)S(1)}, bf16[64,512]{1,0:T(8,128)(2,1)S(1)}, u32[]{:S(2)}, u32[]{:S(2)}) collective-permute-start(bf16[64,512]{1,0:T(8,128)(2,1)S(1)} %get-tuple-element.44.refs_0_), channel_id=1, source_target_pairs={{0,12},{4,8},{8,4},{12,0},{1,13},{5,9},{9,5},{13,1},{2,14},{6,10},... | collective-permute-start | bytes 196616 | tf_op jit(solution)/shard_map/ppermute | solution.py:37
  17.2 6.1 %collective-permute-start.3 = (bf16[80,384]{1,0:T(8,128)(2,1)S(1)}, bf16[80,384]{1,0:T(8,128)(2,1)S(1)}, u32[]{:S(2)}, u32[]{:S(2)}) collective-permute-start(bf16[80,384]{1,0:T(8,128)(2,1)S(1)} %get-tuple-element.46), channel_id=1, source_target_pairs={{0,12},{4,8},{8,4},{12,0},{1,13},{5,9},{9,5},{13,1},{2,14},{6,10},... | collective-permute-start | bytes 184328 | tf_op jit(solution)/shard_map/ppermute | solution.py:37
  18.8 5.8 %collective-permute-start.4 = (bf16[80,384]{1,0:T(8,128)(2,1)S(1)}, bf16[80,384]{1,0:T(8,128)(2,1)S(1)}, u32[]{:S(2)}, u32[]{:S(2)}) collective-permute-start(bf16[80,384]{1,0:T(8,128)(2,1)S(1)} %get-tuple-element.47), channel_id=1, source_target_pairs={{0,8},{4,12},{8,0},{12,4},{1,9},{5,13},{9,1},{13,5},{2,10},{6,14},... | collective-permute-start | bytes 184328 | tf_op jit(solution)/shard_map/ppermute | solution.py:37
  18.8 5.8 %collective-permute-start.5 = (bf16[80,384]{1,0:T(8,128)(2,1)S(1)}, bf16[80,384]{1,0:T(8,128)(2,1)S(1)}, u32[]{:S(2)}, u32[]{:S(2)}) collective-permute-start(bf16[80,384]{1,0:T(8,128)(2,1)S(1)} %get-tuple-element.48), channel_id=1, source_target_pairs={{0,4},{4,0},{8,12},{12,8},{1,5},{5,1},{9,13},{13,9},{2,6},{6,2},{1... | collective-permute-start | bytes 184328 | tf_op jit(solution)/shard_map/ppermute | solution.py:37
  24.8 7.4 %collective-permute-start.8 = (bf16[192,1536]{1,0:T(8,128)(2,1)S(1)}, bf16[192,1536]{1,0:T(8,128)(2,1)S(1)}, u32[]{:S(2)}, u32[]{:S(2)}) collective-permute-start(bf16[192,1536]{1,0:T(8,128)(2,1)S(1)} %get-tuple-element.52), channel_id=1, source_target_pairs={{0,1},{1,0},{2,3},{3,2},{4,5},{5,4},{6,7},{7,6},{8,9},{9,8},{10,11... | collective-permute-start | bytes 1769480 | tf_op jit(solution)/shard_map/ppermute | solution.py:37
  24.9 7.3 %collective-permute-start.7 = (bf16[256,384]{1,0:T(8,128)(2,1)S(1)}, bf16[256,384]{1,0:T(8,128)(2,1)S(1)}, u32[]{:S(2)}, u32[]{:S(2)}) collective-permute-start(bf16[256,384]{1,0:T(8,128)(2,1)S(1)} %get-tuple-element.50.refs_0_), channel_id=1, source_target_pairs={{0,2},{2,0},{1,3},{3,1},{4,6},{6,4},{5,7},{7,5},{8,10},{10,8},{9,1... | collective-permute-start | bytes 589832 | tf_op jit(solution)/shard_map/ppermute | solution.py:37
  33.3 16.7 %collective-permute-start.10 = (bf16[64,1536]{1,0:T(8,128)(2,1)S(1)}, bf16[64,1536]{1,0:T(8,128)(2,1)S(1)}, u32[]{:S(2)}, u32[]{:S(2)}) collective-permute-start(bf16[64,1536]{1,0:T(8,128)(2,1)S(1)} %get-tuple-element.56), channel_id=1, source_target_pairs={{0,8},{4,12},{8,0},{12,4},{1,9},{5,13},{9,1},{13,5},{2,10},{6,14},... | collective-permute-start | bytes 589832 | tf_op jit(solution)/shard_map/ppermute | solution.py:37
  34.6 15.4 %collective-permute-start.11 = (bf16[64,1536]{1,0:T(8,128)(2,1)S(1)}, bf16[64,1536]{1,0:T(8,128)(2,1)S(1)}, u32[]{:S(2)}, u32[]{:S(2)}) collective-permute-start(bf16[64,1536]{1,0:T(8,128)(2,1)S(1)} %get-tuple-element.57), channel_id=1, source_target_pairs={{0,12},{4,8},{8,4},{12,0},{1,13},{5,9},{9,5},{13,1},{2,14},{6,10},... | collective-permute-start | bytes 589832 | tf_op jit(solution)/shard_map/ppermute | solution.py:37
  37.0 13.5 %collective-permute-start.9 = (bf16[64,1536]{1,0:T(8,128)(2,1)S(1)}, bf16[64,1536]{1,0:T(8,128)(2,1)S(1)}, u32[]{:S(2)}, u32[]{:S(2)}) collective-permute-start(bf16[64,1536]{1,0:T(8,128)(2,1)S(1)} %get-tuple-element.55), channel_id=1, source_target_pairs={{0,4},{4,0},{8,12},{12,8},{1,5},{5,1},{9,13},{13,9},{2,6},{6,2},{1... | collective-permute-start | bytes 589832 | tf_op jit(solution)/shard_map/ppermute | solution.py:37
  37.0 13.5 %copy-start.1 = (bf16[1,64,1536]{2,1,0:T(8,128)(2,1)S(1)}, bf16[1,64,1536]{2,1,0:T(8,128)(2,1)}, u32[]{:S(2)}) copy-start(bf16[1,64,1536]{2,1,0:T(8,128)(2,1)} %param.14) | copy-start | bytes 589828
  50.6 20.2 %copy-start = (bf16[64,1536]{1,0:T(8,128)(2,1)}, bf16[64,1536]{1,0:T(8,128)(2,1)S(1)}, u32[]{:S(2)}) copy-start(bf16[64,1536]{1,0:T(8,128)(2,1)S(1)} %fusion.after.refs_0_) | copy-start | bytes 589828
  50.6 10.6 %collective-permute-start.13 = (bf16[64,1536]{1,0:T(8,128)(2,1)S(1)}, bf16[64,1536]{1,0:T(8,128)(2,1)S(1)}, u32[]{:S(2)}, u32[]{:S(2)}) collective-permute-start(bf16[64,1536]{1,0:T(8,128)(2,1)S(1)} %fusion.after.refs_0_), channel_id=1, source_target_pairs={{0,12},{4,8},{8,4},{12,0},{1,13},{5,9},{9,5},{13,1},{2,14},{6,10},... | collective-permute-start | bytes 589832 | tf_op jit(solution)/shard_map/ppermute | solution.py:37
  52.5 10.3 %collective-permute-start.15 = (bf16[64,1536]{1,0:T(8,128)(2,1)S(1)}, bf16[64,1536]{1,0:T(8,128)(2,1)S(1)}, u32[]{:S(2)}, u32[]{:S(2)}) collective-permute-start(bf16[64,1536]{1,0:T(8,128)(2,1)S(1)} %fusion.after.refs_0_), channel_id=1, source_target_pairs={{0,4},{4,0},{8,12},{12,8},{1,5},{5,1},{9,13},{13,9},{2,6},{6,2},{1... | collective-permute-start | bytes 589832 | tf_op jit(solution)/shard_map/ppermute | solution.py:37
  56.3 13.9 %collective-permute-start.17 = (bf16[64,1536]{1,0:T(8,128)(2,1)S(1)}, bf16[64,1536]{1,0:T(8,128)(2,1)S(1)}, u32[]{:S(2)}, u32[]{:S(2)}) collective-permute-start(bf16[64,1536]{1,0:T(8,128)(2,1)S(1)} %fusion.after.refs_0_), channel_id=1, source_target_pairs={{0,8},{4,12},{8,0},{12,4},{1,9},{5,13},{9,1},{13,5},{2,10},{6,14},... | collective-permute-start | bytes 589832 | tf_op jit(solution)/shard_map/ppermute | solution.py:37
  60.7 15.0 %collective-permute-start.12 = (bf16[64,1536]{1,0:T(8,128)(2,1)S(1)}, bf16[64,1536]{1,0:T(8,128)(2,1)S(1)}, u32[]{:S(2)}, u32[]{:S(2)}) collective-permute-start(bf16[64,1536]{1,0:T(8,128)(2,1)S(1)} %fusion.after.refs_0_), channel_id=1, source_target_pairs={{0,2},{2,0},{1,3},{3,1},{4,6},{6,4},{5,7},{7,5},{8,10},{10,8},{9,1... | collective-permute-start | bytes 589832 | tf_op jit(solution)/shard_map/ppermute | solution.py:37
  61.3 14.4 %collective-permute-start.14 = (bf16[64,1536]{1,0:T(8,128)(2,1)S(1)}, bf16[64,1536]{1,0:T(8,128)(2,1)S(1)}, u32[]{:S(2)}, u32[]{:S(2)}) collective-permute-start(bf16[64,1536]{1,0:T(8,128)(2,1)S(1)} %collective-permute-done.13.refs_1_), channel_id=1, source_target_pairs={{0,2},{2,0},{1,3},{3,1},{4,6},{6,4},{5,7},{7,5},{8,10},{10,8},{9,1... | collective-permute-start | bytes 589832 | tf_op jit(solution)/shard_map/ppermute | solution.py:37
  62.8 12.9 %collective-permute-start.16 = (bf16[64,1536]{1,0:T(8,128)(2,1)S(1)}, bf16[64,1536]{1,0:T(8,128)(2,1)S(1)}, u32[]{:S(2)}, u32[]{:S(2)}) collective-permute-start(bf16[64,1536]{1,0:T(8,128)(2,1)S(1)} %collective-permute-done.15.refs_2_), channel_id=1, source_target_pairs={{0,2},{2,0},{1,3},{3,1},{4,6},{6,4},{5,7},{7,5},{8,10},{10,8},{9,1... | collective-permute-start | bytes 589832 | tf_op jit(solution)/shard_map/ppermute | solution.py:37
  70.2 6.5 %collective-permute-start.18 = (bf16[64,1536]{1,0:T(8,128)(2,1)S(1)}, bf16[64,1536]{1,0:T(8,128)(2,1)S(1)}, u32[]{:S(2)}, u32[]{:S(2)}) collective-permute-start(bf16[64,1536]{1,0:T(8,128)(2,1)S(1)} %collective-permute-done.17.refs_3_), channel_id=1, source_target_pairs={{0,2},{2,0},{1,3},{3,1},{4,6},{6,4},{5,7},{7,5},{8,10},{10,8},{9,1... | collective-permute-start | bytes 589832 | tf_op jit(solution)/shard_map/ppermute | solution.py:37

commit v5 on v4

--- a/solution.py
+++ b/solution.py
@@ -61,15 +61,11 @@
     return [lax.all_gather(array, axis, axis=0, tiled=True)]
 
 
-def attention_kernel(shape, lengths, matrix, queries, gain_in, routes, numer, *refs):
+def attention_kernel(shape, lengths, queries, gain_in, routes, numer, *refs):
     tokens, groups, per_group, pieces, split = shape
     kv_refs, refs = refs[:pieces], refs[pieces:]
-    own, gain_out, outs, sem = refs[0], refs[1], refs[2:-1], refs[-1]
+    gain_out, outs = refs[0], refs[1:]
     rank = lax.axis_index("seq")
-    share = own.shape[1]
-    lanes = pl.ds(pl.multiple_of(lax.axis_index("head") * share, share), share)
-    copy = pltpu.make_async_copy(matrix.at[:, lanes], own, sem)
-    copy.start()
     gain_out[...] = gain_in[...]
     flip, valid_len = rank if split else 0, lengths[0]
     width = groups * HEAD_SIZE
@@ -107,7 +103,6 @@
         attended += [mixed[a * tokens : (a + 1) * tokens] for a in range(per_group)]
     if not split:
         outs[0][...] = jnp.concatenate(attended, axis=1).astype(BF16)
-        copy.wait()
         return
     count = len(outs)
     part = HEAD_SIZE // count
@@ -126,10 +121,9 @@
         outs[k][:tokens, :] = chosen
         outs[k][tokens:, :] = jnp.zeros((EXTRA, chosen.shape[1]), BF16)
         outs[k][tokens:, :tokens] = routing
-    copy.wait()
-
-
-def attend(lengths, matrix, queries, gain, routes, numer, kv_parts, count):
+
+
+def attend(lengths, queries, gain, routes, numer, kv_parts, count):
     tokens = queries.shape[0]
     groups = kv_parts[0].shape[1] // (2 * HEAD_SIZE)
     per_group = QUERY_HEAD_COUNT // KEY_VALUE_HEADS
@@ -144,7 +138,6 @@
     length = tokens * count
     limit = min(40 << 20, (4 << 20) + 48 * per_group * tokens * length)
     out_shape = [
-        jax.ShapeDtypeStruct((matrix.shape[0], gain.shape[2]), BF16),
         jax.ShapeDtypeStruct(gain.shape, BF16),
     ] + out_shape
     return pl.pallas_call(
@@ -152,9 +145,8 @@
             attention_kernel, (tokens, groups, per_group, len(kv_parts), split)
         ),
         out_shape=out_shape,
-        in_specs=[SMEM, HBM] + [VMEM] * (4 + len(kv_parts)),
+        in_specs=[SMEM] + [VMEM] * (4 + len(kv_parts)),
         out_specs=[VMEM] * len(out_shape),
-        scratch_shapes=[pltpu.SemaphoreType.DMA],
         compiler_params=pltpu.CompilerParams(vmem_limit_bytes=limit),
         cost_estimate=pl.CostEstimate(
             flops=4 * tokens * length * queries.shape[1],
@@ -162,7 +154,7 @@
             transcendentals=tokens * length * groups * per_group,
         ),
         name="attention",
-    )(lengths, place(matrix, pltpu.HBM), queries, gain, routes, numer, *kv_parts)
+    )(lengths, queries, gain, routes, numer, *kv_parts)
 
 
 def prepare_kernel(matrix, queries, keys, values, routes, numer, *refs):
@@ -216,6 +208,30 @@
         ),
         name="prepare",
     )(*[place(source, pltpu.HBM) for source in sources])
+
+
+def own_columns_kernel(matrix, after, out, sem):
+    share = out.shape[1]
+    lanes = pl.ds(pl.multiple_of(lax.axis_index("head") * share, share), share)
+    copy = pltpu.make_async_copy(matrix.at[:, lanes], out, sem)
+    copy.start()
+    copy.wait()
+
+
+def own_columns_of(matrix, share, after):
+    rows = matrix.shape[0]
+    return pl.pallas_call(
+        own_columns_kernel,
+        out_shape=jax.ShapeDtypeStruct((rows, share), BF16),
+        in_specs=[HBM, ANY],
+        out_specs=VMEM,
+        scratch_shapes=[pltpu.SemaphoreType.DMA],
+        compiler_params=pltpu.CompilerParams(vmem_limit_bytes=4 << 20),
+        cost_estimate=pl.CostEstimate(
+            flops=0, bytes_accessed=4 * rows * share, transcendentals=0
+        ),
+        name="own_columns",
+    )(place(matrix, pltpu.HBM), after)
 
 
 def pack_kernel(tokens, pieces, *refs):
@@ -633,8 +649,8 @@
     kv_parts = spread(own_kv, "seq")
     gain = norm_gain.reshape(head_count, 1, share)
 
-    own_weights, gain, *attended = attend(
-        sequence_lengths, matrix, rows, gain, own_routes, numer, kv_parts, count
+    gain, *attended = attend(
+        sequence_lengths, rows, gain, own_routes, numer, kv_parts, count
     )
     if split:
         attended = swaps(attended, "seq")
@@ -652,6 +668,7 @@
         weights = [[got, swap(again, "dat", 1)] for got, again in zip(weights, carried)]
     else:
         weights = [[got] for got in weights]
+    own_weights = own_columns_of(matrix, share, mine)
     rows = [mine] + [swap(mine, "head", m) for m in range(1, head_count)]
     sums = project(rows, [[own_weights]] + weights, count if split else 1)
     chunk = min(256, expert_gate.shape[2])

time: 84.8 us -> 83.6 us (0.986)
  waiting for transfers between devices: 23.3 us -> 22 us
    ppermute x19, waiting for transfers between devices: 23.3 us -> 22 us  [swap(): return lax.ppermute(array, axis, pairs)]
    pallas_call x0 -> x1, Pallas kernels: none -> 1.28 us  [own_columns_of(): pl.pallas_call(own_columns_kernel, out_shape=jax.ShapeDtypeStruct((rows,...]
    pallas_call x1, Pallas kernels: 2.12 us -> 0.9 us  [attend(): pl.pallas_call(functools.partial(attention_kernel, (tokens, groups, per_g...]
  transfers between devices with their start and end apart: 19 -> 19, of which waited for: 9 -> 9; matrix products, arithmetic and copies ran while one was open for 1% -> 1% of each run, Pallas kernels for 26% -> 27%
where the time goes in v5:
time: 83.6 us; the launch traced here: 83.3 us
  Pallas kernels  32.7 us (39%)
  starting transfers between devices  26.5 us (32%)
  waiting for transfers between devices  22 us (26%)
  between operations  1.41 us (2%)
    ppermute x19, starting transfers between devices, swap(): return lax.ppermute(array, axis, pairs)  26.5 us
    ppermute x19, waiting for transfers between devices, swap(): return lax.ppermute(array, axis, pairs)  22 us
    pallas_call x2, Pallas kernels, run_experts(): pl.pallas_call(functools.partial(expert_kernel, shape), out_shape=out_sha...  12.7 us
    pallas_call x1, Pallas kernels, fetch(): pl.pallas_call(functools.partial(fetch_kernel, chunk), out_shape=[pltpu.V...  12.4 us
    pallas_call x1, Pallas kernels, fetch_rows(): pl.pallas_call(functools.partial(fetch_rows_kernel, chunk, early), out_sh...  2.94 us
  transfers between devices with their start and end apart: 19, of which 9 were waited for; matrix products, arithmetic and copies ran while one was open for 1% of the time, Pallas kernels for 27%

profile of v5, /device:TPU:0, one launch (start us, length us, event | category | flops | bytes accessed | tf_op | source)
XLA Modules:
  0.0 83.3 jit_solution(13551126395435275542)
XLA Ops:
  0.6 1.2 %prepare.1 = (bf16[64,512]{1,0:T(8,128)(2,1)S(1)}, bf16[64,1536]{1,0:T(8,128)(2,1)S(1)}, s32[2,64]{1,0:T(2,128)S(1)}, s32[1,64]{1,0:T(1,128)S(1)}, bf16[192,1536]{1,0:T(8,128)(2,1)S(1)}) custom-call(bf16[384,3072]{1,0:T(8,128)(2,1)} %bitcast.15, bf16[64,1536]{1,0:T(8,128)(2,1)} %bitcast.18, bf16[64,256]{1,0:T(8,128)(2,1)} %bitcast.19, ...), custom_call_target="tpu_custom_call" | custom-call | bytes 4718592 | tf_op jit(solution)/shard_map/prepare/pallas_call | solution.py:199
  1.8 3.0 %collective-permute-start.6 = (bf16[192,1536]{1,0:T(8,128)(2,1)S(1)}, bf16[192,1536]{1,0:T(8,128)(2,1)S(1)}, u32[]{:S(2)}, u32[]{:S(2)}) collective-permute-start(bf16[192,1536]{1,0:T(8,128)(2,1)S(1)} %get-tuple-element.48), channel_id=1, source_target_pairs={{0,2},{2,0},{1,3},{3,1},{4,6},{6,4},{5,7},{7,5},{8,10},{10,8},{9,1... | collective-permute-start | bytes 1769480 | tf_op jit(solution)/shard_map/ppermute | solution.py:37
  4.8 1.6 %collective-permute-start = (bf16[64,512]{1,0:T(8,128)(2,1)S(1)}, bf16[64,512]{1,0:T(8,128)(2,1)S(1)}, u32[]{:S(2)}, u32[]{:S(2)}) collective-permute-start(bf16[64,512]{1,0:T(8,128)(2,1)S(1)} %get-tuple-element.43.refs_0_), channel_id=1, source_target_pairs={{0,4},{4,0},{8,12},{12,8},{1,5},{5,1},{9,13},{13,9},{2,6},{6,2},{1... | collective-permute-start | bytes 196616 | tf_op jit(solution)/shard_map/ppermute | solution.py:37
  6.4 2.6 %collective-permute-start.1 = (bf16[64,512]{1,0:T(8,128)(2,1)S(1)}, bf16[64,512]{1,0:T(8,128)(2,1)S(1)}, u32[]{:S(2)}, u32[]{:S(2)}) collective-permute-start(bf16[64,512]{1,0:T(8,128)(2,1)S(1)} %get-tuple-element.43.refs_0_), channel_id=1, source_target_pairs={{0,8},{4,12},{8,0},{12,4},{1,9},{5,13},{9,1},{13,5},{2,10},{6,14},... | collective-permute-start | bytes 196616 | tf_op jit(solution)/shard_map/ppermute | solution.py:37
  10.6 2.8 %collective-permute-done.1.refs_2_ = bf16[64,512]{1,0:T(8,128)(2,1)S(1)} collective-permute-done((bf16[64,512]{1,0:T(8,128)(2,1)S(1)}, bf16[64,512]{1,0:T(8,128)(2,1)S(1)}, u32[]{:S(2)}, u32[]{:S(2)}) %collective-permute-start.1) | collective-permute-done | bytes 65568 | tf_op jit(solution)/shard_map/ppermute | solution.py:37
  13.4 1.7 %collective-permute-done.2.refs_3_ = bf16[64,512]{1,0:T(8,128)(2,1)S(1)} collective-permute-done((bf16[64,512]{1,0:T(8,128)(2,1)S(1)}, bf16[64,512]{1,0:T(8,128)(2,1)S(1)}, u32[]{:S(2)}, u32[]{:S(2)}) %collective-permute-start.2) | collective-permute-done | bytes 65568 | tf_op jit(solution)/shard_map/ppermute | solution.py:37
  16.0 1.6 %collective-permute-start.3 = (bf16[80,384]{1,0:T(8,128)(2,1)S(1)}, bf16[80,384]{1,0:T(8,128)(2,1)S(1)}, u32[]{:S(2)}, u32[]{:S(2)}) collective-permute-start(bf16[80,384]{1,0:T(8,128)(2,1)S(1)} %get-tuple-element.45), channel_id=1, source_target_pairs={{0,12},{4,8},{8,4},{12,0},{1,13},{5,9},{9,5},{13,1},{2,14},{6,10},... | collective-permute-start | bytes 184328 | tf_op jit(solution)/shard_map/ppermute | solution.py:37
  17.6 2.9 %collective-permute-start.5 = (bf16[80,384]{1,0:T(8,128)(2,1)S(1)}, bf16[80,384]{1,0:T(8,128)(2,1)S(1)}, u32[]{:S(2)}, u32[]{:S(2)}) collective-permute-start(bf16[80,384]{1,0:T(8,128)(2,1)S(1)} %get-tuple-element.47), channel_id=1, source_target_pairs={{0,4},{4,0},{8,12},{12,8},{1,5},{5,1},{9,13},{13,9},{2,6},{6,2},{1... | collective-permute-start | bytes 184328 | tf_op jit(solution)/shard_map/ppermute | solution.py:37
  20.4 1.6 %collective-permute-done.3.refs_1_ = bf16[80,384]{1,0:T(8,128)(2,1)S(1)} collective-permute-done((bf16[80,384]{1,0:T(8,128)(2,1)S(1)}, bf16[80,384]{1,0:T(8,128)(2,1)S(1)}, u32[]{:S(2)}, u32[]{:S(2)}) %collective-permute-start.3) | collective-permute-done | bytes 61472 | tf_op jit(solution)/shard_map/ppermute | solution.py:37
  22.1 1.3 %collective-permute-done.4.refs_2_ = bf16[80,384]{1,0:T(8,128)(2,1)S(1)} collective-permute-done((bf16[80,384]{1,0:T(8,128)(2,1)S(1)}, bf16[80,384]{1,0:T(8,128)(2,1)S(1)}, u32[]{:S(2)}, u32[]{:S(2)}) %collective-permute-start.4) | collective-permute-done | bytes 61472 | tf_op jit(solution)/shard_map/ppermute | solution.py:37
  24.3 1.3 %own_columns.1.refs_2_ = bf16[384,1536]{1,0:T(8,128)(2,1)S(1)} custom-call(bf16[384,3072]{1,0:T(8,128)(2,1)} %bitcast.16, bf16[256,384]{1,0:T(8,128)(2,1)S(1)} %get-tuple-element.49.after.refs_0_), custom_call_target="tpu_custom_call" | custom-call | bytes 2359296 | tf_op jit(solution)/shard_map/own_columns/pallas_call | solution.py:223
  25.6 5.4 %collective-permute-done.7.refs_1_ = bf16[256,384]{1,0:T(8,128)(2,1)S(1)} collective-permute-done((bf16[256,384]{1,0:T(8,128)(2,1)S(1)}, bf16[256,384]{1,0:T(8,128)(2,1)S(1)}, u32[]{:S(2)}, u32[]{:S(2)}) %collective-permute-start.7) | collective-permute-done | bytes 196640 | tf_op jit(solution)/shard_map/ppermute | solution.py:37
  32.0 1.4 %collective-permute-start.10 = (bf16[64,1536]{1,0:T(8,128)(2,1)S(1)}, bf16[64,1536]{1,0:T(8,128)(2,1)S(1)}, u32[]{:S(2)}, u32[]{:S(2)}) collective-permute-start(bf16[64,1536]{1,0:T(8,128)(2,1)S(1)} %get-tuple-element.54), channel_id=1, source_target_pairs={{0,8},{4,12},{8,0},{12,4},{1,9},{5,13},{9,1},{13,5},{2,10},{6,14},... | collective-permute-start | bytes 589832 | tf_op jit(solution)/shard_map/ppermute | solution.py:37
  33.4 2.3 %collective-permute-start.11 = (bf16[64,1536]{1,0:T(8,128)(2,1)S(1)}, bf16[64,1536]{1,0:T(8,128)(2,1)S(1)}, u32[]{:S(2)}, u32[]{:S(2)}) collective-permute-start(bf16[64,1536]{1,0:T(8,128)(2,1)S(1)} %get-tuple-element.55), channel_id=1, source_target_pairs={{0,12},{4,8},{8,4},{12,0},{1,13},{5,9},{9,5},{13,1},{2,14},{6,10},... | collective-permute-start | bytes 589832 | tf_op jit(solution)/shard_map/ppermute | solution.py:37
  35.7 12.4 %fetch.1 = (bf16[2,3072,256]{2,1,0:T(8,128)(2,1)S(1)}, bf16[2,3072,256]{2,1,0:T(8,128)(2,1)S(1)}, bf16[2,3072,256]{2,1,0:T(8,128)(2,1)S(1)}, bf16[2,3072,256]{2,...) custom-call(bf16[2,3072,2048]{2,1,0:T(8,128)(2,1)} %refs_21_.1, ...), custom_call_target="tpu_custom_call" | custom-call | bytes 75497472 | tf_op jit(solution)/shard_map/fetch/pallas_call | solution.py:339
  49.4 1.8 %collective-permute-start.13 = (bf16[64,1536]{1,0:T(8,128)(2,1)S(1)}, bf16[64,1536]{1,0:T(8,128)(2,1)S(1)}, u32[]{:S(2)}, u32[]{:S(2)}) collective-permute-start(bf16[64,1536]{1,0:T(8,128)(2,1)S(1)} %fusion.after.refs_0_), channel_id=1, source_target_pairs={{0,12},{4,8},{8,4},{12,0},{1,13},{5,9},{9,5},{13,1},{2,14},{6,10},... | collective-permute-start | bytes 589832 | tf_op jit(solution)/shard_map/ppermute | solution.py:37
  51.2 3.9 %collective-permute-start.15 = (bf16[64,1536]{1,0:T(8,128)(2,1)S(1)}, bf16[64,1536]{1,0:T(8,128)(2,1)S(1)}, u32[]{:S(2)}, u32[]{:S(2)}) collective-permute-start(bf16[64,1536]{1,0:T(8,128)(2,1)S(1)} %fusion.after.refs_0_), channel_id=1, source_target_pairs={{0,4},{4,0},{8,12},{12,8},{1,5},{5,1},{9,13},{13,9},{2,6},{6,2},{1... | collective-permute-start | bytes 589832 | tf_op jit(solution)/shard_map/ppermute | solution.py:37
  55.1 1.4 %collective-permute-start.17 = (bf16[64,1536]{1,0:T(8,128)(2,1)S(1)}, bf16[64,1536]{1,0:T(8,128)(2,1)S(1)}, u32[]{:S(2)}, u32[]{:S(2)}) collective-permute-start(bf16[64,1536]{1,0:T(8,128)(2,1)S(1)} %fusion.after.refs_0_), channel_id=1, source_target_pairs={{0,8},{4,12},{8,0},{12,4},{1,9},{5,13},{9,1},{13,5},{2,10},{6,14},... | collective-permute-start | bytes 589832 | tf_op jit(solution)/shard_map/ppermute | solution.py:37
  56.5 2.9 %fetch_rows.1 = (bf16[2,1536,256]{2,1,0:T(8,128)(2,1)S(1)}, bf16[2,1536,256]{2,1,0:T(8,128)(2,1)S(1)}, bf16[2,1536,256]{2,1,0:T(8,128)(2,1)S(1)}, bf16[2,1536,256]{2,1,0:T(8,128)(2,1)S(1)}) custom-call(bf16[2,3072,2048]{2,1,0:T(8,128)(2,1)} %refs_21_.1, bf16[2,3072,2048]{2,1,0:T(8,128)(2,1)} %refs_22_.3, bf16[64,1536]{1,0:T(8,128)(2,1)S(1)} %fusion.after.refs_0_), custom_call_target="tpu_custom_call" | custom-call | bytes 12582912 | tf_op jit(solution)/shard_map/fetch_rows/pallas_call | solution.py:382
  60.0 1.5 %collective-permute-start.14 = (bf16[64,1536]{1,0:T(8,128)(2,1)S(1)}, bf16[64,1536]{1,0:T(8,128)(2,1)S(1)}, u32[]{:S(2)}, u32[]{:S(2)}) collective-permute-start(bf16[64,1536]{1,0:T(8,128)(2,1)S(1)} %collective-permute-done.13.refs_1_), channel_id=1, source_target_pairs={{0,2},{2,0},{1,3},{3,1},{4,6},{6,4},{5,7},{7,5},{8,10},{10,8},{9,1... | collective-permute-start | bytes 589832 | tf_op jit(solution)/shard_map/ppermute | solution.py:37
  62.1 6.9 %collective-permute-done.17.refs_3_ = bf16[64,1536]{1,0:T(8,128)(2,1)S(1)} collective-permute-done((bf16[64,1536]{1,0:T(8,128)(2,1)S(1)}, bf16[64,1536]{1,0:T(8,128)(2,1)S(1)}, u32[]{:S(2)}, u32[]{:S(2)}) %collective-permute-start.17) | collective-permute-done | bytes 196640 | tf_op jit(solution)/shard_map/ppermute | solution.py:37
  69.5 4.9 %experts.2 = (bf16[1,320,256]{2,1,0:T(8,128)(2,1)S(1)}, f32[2,160,1]{2,1,0:T(8,128)S(1)}, f32[2,160,1]{2,1,0:T(8,128)S(1)}, bf16[2,2,160,2048]{3,2,1,0:T(8,128)(2,1)S(1)}) custom-call(bf16[64,1536]{1,0:T(8,128)(2,1)S(1)} %fusion.after.refs_0_, bf16[64,1536]{1,0:T(8,128)(2,1)S(1)} %collective-permute-done.13.refs_1_, ...), custom_call_target="tpu_custom_call" | custom-call | flops 4026531840 | bytes 25165824 | tf_op jit(solution)/shard_map/experts/pallas_call | solution.py:590
  74.5 1.1 %collective-permute-done.18.refs_3_ = bf16[64,1536]{1,0:T(8,128)(2,1)S(1)} collective-permute-done((bf16[64,1536]{1,0:T(8,128)(2,1)S(1)}, bf16[64,1536]{1,0:T(8,128)(2,1)S(1)}, u32[]{:S(2)}, u32[]{:S(2)}) %collective-permute-start.18) | collective-permute-done | bytes 196640 | tf_op jit(solution)/shard_map/ppermute | solution.py:37
  75.5 7.8 %experts.3 = bf16[2,160,2048]{2,1,0:T(8,128)(2,1)} custom-call(bf16[64,1536]{1,0:T(8,128)(2,1)S(1)} %collective-permute-done.12.refs_0_, bf16[64,1536]{1,0:T(8,128)(2,1)S(1)} %collective-permute-done.14.refs_1_, bf16[64,1536]{1,0:T(8,128)(2,1)S(1)} %collective-permute-done.16.refs_2_, bf16[64,1536]{1,0:T(8,128)(2,1)S(1)} %collective-permute-done.18.refs_3_, ...), custom_call_target="tpu_custom_call" | custom-call | flops 4026531840 | bytes 25165824 | tf_op jit(solution)/shard_map/experts/pallas_call | solution.py:590
  (29 shorter events, 6.6 us)
Async XLA Ops:
  1.8 21.6 %collective-permute-start.6 = (bf16[192,1536]{1,0:T(8,128)(2,1)S(1)}, bf16[192,1536]{1,0:T(8,128)(2,1)S(1)}, u32[]{:S(2)}, u32[]{:S(2)}) collective-permute-start(bf16[192,1536]{1,0:T(8,128)(2,1)S(1)} %get-tuple-element.48), channel_id=1, source_target_pairs={{0,2},{2,0},{1,3},{3,1},{4,6},{6,4},{5,7},{7,5},{8,10},{10,8},{9,1... | collective-permute-start | bytes 1769480 | tf_op jit(solution)/shard_map/ppermute | solution.py:37
  4.8 5.7 %collective-permute-start = (bf16[64,512]{1,0:T(8,128)(2,1)S(1)}, bf16[64,512]{1,0:T(8,128)(2,1)S(1)}, u32[]{:S(2)}, u32[]{:S(2)}) collective-permute-start(bf16[64,512]{1,0:T(8,128)(2,1)S(1)} %get-tuple-element.43.refs_0_), channel_id=1, source_target_pairs={{0,4},{4,0},{8,12},{12,8},{1,5},{5,1},{9,13},{13,9},{2,6},{6,2},{1... | collective-permute-start | bytes 196616 | tf_op jit(solution)/shard_map/ppermute | solution.py:37
  6.4 7.0 %collective-permute-start.1 = (bf16[64,512]{1,0:T(8,128)(2,1)S(1)}, bf16[64,512]{1,0:T(8,128)(2,1)S(1)}, u32[]{:S(2)}, u32[]{:S(2)}) collective-permute-start(bf16[64,512]{1,0:T(8,128)(2,1)S(1)} %get-tuple-element.43.refs_0_), channel_id=1, source_target_pairs={{0,8},{4,12},{8,0},{12,4},{1,9},{5,13},{9,1},{13,5},{2,10},{6,14},... | collective-permute-start | bytes 196616 | tf_op jit(solution)/shard_map/ppermute | solution.py:37
  9.0 6.1 %collective-permute-start.2 = (bf16[64,512]{1,0:T(8,128)(2,1)S(1)}, bf16[64,512]{1,0:T(8,128)(2,1)S(1)}, u32[]{:S(2)}, u32[]{:S(2)}) collective-permute-start(bf16[64,512]{1,0:T(8,128)(2,1)S(1)} %get-tuple-element.43.refs_0_), channel_id=1, source_target_pairs={{0,12},{4,8},{8,4},{12,0},{1,13},{5,9},{9,5},{13,1},{2,14},{6,10},... | collective-permute-start | bytes 196616 | tf_op jit(solution)/shard_map/ppermute | solution.py:37
  16.0 6.1 %collective-permute-start.3 = (bf16[80,384]{1,0:T(8,128)(2,1)S(1)}, bf16[80,384]{1,0:T(8,128)(2,1)S(1)}, u32[]{:S(2)}, u32[]{:S(2)}) collective-permute-start(bf16[80,384]{1,0:T(8,128)(2,1)S(1)} %get-tuple-element.45), channel_id=1, source_target_pairs={{0,12},{4,8},{8,4},{12,0},{1,13},{5,9},{9,5},{13,1},{2,14},{6,10},... | collective-permute-start | bytes 184328 | tf_op jit(solution)/shard_map/ppermute | solution.py:37
  17.6 5.8 %collective-permute-start.4 = (bf16[80,384]{1,0:T(8,128)(2,1)S(1)}, bf16[80,384]{1,0:T(8,128)(2,1)S(1)}, u32[]{:S(2)}, u32[]{:S(2)}) collective-permute-start(bf16[80,384]{1,0:T(8,128)(2,1)S(1)} %get-tuple-element.46), channel_id=1, source_target_pairs={{0,8},{4,12},{8,0},{12,4},{1,9},{5,13},{9,1},{13,5},{2,10},{6,14},... | collective-permute-start | bytes 184328 | tf_op jit(solution)/shard_map/ppermute | solution.py:37
  17.6 5.8 %collective-permute-start.5 = (bf16[80,384]{1,0:T(8,128)(2,1)S(1)}, bf16[80,384]{1,0:T(8,128)(2,1)S(1)}, u32[]{:S(2)}, u32[]{:S(2)}) collective-permute-start(bf16[80,384]{1,0:T(8,128)(2,1)S(1)} %get-tuple-element.47), channel_id=1, source_target_pairs={{0,4},{4,0},{8,12},{12,8},{1,5},{5,1},{9,13},{13,9},{2,6},{6,2},{1... | collective-permute-start | bytes 184328 | tf_op jit(solution)/shard_map/ppermute | solution.py:37
  23.6 7.4 %collective-permute-start.8 = (bf16[192,1536]{1,0:T(8,128)(2,1)S(1)}, bf16[192,1536]{1,0:T(8,128)(2,1)S(1)}, u32[]{:S(2)}, u32[]{:S(2)}) collective-permute-start(bf16[192,1536]{1,0:T(8,128)(2,1)S(1)} %get-tuple-element.50), channel_id=1, source_target_pairs={{0,1},{1,0},{2,3},{3,2},{4,5},{5,4},{6,7},{7,6},{8,9},{9,8},{10,11... | collective-permute-start | bytes 1769480 | tf_op jit(solution)/shard_map/ppermute | solution.py:37
  23.7 7.3 %collective-permute-start.7 = (bf16[256,384]{1,0:T(8,128)(2,1)S(1)}, bf16[256,384]{1,0:T(8,128)(2,1)S(1)}, u32[]{:S(2)}, u32[]{:S(2)}) collective-permute-start(bf16[256,384]{1,0:T(8,128)(2,1)S(1)} %get-tuple-element.49.after.refs_0_), channel_id=1, source_target_pairs={{0,2},{2,0},{1,3},{3,1},{4,6},{6,4},{5,7},{7,5},{8,10},{10,8},{9,1... | collective-permute-start | bytes 589832 | tf_op jit(solution)/shard_map/ppermute | solution.py:37
  32.0 16.8 %collective-permute-start.10 = (bf16[64,1536]{1,0:T(8,128)(2,1)S(1)}, bf16[64,1536]{1,0:T(8,128)(2,1)S(1)}, u32[]{:S(2)}, u32[]{:S(2)}) collective-permute-start(bf16[64,1536]{1,0:T(8,128)(2,1)S(1)} %get-tuple-element.54), channel_id=1, source_target_pairs={{0,8},{4,12},{8,0},{12,4},{1,9},{5,13},{9,1},{13,5},{2,10},{6,14},... | collective-permute-start | bytes 589832 | tf_op jit(solution)/shard_map/ppermute | solution.py:37
  33.4 15.4 %collective-permute-start.11 = (bf16[64,1536]{1,0:T(8,128)(2,1)S(1)}, bf16[64,1536]{1,0:T(8,128)(2,1)S(1)}, u32[]{:S(2)}, u32[]{:S(2)}) collective-permute-start(bf16[64,1536]{1,0:T(8,128)(2,1)S(1)} %get-tuple-element.55), channel_id=1, source_target_pairs={{0,12},{4,8},{8,4},{12,0},{1,13},{5,9},{9,5},{13,1},{2,14},{6,10},... | collective-permute-start | bytes 589832 | tf_op jit(solution)/shard_map/ppermute | solution.py:37
  35.7 13.5 %collective-permute-start.9 = (bf16[64,1536]{1,0:T(8,128)(2,1)S(1)}, bf16[64,1536]{1,0:T(8,128)(2,1)S(1)}, u32[]{:S(2)}, u32[]{:S(2)}) collective-permute-start(bf16[64,1536]{1,0:T(8,128)(2,1)S(1)} %get-tuple-element.53), channel_id=1, source_target_pairs={{0,4},{4,0},{8,12},{12,8},{1,5},{5,1},{9,13},{13,9},{2,6},{6,2},{1... | collective-permute-start | bytes 589832 | tf_op jit(solution)/shard_map/ppermute | solution.py:37
  35.7 13.5 %copy-start.1 = (bf16[1,64,1536]{2,1,0:T(8,128)(2,1)S(1)}, bf16[1,64,1536]{2,1,0:T(8,128)(2,1)}, u32[]{:S(2)}) copy-start(bf16[1,64,1536]{2,1,0:T(8,128)(2,1)} %param.14) | copy-start | bytes 589828
  49.4 20.2 %copy-start = (bf16[64,1536]{1,0:T(8,128)(2,1)}, bf16[64,1536]{1,0:T(8,128)(2,1)S(1)}, u32[]{:S(2)}) copy-start(bf16[64,1536]{1,0:T(8,128)(2,1)S(1)} %fusion.after.refs_0_) | copy-start | bytes 589828
  49.4 10.7 %collective-permute-start.13 = (bf16[64,1536]{1,0:T(8,128)(2,1)S(1)}, bf16[64,1536]{1,0:T(8,128)(2,1)S(1)}, u32[]{:S(2)}, u32[]{:S(2)}) collective-permute-start(bf16[64,1536]{1,0:T(8,128)(2,1)S(1)} %fusion.after.refs_0_), channel_id=1, source_target_pairs={{0,12},{4,8},{8,4},{12,0},{1,13},{5,9},{9,5},{13,1},{2,14},{6,10},... | collective-permute-start | bytes 589832 | tf_op jit(solution)/shard_map/ppermute | solution.py:37
  51.2 10.3 %collective-permute-start.15 = (bf16[64,1536]{1,0:T(8,128)(2,1)S(1)}, bf16[64,1536]{1,0:T(8,128)(2,1)S(1)}, u32[]{:S(2)}, u32[]{:S(2)}) collective-permute-start(bf16[64,1536]{1,0:T(8,128)(2,1)S(1)} %fusion.after.refs_0_), channel_id=1, source_target_pairs={{0,4},{4,0},{8,12},{12,8},{1,5},{5,1},{9,13},{13,9},{2,6},{6,2},{1... | collective-permute-start | bytes 589832 | tf_op jit(solution)/shard_map/ppermute | solution.py:37
  55.1 13.9 %collective-permute-start.17 = (bf16[64,1536]{1,0:T(8,128)(2,1)S(1)}, bf16[64,1536]{1,0:T(8,128)(2,1)S(1)}, u32[]{:S(2)}, u32[]{:S(2)}) collective-permute-start(bf16[64,1536]{1,0:T(8,128)(2,1)S(1)} %fusion.after.refs_0_), channel_id=1, source_target_pairs={{0,8},{4,12},{8,0},{12,4},{1,9},{5,13},{9,1},{13,5},{2,10},{6,14},... | collective-permute-start | bytes 589832 | tf_op jit(solution)/shard_map/ppermute | solution.py:37
  59.4 15.0 %collective-permute-start.12 = (bf16[64,1536]{1,0:T(8,128)(2,1)S(1)}, bf16[64,1536]{1,0:T(8,128)(2,1)S(1)}, u32[]{:S(2)}, u32[]{:S(2)}) collective-permute-start(bf16[64,1536]{1,0:T(8,128)(2,1)S(1)} %fusion.after.refs_0_), channel_id=1, source_target_pairs={{0,2},{2,0},{1,3},{3,1},{4,6},{6,4},{5,7},{7,5},{8,10},{10,8},{9,1... | collective-permute-start | bytes 589832 | tf_op jit(solution)/shard_map/ppermute | solution.py:37
  60.0 14.4 %collective-permute-start.14 = (bf16[64,1536]{1,0:T(8,128)(2,1)S(1)}, bf16[64,1536]{1,0:T(8,128)(2,1)S(1)}, u32[]{:S(2)}, u32[]{:S(2)}) collective-permute-start(bf16[64,1536]{1,0:T(8,128)(2,1)S(1)} %collective-permute-done.13.refs_1_), channel_id=1, source_target_pairs={{0,2},{2,0},{1,3},{3,1},{4,6},{6,4},{5,7},{7,5},{8,10},{10,8},{9,1... | collective-permute-start | bytes 589832 | tf_op jit(solution)/shard_map/ppermute | solution.py:37
  61.5 12.9 %collective-permute-start.16 = (bf16[64,1536]{1,0:T(8,128)(2,1)S(1)}, bf16[64,1536]{1,0:T(8,128)(2,1)S(1)}, u32[]{:S(2)}, u32[]{:S(2)}) collective-permute-start(bf16[64,1536]{1,0:T(8,128)(2,1)S(1)} %collective-permute-done.15.refs_2_), channel_id=1, source_target_pairs={{0,2},{2,0},{1,3},{3,1},{4,6},{6,4},{5,7},{7,5},{8,10},{10,8},{9,1... | collective-permute-start | bytes 589832 | tf_op jit(solution)/shard_map/ppermute | solution.py:37
  69.0 6.5 %collective-permute-start.18 = (bf16[64,1536]{1,0:T(8,128)(2,1)S(1)}, bf16[64,1536]{1,0:T(8,128)(2,1)S(1)}, u32[]{:S(2)}, u32[]{:S(2)}) collective-permute-start(bf16[64,1536]{1,0:T(8,128)(2,1)S(1)} %collective-permute-done.17.refs_3_), channel_id=1, source_target_pairs={{0,2},{2,0},{1,3},{3,1},{4,6},{6,4},{5,7},{7,5},{8,10},{10,8},{9,1... | collective-permute-start | bytes 589832 | tf_op jit(solution)/shard_map/ppermute | solution.py:37

commit v6 on v5

--- a/solution.py
+++ b/solution.py
@@ -236,8 +236,9 @@
 
 def pack_kernel(tokens, pieces, *refs):
     parts, refs = sorted_back(refs[:pieces], ATTENDED_ORDER), refs[pieces:]
-    carried = (len(refs) - 3) // 2
-    carried_in, packed, route, refs = refs[:carried], refs[carried], refs[carried + 1], refs[carried + 2 :]
+    carried = (len(refs) - 4) // 2
+    carried_in, refs = refs[:carried], refs[carried:]
+    packed, others, route, refs = refs[0], refs[1], refs[2], refs[3:]
     copies = [
         pltpu.make_async_copy(source, out, refs[-1].at[i])
         for i, (source, out) in enumerate(zip(carried_in, refs[:-1]))
@@ -247,6 +248,8 @@
     for k, ref in enumerate(parts):
         at = slice(k * tokens, (k + 1) * tokens)
         packed[at, :] = ref[:tokens, :]
+        if k:
+            others[(k - 1) * tokens : k * tokens, :] = ref[:tokens, :]
         route[:, at] = ref[tokens : tokens + 8, :tokens]
     for copy in copies:
         copy.wait()
@@ -257,6 +260,7 @@
     rows = tokens * len(parts)
     out_shape = [
         jax.ShapeDtypeStruct((rows, width), BF16),
+        jax.ShapeDtypeStruct((max(rows - tokens, tokens), width), BF16),
         jax.ShapeDtypeStruct((8, rows), BF16),
         *[jax.ShapeDtypeStruct(array.shape, array.dtype) for array in carried],
     ]
@@ -271,16 +275,22 @@
     )(*shuffled(parts, ATTENDED_ORDER), *carried)
 
 
-def project_kernel(parts, halves, *refs):
-    rows, refs = refs[:parts], refs[parts:]
+def project_kernel(parts, halves, sent, tokens, *refs):
+    rows, refs = [refs[:1]], refs[1:]
+    for _ in range(1, parts):
+        rows.append(refs[:sent])
+        refs = refs[sent:]
     weights = [refs[:1]] + [refs[1 + m * halves : 1 + (m + 1) * halves] for m in range(parts - 1)]
     outs = refs[1 + (parts - 1) * halves :]
     core = lax.axis_index("dat")
     total = None
     for m in range(parts):
-        factors = [rows[m][...]]
+        pieces = [ref[...] for ref in rows[m]]
+        if len(pieces) > 1:
+            pieces[0] = pieces[0][:tokens]
+        factors = [jnp.concatenate(pieces, axis=0)]
         if len(weights[m]) > 1:
-            half = rows[m].shape[1] // 2
+            half = factors[0].shape[1] // 2
             low, high = factors[0][:, :half], factors[0][:, half:]
             factors = [jnp.where(core == 0, low, high), jnp.where(core == 0, high, low)]
         for factor, weight in zip(factors, weights[m]):
@@ -293,15 +303,18 @@
 
 
 def project(rows, weights, pieces):
-    parts, (tokens, depth), width = len(rows), rows[0].shape, weights[0][0].shape[1]
+    parts, (tokens, depth), width = len(rows), rows[0][0].shape, weights[0][0].shape[1]
+    flat = [piece for part in rows for piece in part]
     flat_weights = [w for part in weights for w in part]
     return pl.pallas_call(
-        functools.partial(project_kernel, parts, len(weights[-1])),
+        functools.partial(
+            project_kernel, parts, len(weights[-1]), len(rows[-1]), tokens // pieces
+        ),
         out_shape=[
             jax.ShapeDtypeStruct((tokens // pieces, width), BF16 if i else F32)
             for i in range(pieces)
         ],
-        in_specs=[VMEM] * (parts + len(flat_weights)),
+        in_specs=[VMEM] * (len(flat) + len(flat_weights)),
         out_specs=[VMEM] * pieces,
         compiler_params=pltpu.CompilerParams(
             vmem_limit_bytes=min(40 << 20, (4 << 20) + 16 * tokens * width)
@@ -312,7 +325,7 @@
             transcendentals=0,
         ),
         name="projection",
-    )(*rows, *flat_weights)
+    )(*flat, *flat_weights)
 
 
 def fetch_kernel(chunk, gate_hbm, up_hbm, kept, *refs):
@@ -653,8 +666,12 @@
         sequence_lengths, rows, gain, own_routes, numer, kv_parts, count
     )
     if split:
+        own_piece = attended[0]
         attended = swaps(attended, "seq")
-        mine, routing, *carried = pack(attended, tokens, weights if halves == 2 else [])
+        ahead = [swap(own_piece, "head", m) for m in range(1, head_count)] if count > 1 else []
+        relayed = weights if halves == 2 else []
+        mine, others, routing, *carried = pack(attended, tokens, relayed + ahead)
+        carried, ahead = carried[: len(relayed)], carried[len(relayed) :]
     else:
         shares = attended[0].reshape(tokens, heads, count, part).transpose(2, 0, 1, 3)
         shares = shares.reshape(count * tokens, heads * part)
@@ -669,14 +686,19 @@
     else:
         weights = [[got] for got in weights]
     own_weights = own_columns_of(matrix, share, mine)
-    rows = [mine] + [swap(mine, "head", m) for m in range(1, head_count)]
+    if split and count > 1:
+        rows = [[mine]] + [
+            [first, swap(others, "head", m + 1)] for m, first in enumerate(ahead)
+        ]
+    else:
+        rows = [[mine]] + [[swap(mine, "head", m)] for m in range(1, head_count)]
     sums = project(rows, [[own_weights]] + weights, count if split else 1)
     chunk = min(256, expert_gate.shape[2])
     early = max(1, expert_gate.shape[0] * (expert_gate.shape[2] // chunk) * 12 // 16)
     *fetched, mixed = fetch(expert_gate, expert_up, sums[0], chunk, early)
     if split:
         received = swaps(sums, "seq")[1:]
-        for part_sum in received:
+        for part_sum in received[1:] + received[:1]:
             mixed = mixed + part_sum.astype(F32)
     else:
         mixed = lax.psum_scatter(mixed, "seq", scatter_dimension=0, tiled=True)

time: 83.6 us -> 83.1 us (level)
  waiting for transfers between devices: 22 us -> 18 us
  starting transfers between devices: 26.5 us -> 29.9 us
    ppermute x19 -> x20, waiting for transfers between devices: 22 us -> 18 us  [swap(): return lax.ppermute(array, axis, pairs)]
    ppermute x19 -> x20, starting transfers between devices: 26.5 us -> 29.9 us  [swap(): return lax.ppermute(array, axis, pairs)]
  transfers between devices with their start and end apart: 19 -> 20, of which waited for: 9 -> 9; matrix products, arithmetic and copies ran while one was open for 1% -> 1% of each run, Pallas kernels for 27% -> 27%
where the time goes in v6:
time: 83.1 us; the launch traced here: 82.9 us
  Pallas kernels  32.7 us (39%)
  starting transfers between devices  29.9 us (36%)
  waiting for transfers between devices  18 us (22%)
  between operations  1.41 us (2%)
    ppermute x20, starting transfers between devices, swap(): return lax.ppermute(array, axis, pairs)  29.9 us
    ppermute x20, waiting for transfers between devices, swap(): return lax.ppermute(array, axis, pairs)  18 us
    pallas_call x2, Pallas kernels, run_experts(): pl.pallas_call(functools.partial(expert_kernel, shape), out_shape=out_sha...  12.7 us
    pallas_call x1, Pallas kernels, fetch(): pl.pallas_call(functools.partial(fetch_kernel, chunk), out_shape=[pltpu.V...  12.4 us
    pallas_call x1, Pallas kernels, fetch_rows(): pl.pallas_call(functools.partial(fetch_rows_kernel, chunk, early), out_sh...  2.94 us
  transfers between devices with their start and end apart: 20, of which 9 were waited for; matrix products, arithmetic and copies ran while one was open for 1% of the time, Pallas kernels for 27%

profile of v6, /device:TPU:0, one launch (start us, length us, event | category | flops | bytes accessed | tf_op | source)
XLA Modules:
  0.0 82.9 jit_solution(6441404967198977228)
XLA Ops:
  1.8 3.0 %collective-permute-start.6 = (bf16[192,1536]{1,0:T(8,128)(2,1)S(1)}, bf16[192,1536]{1,0:T(8,128)(2,1)S(1)}, u32[]{:S(2)}, u32[]{:S(2)}) collective-permute-start(bf16[192,1536]{1,0:T(8,128)(2,1)S(1)} %get-tuple-element.50), channel_id=1, source_target_pairs={{0,2},{2,0},{1,3},{3,1},{4,6},{6,4},{5,7},{7,5},{8,10},{10,8},{9,1... | collective-permute-start | bytes 1769480 | tf_op jit(solution)/shard_map/ppermute | solution.py:37
  4.8 1.6 %collective-permute-start = (bf16[64,512]{1,0:T(8,128)(2,1)S(1)}, bf16[64,512]{1,0:T(8,128)(2,1)S(1)}, u32[]{:S(2)}, u32[]{:S(2)}) collective-permute-start(bf16[64,512]{1,0:T(8,128)(2,1)S(1)} %get-tuple-element.45.refs_0_), channel_id=1, source_target_pairs={{0,4},{4,0},{8,12},{12,8},{1,5},{5,1},{9,13},{13,9},{2,6},{6,2},{1... | collective-permute-start | bytes 196616 | tf_op jit(solution)/shard_map/ppermute | solution.py:37
  6.4 2.6 %collective-permute-start.1 = (bf16[64,512]{1,0:T(8,128)(2,1)S(1)}, bf16[64,512]{1,0:T(8,128)(2,1)S(1)}, u32[]{:S(2)}, u32[]{:S(2)}) collective-permute-start(bf16[64,512]{1,0:T(8,128)(2,1)S(1)} %get-tuple-element.45.refs_0_), channel_id=1, source_target_pairs={{0,8},{4,12},{8,0},{12,4},{1,9},{5,13},{9,1},{13,5},{2,10},{6,14},... | collective-permute-start | bytes 196616 | tf_op jit(solution)/shard_map/ppermute | solution.py:37
  10.6 2.8 %collective-permute-done.1.refs_2_ = bf16[64,512]{1,0:T(8,128)(2,1)S(1)} collective-permute-done((bf16[64,512]{1,0:T(8,128)(2,1)S(1)}, bf16[64,512]{1,0:T(8,128)(2,1)S(1)}, u32[]{:S(2)}, u32[]{:S(2)}) %collective-permute-start.1) | collective-permute-done | bytes 65568 | tf_op jit(solution)/shard_map/ppermute | solution.py:37
  13.4 1.7 %collective-permute-done.2.refs_3_ = bf16[64,512]{1,0:T(8,128)(2,1)S(1)} collective-permute-done((bf16[64,512]{1,0:T(8,128)(2,1)S(1)}, bf16[64,512]{1,0:T(8,128)(2,1)S(1)}, u32[]{:S(2)}, u32[]{:S(2)}) %collective-permute-start.2) | collective-permute-done | bytes 65568 | tf_op jit(solution)/shard_map/ppermute | solution.py:37
  16.6 1.5 %collective-permute-start.3 = (bf16[80,384]{1,0:T(8,128)(2,1)S(1)}, bf16[80,384]{1,0:T(8,128)(2,1)S(1)}, u32[]{:S(2)}, u32[]{:S(2)}) collective-permute-start(bf16[80,384]{1,0:T(8,128)(2,1)S(1)} %get-tuple-element.47), channel_id=1, source_target_pairs={{0,12},{4,8},{8,4},{12,0},{1,13},{5,9},{9,5},{13,1},{2,14},{6,10},... | collective-permute-start | bytes 184328 | tf_op jit(solution)/shard_map/ppermute | solution.py:37
  18.1 2.9 %collective-permute-start.5 = (bf16[80,384]{1,0:T(8,128)(2,1)S(1)}, bf16[80,384]{1,0:T(8,128)(2,1)S(1)}, u32[]{:S(2)}, u32[]{:S(2)}) collective-permute-start(bf16[80,384]{1,0:T(8,128)(2,1)S(1)} %get-tuple-element.49), channel_id=1, source_target_pairs={{0,4},{4,0},{8,12},{12,8},{1,5},{5,1},{9,13},{13,9},{2,6},{6,2},{1... | collective-permute-start | bytes 184328 | tf_op jit(solution)/shard_map/ppermute | solution.py:37
  21.0 1.6 %collective-permute-done.3.refs_1_ = bf16[80,384]{1,0:T(8,128)(2,1)S(1)} collective-permute-done((bf16[80,384]{1,0:T(8,128)(2,1)S(1)}, bf16[80,384]{1,0:T(8,128)(2,1)S(1)}, u32[]{:S(2)}, u32[]{:S(2)}) %collective-permute-start.3) | collective-permute-done | bytes 61472 | tf_op jit(solution)/shard_map/ppermute | solution.py:37
  22.6 1.3 %collective-permute-done.4.refs_2_ = bf16[80,384]{1,0:T(8,128)(2,1)S(1)} collective-permute-done((bf16[80,384]{1,0:T(8,128)(2,1)S(1)}, bf16[80,384]{1,0:T(8,128)(2,1)S(1)}, u32[]{:S(2)}, u32[]{:S(2)}) %collective-permute-start.4) | collective-permute-done | bytes 61472 | tf_op jit(solution)/shard_map/ppermute | solution.py:37
  24.3 1.6 %collective-permute-start.8 = (bf16[192,384]{1,0:T(8,128)(2,1)S(1)}, bf16[192,384]{1,0:T(8,128)(2,1)S(1)}, u32[]{:S(2)}, u32[]{:S(2)}) collective-permute-start(bf16[192,384]{1,0:T(8,128)(2,1)S(1)} %get-tuple-element.53), channel_id=1, source_target_pairs={{0,2},{2,0},{1,3},{3,1},{4,6},{6,4},{5,7},{7,5},{8,10},{10,8},{9,1... | collective-permute-start | bytes 442376 | tf_op jit(solution)/shard_map/ppermute | solution.py:37
  27.1 3.4 %collective-permute-done.8.refs_2_ = bf16[192,384]{1,0:T(8,128)(2,1)S(1)} collective-permute-done((bf16[192,384]{1,0:T(8,128)(2,1)S(1)}, bf16[192,384]{1,0:T(8,128)(2,1)S(1)}, u32[]{:S(2)}, u32[]{:S(2)}) %collective-permute-start.8) | collective-permute-done | bytes 147488 | tf_op jit(solution)/shard_map/ppermute | solution.py:37
  31.6 1.4 %collective-permute-start.10 = (bf16[64,1536]{1,0:T(8,128)(2,1)S(1)}, bf16[64,1536]{1,0:T(8,128)(2,1)S(1)}, u32[]{:S(2)}, u32[]{:S(2)}) collective-permute-start(bf16[64,1536]{1,0:T(8,128)(2,1)S(1)} %get-tuple-element.57), channel_id=1, source_target_pairs={{0,8},{4,12},{8,0},{12,4},{1,9},{5,13},{9,1},{13,5},{2,10},{6,14},... | collective-permute-start | bytes 589832 | tf_op jit(solution)/shard_map/ppermute | solution.py:37
  33.0 2.3 %collective-permute-start.11 = (bf16[64,1536]{1,0:T(8,128)(2,1)S(1)}, bf16[64,1536]{1,0:T(8,128)(2,1)S(1)}, u32[]{:S(2)}, u32[]{:S(2)}) collective-permute-start(bf16[64,1536]{1,0:T(8,128)(2,1)S(1)} %get-tuple-element.58), channel_id=1, source_target_pairs={{0,12},{4,8},{8,4},{12,0},{1,13},{5,9},{9,5},{13,1},{2,14},{6,10},... | collective-permute-start | bytes 589832 | tf_op jit(solution)/shard_map/ppermute | solution.py:37
  35.3 12.4 %fetch.1 = (bf16[2,3072,256]{2,1,0:T(8,128)(2,1)S(1)}, bf16[2,3072,256]{2,1,0:T(8,128)(2,1)S(1)}, bf16[2,3072,256]{2,1,0:T(8,128)(2,1)S(1)}, bf16[2,3072,256]{2,...) custom-call(bf16[2,3072,2048]{2,1,0:T(8,128)(2,1)} %refs_21_.1, ...), custom_call_target="tpu_custom_call" | custom-call | bytes 75497472 | tf_op jit(solution)/shard_map/fetch/pallas_call | solution.py:352
  49.0 1.8 %collective-permute-start.14 = (bf16[64,1536]{1,0:T(8,128)(2,1)S(1)}, bf16[64,1536]{1,0:T(8,128)(2,1)S(1)}, u32[]{:S(2)}, u32[]{:S(2)}) collective-permute-start(bf16[64,1536]{1,0:T(8,128)(2,1)S(1)} %fusion.after.refs_0_), channel_id=1, source_target_pairs={{0,12},{4,8},{8,4},{12,0},{1,13},{5,9},{9,5},{13,1},{2,14},{6,10},... | collective-permute-start | bytes 589832 | tf_op jit(solution)/shard_map/ppermute | solution.py:37
  50.8 3.9 %collective-permute-start.16 = (bf16[64,1536]{1,0:T(8,128)(2,1)S(1)}, bf16[64,1536]{1,0:T(8,128)(2,1)S(1)}, u32[]{:S(2)}, u32[]{:S(2)}) collective-permute-start(bf16[64,1536]{1,0:T(8,128)(2,1)S(1)} %fusion.after.refs_0_), channel_id=1, source_target_pairs={{0,4},{4,0},{8,12},{12,8},{1,5},{5,1},{9,13},{13,9},{2,6},{6,2},{1... | collective-permute-start | bytes 589832 | tf_op jit(solution)/shard_map/ppermute | solution.py:37
  54.7 1.4 %collective-permute-start.18 = (bf16[64,1536]{1,0:T(8,128)(2,1)S(1)}, bf16[64,1536]{1,0:T(8,128)(2,1)S(1)}, u32[]{:S(2)}, u32[]{:S(2)}) collective-permute-start(bf16[64,1536]{1,0:T(8,128)(2,1)S(1)} %fusion.after.refs_0_), channel_id=1, source_target_pairs={{0,8},{4,12},{8,0},{12,4},{1,9},{5,13},{9,1},{13,5},{2,10},{6,14},... | collective-permute-start | bytes 589832 | tf_op jit(solution)/shard_map/ppermute | solution.py:37
  56.1 2.9 %fetch_rows.1 = (bf16[2,1536,256]{2,1,0:T(8,128)(2,1)S(1)}, bf16[2,1536,256]{2,1,0:T(8,128)(2,1)S(1)}, bf16[2,1536,256]{2,1,0:T(8,128)(2,1)S(1)}, bf16[2,1536,256]{2,1,0:T(8,128)(2,1)S(1)}) custom-call(bf16[2,3072,2048]{2,1,0:T(8,128)(2,1)} %refs_21_.1, bf16[2,3072,2048]{2,1,0:T(8,128)(2,1)} %refs_22_.3, bf16[64,1536]{1,0:T(8,128)(2,1)S(1)} %fusion.after.refs_0_), custom_call_target="tpu_custom_call" | custom-call | bytes 12582912 | tf_op jit(solution)/shard_map/fetch_rows/pallas_call | solution.py:395
  59.0 1.6 %collective-permute-start.13 = (bf16[64,1536]{1,0:T(8,128)(2,1)S(1)}, bf16[64,1536]{1,0:T(8,128)(2,1)S(1)}, u32[]{:S(2)}, u32[]{:S(2)}) collective-permute-start(bf16[64,1536]{1,0:T(8,128)(2,1)S(1)} %fusion.after.refs_0_), channel_id=1, source_target_pairs={{0,2},{2,0},{1,3},{3,1},{4,6},{6,4},{5,7},{7,5},{8,10},{10,8},{9,1... | collective-permute-start | bytes 589832 | tf_op jit(solution)/shard_map/ppermute | solution.py:37
  61.1 1.5 %collective-permute-start.17 = (bf16[64,1536]{1,0:T(8,128)(2,1)S(1)}, bf16[64,1536]{1,0:T(8,128)(2,1)S(1)}, u32[]{:S(2)}, u32[]{:S(2)}) collective-permute-start(bf16[64,1536]{1,0:T(8,128)(2,1)S(1)} %collective-permute-done.16.refs_2_), channel_id=1, source_target_pairs={{0,2},{2,0},{1,3},{3,1},{4,6},{6,4},{5,7},{7,5},{8,10},{10,8},{9,1... | collective-permute-start | bytes 589832 | tf_op jit(solution)/shard_map/ppermute | solution.py:37
  62.6 6.0 %collective-permute-done.18.refs_3_ = bf16[64,1536]{1,0:T(8,128)(2,1)S(1)} collective-permute-done((bf16[64,1536]{1,0:T(8,128)(2,1)S(1)}, bf16[64,1536]{1,0:T(8,128)(2,1)S(1)}, u32[]{:S(2)}, u32[]{:S(2)}) %collective-permute-start.18) | collective-permute-done | bytes 196640 | tf_op jit(solution)/shard_map/ppermute | solution.py:37
  68.6 1.5 %collective-permute-start.19 = (bf16[64,1536]{1,0:T(8,128)(2,1)S(1)}, bf16[64,1536]{1,0:T(8,128)(2,1)S(1)}, u32[]{:S(2)}, u32[]{:S(2)}) collective-permute-start(bf16[64,1536]{1,0:T(8,128)(2,1)S(1)} %collective-permute-done.18.refs_3_), channel_id=1, source_target_pairs={{0,2},{2,0},{1,3},{3,1},{4,6},{6,4},{5,7},{7,5},{8,10},{10,8},{9,1... | collective-permute-start | bytes 589832 | tf_op jit(solution)/shard_map/ppermute | solution.py:37
  70.1 4.9 %experts.2 = (bf16[1,320,256]{2,1,0:T(8,128)(2,1)S(1)}, f32[2,160,1]{2,1,0:T(8,128)S(1)}, f32[2,160,1]{2,1,0:T(8,128)S(1)}, bf16[2,2,160,2048]{3,2,1,0:T(8,128)(2,1)S(1)}) custom-call(bf16[64,1536]{1,0:T(8,128)(2,1)S(1)} %fusion.after.refs_0_, bf16[64,1536]{1,0:T(8,128)(2,1)S(1)} %collective-permute-done.14.refs_1_, ...), custom_call_target="tpu_custom_call" | custom-call | flops 4026531840 | bytes 25165824 | tf_op jit(solution)/shard_map/experts/pallas_call | solution.py:603
  75.1 7.8 %experts.3 = bf16[2,160,2048]{2,1,0:T(8,128)(2,1)} custom-call(bf16[64,1536]{1,0:T(8,128)(2,1)S(1)} %collective-permute-done.13.refs_0_, bf16[64,1536]{1,0:T(8,128)(2,1)S(1)} %collective-permute-done.15.refs_1_, bf16[64,1536]{1,0:T(8,128)(2,1)S(1)} %collective-permute-done.17.refs_2_, bf16[64,1536]{1,0:T(8,128)(2,1)S(1)} %collective-permute-done.19.refs_3_, ...), custom_call_target="tpu_custom_call" | custom-call | flops 4026531840 | bytes 25165824 | tf_op jit(solution)/shard_map/experts/pallas_call | solution.py:603
  (31 shorter events, 8.2 us)
Async XLA Ops:
  1.8 22.1 %collective-permute-start.6 = (bf16[192,1536]{1,0:T(8,128)(2,1)S(1)}, bf16[192,1536]{1,0:T(8,128)(2,1)S(1)}, u32[]{:S(2)}, u32[]{:S(2)}) collective-permute-start(bf16[192,1536]{1,0:T(8,128)(2,1)S(1)} %get-tuple-element.50), channel_id=1, source_target_pairs={{0,2},{2,0},{1,3},{3,1},{4,6},{6,4},{5,7},{7,5},{8,10},{10,8},{9,1... | collective-permute-start | bytes 1769480 | tf_op jit(solution)/shard_map/ppermute | solution.py:37
  4.8 5.7 %collective-permute-start = (bf16[64,512]{1,0:T(8,128)(2,1)S(1)}, bf16[64,512]{1,0:T(8,128)(2,1)S(1)}, u32[]{:S(2)}, u32[]{:S(2)}) collective-permute-start(bf16[64,512]{1,0:T(8,128)(2,1)S(1)} %get-tuple-element.45.refs_0_), channel_id=1, source_target_pairs={{0,4},{4,0},{8,12},{12,8},{1,5},{5,1},{9,13},{13,9},{2,6},{6,2},{1... | collective-permute-start | bytes 196616 | tf_op jit(solution)/shard_map/ppermute | solution.py:37
  6.4 7.0 %collective-permute-start.1 = (bf16[64,512]{1,0:T(8,128)(2,1)S(1)}, bf16[64,512]{1,0:T(8,128)(2,1)S(1)}, u32[]{:S(2)}, u32[]{:S(2)}) collective-permute-start(bf16[64,512]{1,0:T(8,128)(2,1)S(1)} %get-tuple-element.45.refs_0_), channel_id=1, source_target_pairs={{0,8},{4,12},{8,0},{12,4},{1,9},{5,13},{9,1},{13,5},{2,10},{6,14},... | collective-permute-start | bytes 196616 | tf_op jit(solution)/shard_map/ppermute | solution.py:37
  9.0 6.1 %collective-permute-start.2 = (bf16[64,512]{1,0:T(8,128)(2,1)S(1)}, bf16[64,512]{1,0:T(8,128)(2,1)S(1)}, u32[]{:S(2)}, u32[]{:S(2)}) collective-permute-start(bf16[64,512]{1,0:T(8,128)(2,1)S(1)} %get-tuple-element.45.refs_0_), channel_id=1, source_target_pairs={{0,12},{4,8},{8,4},{12,0},{1,13},{5,9},{9,5},{13,1},{2,14},{6,10},... | collective-permute-start | bytes 196616 | tf_op jit(solution)/shard_map/ppermute | solution.py:37
  16.0 5.0 %collective-permute-start.7 = (bf16[80,384]{1,0:T(8,128)(2,1)S(1)}, bf16[80,384]{1,0:T(8,128)(2,1)S(1)}, u32[]{:S(2)}, u32[]{:S(2)}) collective-permute-start(bf16[80,384]{1,0:T(8,128)(2,1)S(1)} %get-tuple-element.46.refs_0_), channel_id=1, source_target_pairs={{0,2},{2,0},{1,3},{3,1},{4,6},{6,4},{5,7},{7,5},{8,10},{10,8},{9,1... | collective-permute-start | bytes 184328 | tf_op jit(solution)/shard_map/ppermute | solution.py:37
  16.6 6.0 %collective-permute-start.3 = (bf16[80,384]{1,0:T(8,128)(2,1)S(1)}, bf16[80,384]{1,0:T(8,128)(2,1)S(1)}, u32[]{:S(2)}, u32[]{:S(2)}) collective-permute-start(bf16[80,384]{1,0:T(8,128)(2,1)S(1)} %get-tuple-element.47), channel_id=1, source_target_pairs={{0,12},{4,8},{8,4},{12,0},{1,13},{5,9},{9,5},{13,1},{2,14},{6,10},... | collective-permute-start | bytes 184328 | tf_op jit(solution)/shard_map/ppermute | solution.py:37
  18.1 5.8 %collective-permute-start.4 = (bf16[80,384]{1,0:T(8,128)(2,1)S(1)}, bf16[80,384]{1,0:T(8,128)(2,1)S(1)}, u32[]{:S(2)}, u32[]{:S(2)}) collective-permute-start(bf16[80,384]{1,0:T(8,128)(2,1)S(1)} %get-tuple-element.48), channel_id=1, source_target_pairs={{0,8},{4,12},{8,0},{12,4},{1,9},{5,13},{9,1},{13,5},{2,10},{6,14},... | collective-permute-start | bytes 184328 | tf_op jit(solution)/shard_map/ppermute | solution.py:37
  18.1 5.8 %collective-permute-start.5 = (bf16[80,384]{1,0:T(8,128)(2,1)S(1)}, bf16[80,384]{1,0:T(8,128)(2,1)S(1)}, u32[]{:S(2)}, u32[]{:S(2)}) collective-permute-start(bf16[80,384]{1,0:T(8,128)(2,1)S(1)} %get-tuple-element.49), channel_id=1, source_target_pairs={{0,4},{4,0},{8,12},{12,8},{1,5},{5,1},{9,13},{13,9},{2,6},{6,2},{1... | collective-permute-start | bytes 184328 | tf_op jit(solution)/shard_map/ppermute | solution.py:37
  24.2 6.3 %collective-permute-start.9 = (bf16[192,1536]{1,0:T(8,128)(2,1)S(1)}, bf16[192,1536]{1,0:T(8,128)(2,1)S(1)}, u32[]{:S(2)}, u32[]{:S(2)}) collective-permute-start(bf16[192,1536]{1,0:T(8,128)(2,1)S(1)} %get-tuple-element.54), channel_id=1, source_target_pairs={{0,1},{1,0},{2,3},{3,2},{4,5},{5,4},{6,7},{7,6},{8,9},{9,8},{10,11... | collective-permute-start | bytes 1769480 | tf_op jit(solution)/shard_map/ppermute | solution.py:37
  24.3 6.3 %collective-permute-start.8 = (bf16[192,384]{1,0:T(8,128)(2,1)S(1)}, bf16[192,384]{1,0:T(8,128)(2,1)S(1)}, u32[]{:S(2)}, u32[]{:S(2)}) collective-permute-start(bf16[192,384]{1,0:T(8,128)(2,1)S(1)} %get-tuple-element.53), channel_id=1, source_target_pairs={{0,2},{2,0},{1,3},{3,1},{4,6},{6,4},{5,7},{7,5},{8,10},{10,8},{9,1... | collective-permute-start | bytes 442376 | tf_op jit(solution)/shard_map/ppermute | solution.py:37
  31.6 16.7 %collective-permute-start.10 = (bf16[64,1536]{1,0:T(8,128)(2,1)S(1)}, bf16[64,1536]{1,0:T(8,128)(2,1)S(1)}, u32[]{:S(2)}, u32[]{:S(2)}) collective-permute-start(bf16[64,1536]{1,0:T(8,128)(2,1)S(1)} %get-tuple-element.57), channel_id=1, source_target_pairs={{0,8},{4,12},{8,0},{12,4},{1,9},{5,13},{9,1},{13,5},{2,10},{6,14},... | collective-permute-start | bytes 589832 | tf_op jit(solution)/shard_map/ppermute | solution.py:37
  33.0 15.4 %collective-permute-start.11 = (bf16[64,1536]{1,0:T(8,128)(2,1)S(1)}, bf16[64,1536]{1,0:T(8,128)(2,1)S(1)}, u32[]{:S(2)}, u32[]{:S(2)}) collective-permute-start(bf16[64,1536]{1,0:T(8,128)(2,1)S(1)} %get-tuple-element.58), channel_id=1, source_target_pairs={{0,12},{4,8},{8,4},{12,0},{1,13},{5,9},{9,5},{13,1},{2,14},{6,10},... | collective-permute-start | bytes 589832 | tf_op jit(solution)/shard_map/ppermute | solution.py:37
  35.3 13.5 %collective-permute-start.12 = (bf16[64,1536]{1,0:T(8,128)(2,1)S(1)}, bf16[64,1536]{1,0:T(8,128)(2,1)S(1)}, u32[]{:S(2)}, u32[]{:S(2)}) collective-permute-start(bf16[64,1536]{1,0:T(8,128)(2,1)S(1)} %get-tuple-element.59), channel_id=1, source_target_pairs={{0,4},{4,0},{8,12},{12,8},{1,5},{5,1},{9,13},{13,9},{2,6},{6,2},{1... | collective-permute-start | bytes 589832 | tf_op jit(solution)/shard_map/ppermute | solution.py:37
  35.3 13.5 %copy-start.1 = (bf16[1,64,1536]{2,1,0:T(8,128)(2,1)S(1)}, bf16[1,64,1536]{2,1,0:T(8,128)(2,1)}, u32[]{:S(2)}) copy-start(bf16[1,64,1536]{2,1,0:T(8,128)(2,1)} %param.14) | copy-start | bytes 589828
  48.9 21.1 %copy-start = (bf16[64,1536]{1,0:T(8,128)(2,1)}, bf16[64,1536]{1,0:T(8,128)(2,1)S(1)}, u32[]{:S(2)}) copy-start(bf16[64,1536]{1,0:T(8,128)(2,1)S(1)} %fusion.after.refs_0_) | copy-start | bytes 589828
  49.0 11.6 %collective-permute-start.14 = (bf16[64,1536]{1,0:T(8,128)(2,1)S(1)}, bf16[64,1536]{1,0:T(8,128)(2,1)S(1)}, u32[]{:S(2)}, u32[]{:S(2)}) collective-permute-start(bf16[64,1536]{1,0:T(8,128)(2,1)S(1)} %fusion.after.refs_0_), channel_id=1, source_target_pairs={{0,12},{4,8},{8,4},{12,0},{1,13},{5,9},{9,5},{13,1},{2,14},{6,10},... | collective-permute-start | bytes 589832 | tf_op jit(solution)/shard_map/ppermute | solution.py:37
  50.8 10.3 %collective-permute-start.16 = (bf16[64,1536]{1,0:T(8,128)(2,1)S(1)}, bf16[64,1536]{1,0:T(8,128)(2,1)S(1)}, u32[]{:S(2)}, u32[]{:S(2)}) collective-permute-start(bf16[64,1536]{1,0:T(8,128)(2,1)S(1)} %fusion.after.refs_0_), channel_id=1, source_target_pairs={{0,4},{4,0},{8,12},{12,8},{1,5},{5,1},{9,13},{13,9},{2,6},{6,2},{1... | collective-permute-start | bytes 589832 | tf_op jit(solution)/shard_map/ppermute | solution.py:37
  54.7 13.9 %collective-permute-start.18 = (bf16[64,1536]{1,0:T(8,128)(2,1)S(1)}, bf16[64,1536]{1,0:T(8,128)(2,1)S(1)}, u32[]{:S(2)}, u32[]{:S(2)}) collective-permute-start(bf16[64,1536]{1,0:T(8,128)(2,1)S(1)} %fusion.after.refs_0_), channel_id=1, source_target_pairs={{0,8},{4,12},{8,0},{12,4},{1,9},{5,13},{9,1},{13,5},{2,10},{6,14},... | collective-permute-start | bytes 589832 | tf_op jit(solution)/shard_map/ppermute | solution.py:37
  59.0 16.0 %collective-permute-start.13 = (bf16[64,1536]{1,0:T(8,128)(2,1)S(1)}, bf16[64,1536]{1,0:T(8,128)(2,1)S(1)}, u32[]{:S(2)}, u32[]{:S(2)}) collective-permute-start(bf16[64,1536]{1,0:T(8,128)(2,1)S(1)} %fusion.after.refs_0_), channel_id=1, source_target_pairs={{0,2},{2,0},{1,3},{3,1},{4,6},{6,4},{5,7},{7,5},{8,10},{10,8},{9,1... | collective-permute-start | bytes 589832 | tf_op jit(solution)/shard_map/ppermute | solution.py:37
  60.6 14.4 %collective-permute-start.15 = (bf16[64,1536]{1,0:T(8,128)(2,1)S(1)}, bf16[64,1536]{1,0:T(8,128)(2,1)S(1)}, u32[]{:S(2)}, u32[]{:S(2)}) collective-permute-start(bf16[64,1536]{1,0:T(8,128)(2,1)S(1)} %collective-permute-done.14.refs_1_), channel_id=1, source_target_pairs={{0,2},{2,0},{1,3},{3,1},{4,6},{6,4},{5,7},{7,5},{8,10},{10,8},{9,1... | collective-permute-start | bytes 589832 | tf_op jit(solution)/shard_map/ppermute | solution.py:37
  61.1 13.9 %collective-permute-start.17 = (bf16[64,1536]{1,0:T(8,128)(2,1)S(1)}, bf16[64,1536]{1,0:T(8,128)(2,1)S(1)}, u32[]{:S(2)}, u32[]{:S(2)}) collective-permute-start(bf16[64,1536]{1,0:T(8,128)(2,1)S(1)} %collective-permute-done.16.refs_2_), channel_id=1, source_target_pairs={{0,2},{2,0},{1,3},{3,1},{4,6},{6,4},{5,7},{7,5},{8,10},{10,8},{9,1... | collective-permute-start | bytes 589832 | tf_op jit(solution)/shard_map/ppermute | solution.py:37
  68.6 6.5 %collective-permute-start.19 = (bf16[64,1536]{1,0:T(8,128)(2,1)S(1)}, bf16[64,1536]{1,0:T(8,128)(2,1)S(1)}, u32[]{:S(2)}, u32[]{:S(2)}) collective-permute-start(bf16[64,1536]{1,0:T(8,128)(2,1)S(1)} %collective-permute-done.18.refs_3_), channel_id=1, source_target_pairs={{0,2},{2,0},{1,3},{3,1},{4,6},{6,4},{5,7},{7,5},{8,10},{10,8},{9,1... | collective-permute-start | bytes 589832 | tf_op jit(solution)/shard_map/ppermute | solution.py:37
